TPU v7x, 32 devices: a whole 2x2x4 slice. The times are simulated.
32 devices in a mesh: row: 8 (over z, x), col: 4 (over y, core).
Axes of the slice: x: 2, y: 2, z: 4, core: 2. Of those that a mesh axis runs over, the one named last changes fastest.
Arguments:
- tokens: bfloat16 [8192, 2048], P('row', 'col'), may hold values from -5 to 5
- segment_ids: int32 [8192], P('row'), may hold values from 0 to 7, never falling along the last dimension, each value on 1 to 2048 neighbouring positions
- positions: int32 [8192], P('row'), may hold values from 0 to 4095
- attn_gain: float32 [2048], P('col'), may hold values from 0.5 to 1.5
- query_weight: bfloat16 [2048, 2048], P('row', 'col'), may hold values from -0.22097087 to 0.22097087
- query_bias: float32 [2048], P('col'), may hold values from -3 to 3
- key_weight: bfloat16 [2048, 2048], P('row', 'col'), may hold values from -0.22097087 to 0.22097087
- key_bias: float32 [2048], P('col'), may hold values from -3 to 3
- value_weight: bfloat16 [2048, 2048], P('row', 'col'), may hold values from -0.125 to 0.125
- value_bias: float32 [2048], P('col'), may hold values from -3 to 3
- out_weight: bfloat16 [2048, 2048], P('row', 'col'), may hold values from -1 to 1
- mlp_gain: float32 [2048], P('col'), may hold values from 0.5 to 1.5
- gate_weight: bfloat16 [2048, 5632], P('row', 'col'), may hold values from -0.13258252 to 0.176776695
- up_weight: bfloat16 [2048, 5632], P('row', 'col'), may hold values from -0.13258252 to 0.176776695
- down_weight: bfloat16 [5632, 2048], P('row', 'col'), may hold values from -0.15625 to 0.15625
- out_grad: bfloat16 [8192, 2048], P('row', 'col'), may hold values from -6 to 6
Outputs:
- mixed: bfloat16 [8192, 2048], P('row', 'col')
- tokens_grad: float32 [8192, 2048], P('row', 'col')
- attn_gain_grad: float32 [2048], P('col')
- query_weight_grad: float32 [2048, 2048], P('row', 'col')
- query_bias_grad: float32 [2048], P('col')
- key_weight_grad: float32 [2048, 2048], P('row', 'col')
- key_bias_grad: float32 [2048], P('col')
- value_weight_grad: float32 [2048, 2048], P('row', 'col')
- value_bias_grad: float32 [2048], P('col')
- out_weight_grad: float32 [2048, 2048], P('row', 'col')
- mlp_gain_grad: float32 [2048], P('col')
- gate_weight_grad: float32 [2048, 5632], P('row', 'col')
- up_weight_grad: float32 [2048, 5632], P('row', 'col')
- down_weight_grad: float32 [5632, 2048], P('row', 'col')
Inputs may be any that keep to these rules, and one draw needn't show every extreme that they name: `segment_ids`: ids never fall along the tokens; each document has at most 2048 tokens and one has exactly that many.
All inputs are finite; a program needn't handle non-finite values.
Results may differ from a plain program's by a relative error of at most 0.023.
Values may be sent and summed in bfloat16 or wider, within the bound.
A program may use at most 320 MiB of HBM per device.

v0:
```python
import jax
import jax.numpy as jnp
from jax import lax
from jax.sharding import PartitionSpec as P

HEAD_DIM = 64
ROT = 16
SEQ = 1024


BASE = 10000.0
NEG = -1e30
F32 = jnp.float32
BF16 = jnp.bfloat16


def contract_rows(left, right):
    return lax.dot_general(left, right, (((0,), (0,)), ((), ())), preferred_element_type=F32)


def contract_cols(left, right):
    return lax.dot_general(left, right, (((1,), (1,)), ((), ())), preferred_element_type=F32)


def rotate(values, positions, rot_dims, sign):
    half_dims = rot_dims // 2
    inv_freq = BASE ** (-(jnp.arange(half_dims, dtype=F32) * 2.0) / rot_dims)
    angles = positions.astype(F32)[:, None] * inv_freq[None, :]
    cosine = jnp.cos(angles)[:, None, :]
    sine_part = sign * jnp.sin(angles)[:, None, :]
    first_half = values[..., :half_dims]
    second = values[..., half_dims:rot_dims]
    return jnp.concatenate(
        [
            first_half * cosine - second * sine_part,
            second * cosine + first_half * sine_part,
            values[..., rot_dims:],
        ],
        axis=-1,
    )


def visible(segment):
    length = segment.shape[0]
    query_pos = lax.broadcasted_iota(jnp.int32, (length, length), 0)
    key_pos = lax.broadcasted_iota(jnp.int32, (length, length), 1)
    return (segment[:, None] == segment[None, :]) & (query_pos >= key_pos)


def masked_scores(queries, keys_rot, segment):
    scale = queries.shape[-1] ** (-0.5)
    scores = jnp.einsum("qhe,khe->hqk", queries, keys_rot, preferred_element_type=F32) * scale
    return jnp.where(visible(segment)[None], scores, NEG)


def attend_forward(pieces):
    queries, keys_rot, values, segment = pieces
    scores = masked_scores(queries, keys_rot, segment)
    row_peak = jnp.max(scores, axis=-1, keepdims=True)
    exp_scores = jnp.exp(scores - row_peak)
    row_total = jnp.sum(exp_scores, axis=-1, keepdims=True)
    soft_probs = (exp_scores / row_total).astype(BF16)
    output = jnp.einsum("hqk,khe->qhe", soft_probs, values, preferred_element_type=F32)
    return (output, (row_peak + jnp.log(row_total))[..., 0])


def attend_backward(pieces):
    queries, keys_rot, values, segment, log_total, grad_out = pieces
    scale = queries.shape[-1] ** (-0.5)
    scores = masked_scores(queries, keys_rot, segment)
    soft_probs = jnp.exp(scores - log_total[..., None])
    grad_probs = jnp.einsum("qhe,khe->hqk", grad_out, values, preferred_element_type=F32)
    grad_values = jnp.einsum(
        "hqk,qhe->khe", soft_probs.astype(BF16), grad_out, preferred_element_type=F32
    )
    row_delta = jnp.sum(soft_probs * grad_probs, axis=-1, keepdims=True)
    grad_scores = (soft_probs * (grad_probs - row_delta)).astype(BF16)
    grad_queries = (
        jnp.einsum("hqk,khe->qhe", grad_scores, keys_rot, preferred_element_type=F32) * scale
    )
    grad_keys = jnp.einsum("hqk,qhe->khe", grad_scores, queries, preferred_element_type=F32) * scale
    return (grad_queries, grad_keys, grad_values)


def normalize(values):
    full_width = values.shape[1] * lax.axis_size("col")
    row_sums = lax.psum((jnp.sum(values, axis=1), jnp.sum(values * values, axis=1)), "col")
    row_mean = row_sums[0] / full_width
    row_var = row_sums[1] / full_width - row_mean * row_mean
    inv_std = lax.rsqrt(row_var + 1e-05)
    return ((values - row_mean[:, None]) * inv_std[:, None], inv_std)


def norm_backward(grad_norm, unit_values, inv_std, norm_gain):
    full_width = grad_norm.shape[1] * lax.axis_size("col")
    grad_unit = grad_norm * norm_gain
    row_sums = lax.psum(
        (jnp.sum(grad_unit, axis=1), jnp.sum(grad_unit * unit_values, axis=1)), "col"
    )
    grad_in = inv_std[:, None] * (
        grad_unit
        - row_sums[0][:, None] / full_width
        - unit_values * row_sums[1][:, None] / full_width
    )
    return (grad_in, jnp.sum(grad_norm * unit_values, axis=0))


def gather_cols(values):
    return lax.all_gather(values, "col", axis=1, tiled=True)


def scatter_cols(values):
    return lax.psum_scatter(values, "col", scatter_dimension=1, tiled=True)


def per_device(
    tokens,
    segment_ids,
    positions,
    attn_gain,
    query_weight,
    query_bias,
    key_weight,
    key_bias,
    value_weight,
    value_bias,
    out_weight,
    mlp_gain,
    gate_weight,
    up_weight,
    down_weight,
    out_grad,
):
    row_count = tokens.shape[0]
    width_block = tokens.shape[1]
    local_heads = width_block // HEAD_DIM
    seq_count = row_count // SEQ
    head_shape = (row_count, local_heads, HEAD_DIM)
    seq_shape = (seq_count, SEQ, local_heads, HEAD_DIM)
    segments = segment_ids.reshape(seq_count, SEQ)
    inputs = tokens.astype(F32)
    unit_first, inv_first = normalize(inputs)
    normed_first = gather_cols((unit_first * attn_gain).astype(BF16))
    query_all, key_all, value_all, out_all = (
        lax.all_gather(query_weight, "row", axis=0, tiled=True),
        lax.all_gather(key_weight, "row", axis=0, tiled=True),
        lax.all_gather(value_weight, "row", axis=0, tiled=True),
        lax.all_gather(out_weight, "row", axis=0, tiled=True),
    )
    query_pre = jnp.dot(normed_first, query_all, preferred_element_type=F32) + query_bias
    key_pre = jnp.dot(normed_first, key_all, preferred_element_type=F32) + key_bias
    value_low = (jnp.dot(normed_first, value_all, preferred_element_type=F32) + value_bias).astype(
        BF16
    )
    query_rot = (
        rotate(query_pre.reshape(head_shape), positions, ROT, 1.0).astype(BF16).reshape(seq_shape)
    )
    key_rot = (
        rotate(key_pre.reshape(head_shape), positions, ROT, 1.0).astype(BF16).reshape(seq_shape)
    )
    value_seq = value_low.reshape(seq_shape)
    attended, log_total = lax.map(attend_forward, (query_rot, key_rot, value_seq, segments))
    attn_low = attended.reshape(row_count, width_block).astype(BF16)
    attn_all = lax.all_gather(attn_low, "col", axis=1, tiled=True)
    resid = inputs + jnp.dot(attn_all, out_all, preferred_element_type=F32)
    unit_second, inv_second = normalize(resid)
    normed_second = gather_cols((unit_second * mlp_gain).astype(BF16))
    gate_all, up_all, down_all = (
        lax.all_gather(gate_weight, "row", axis=0, tiled=True),
        lax.all_gather(up_weight, "row", axis=0, tiled=True),
        lax.all_gather(down_weight, "row", axis=0, tiled=True),
    )
    gate_pre = jnp.dot(normed_second, gate_all, preferred_element_type=F32)
    up_pre = jnp.dot(normed_second, up_all, preferred_element_type=F32)
    gate_sigmoid = jax.nn.sigmoid(gate_pre)
    gate_silu = gate_pre * gate_sigmoid
    hidden = (gate_silu * up_pre).astype(BF16)
    hidden_all = lax.all_gather(hidden, "col", axis=1, tiled=True)
    mixed = (resid + jnp.dot(hidden_all, down_all, preferred_element_type=F32)).astype(BF16)
    grad_down = contract_rows(hidden_all, out_grad)
    grad_hidden = lax.psum_scatter(
        contract_cols(out_grad, down_all), "col", scatter_dimension=1, tiled=True
    )
    grad_gate = (
        grad_hidden * up_pre * gate_sigmoid * (1.0 + gate_pre * (1.0 - gate_sigmoid))
    ).astype(BF16)
    grad_up = (grad_hidden * gate_silu).astype(BF16)
    grad_gate_weight = contract_rows(normed_second, grad_gate)
    grad_up_weight = contract_rows(normed_second, grad_up)
    mlp_grads = (
        lax.psum_scatter(
            grad_gate_weight.astype(jnp.bfloat16), "row", scatter_dimension=0, tiled=True
        ).astype(jnp.float32),
        lax.psum_scatter(
            grad_up_weight.astype(jnp.bfloat16), "row", scatter_dimension=0, tiled=True
        ).astype(jnp.float32),
        lax.psum_scatter(
            grad_down.astype(jnp.bfloat16), "row", scatter_dimension=0, tiled=True
        ).astype(jnp.float32),
    )
    grad_second = scatter_cols(contract_cols(grad_gate, gate_all) + contract_cols(grad_up, up_all))
    grad_resid, mlp_gain_part = norm_backward(grad_second, unit_second, inv_second, mlp_gain)
    grad_resid = grad_resid + out_grad.astype(F32)
    grad_resid_low = grad_resid.astype(BF16)
    grad_out_weight = contract_rows(attn_all, grad_resid_low)
    grad_attn = scatter_cols(contract_cols(grad_resid_low, out_all)).astype(BF16).reshape(seq_shape)
    grad_qrot, grad_krot, grad_vseq = lax.map(
        attend_backward, (query_rot, key_rot, value_seq, segments, log_total, grad_attn)
    )
    grad_query = (
        rotate(grad_qrot.reshape(head_shape), positions, ROT, -1.0)
        .reshape(row_count, width_block)
        .astype(BF16)
    )
    grad_key = (
        rotate(grad_krot.reshape(head_shape), positions, ROT, -1.0)
        .reshape(row_count, width_block)
        .astype(BF16)
    )
    grad_value = grad_vseq.reshape(row_count, width_block).astype(BF16)
    grad_query_weight = contract_rows(normed_first, grad_query)
    grad_key_weight = contract_rows(normed_first, grad_key)
    grad_value_weight = contract_rows(normed_first, grad_value)
    attn_grads = (
        lax.psum_scatter(
            grad_query_weight.astype(jnp.bfloat16), "row", scatter_dimension=0, tiled=True
        ).astype(jnp.float32),
        lax.psum_scatter(
            grad_key_weight.astype(jnp.bfloat16), "row", scatter_dimension=0, tiled=True
        ).astype(jnp.float32),
        lax.psum_scatter(
            grad_value_weight.astype(jnp.bfloat16), "row", scatter_dimension=0, tiled=True
        ).astype(jnp.float32),
        lax.psum_scatter(
            grad_out_weight.astype(jnp.bfloat16), "row", scatter_dimension=0, tiled=True
        ).astype(jnp.float32),
    )
    grad_first = scatter_cols(
        contract_cols(grad_query, query_all)
        + contract_cols(grad_key, key_all)
        + contract_cols(grad_value, value_all)
    )
    grad_input, attn_gain_part = norm_backward(grad_first, unit_first, inv_first, attn_gain)
    tokens_grad = grad_input + grad_resid
    vectors = lax.psum(
        (
            attn_gain_part,
            jnp.sum(grad_query.astype(F32), axis=0),
            jnp.sum(grad_key.astype(F32), axis=0),
            jnp.sum(grad_value.astype(F32), axis=0),
            mlp_gain_part,
        ),
        "row",
    )
    return (
        mixed,
        tokens_grad,
        vectors[0],
        attn_grads[0],
        vectors[1],
        attn_grads[1],
        vectors[2],
        attn_grads[2],
        vectors[3],
        attn_grads[3],
        vectors[4],
        mlp_grads[0],
        mlp_grads[1],
        mlp_grads[2],
    )


def solution(mesh):
    in_specs = (
        P("row", "col"),
        P("row"),
        P("row"),
        P("col"),
        P("row", "col"),
        P("col"),
        P("row", "col"),
        P("col"),
        P("row", "col"),
        P("col"),
        P("row", "col"),
        P("col"),
        P("row", "col"),
        P("row", "col"),
        P("row", "col"),
        P("row", "col"),
    )
    out_specs = (
        P("row", "col"),
        P("row", "col"),
        P("col"),
        P("row", "col"),
        P("col"),
        P("row", "col"),
        P("col"),
        P("row", "col"),
        P("col"),
        P("row", "col"),
        P("col"),
        P("row", "col"),
        P("row", "col"),
        P("row", "col"),
    )
    return jax.shard_map(
        per_device, mesh=mesh, in_specs=in_specs, out_specs=out_specs, check_vma=False
    )
```

profile of v0, /device:TPU:0, one launch (start us, length us, event | category | flops | bytes accessed | tf_op | source)
XLA Modules:
  0.0 1785.3 jit_solution(13005500443280974494)
XLA Ops:
  23.7 38.6 %all-gather.18.cloned.1.call-done = bf16[2048,512]{1,0:T(8,128)(2,1)} async-done(((bf16[256,512]{1,0:T(8,128)(2,1)}), bf16[2048,512]{1,0:T(8,128)(2,1)}) %all-gather.18.cloned.1.call-update) | async-done | bytes 2097168 | tf_op jit(solution)/shard_map/all_gather | solution.py:146
  62.3 35.1 %all-gather.12.cloned.1.call-done = bf16[1024,2048]{0,1:T(8,128)(2,1)} async-done(((bf16[1024,512]{0,1:T(8,128)(2,1)}), bf16[1024,2048]{0,1:T(8,128)(2,1)}) %all-gather.12.cloned.1.call-update) | async-done | bytes 4194320 | tf_op jit(solution)/shard_map/all_gather | solution.py:109
  104.2 44.8 %all-gather.16.cloned.1.call-done = bf16[2048,512]{1,0:T(8,128)(2,1)} async-done(((bf16[256,512]{1,0:T(8,128)(2,1)}), bf16[2048,512]{1,0:T(8,128)(2,1)}) %all-gather.16.cloned.1.call-update) | async-done | bytes 2097168 | tf_op jit(solution)/shard_map/all_gather | solution.py:145
  220.8 27.7 %all-gather.22.cloned.1.call-done = bf16[2048,512]{1,0:T(8,128)(2,1)} async-done(((bf16[256,512]{1,0:T(8,128)(2,1)}), bf16[2048,512]{1,0:T(8,128)(2,1)}) %all-gather.22.cloned.1.call-update) | async-done | bytes 2097168 | tf_op jit(solution)/shard_map/all_gather | solution.py:148
  248.5 35.0 %all-gather.20.cloned.1.call-done = bf16[1024,2048]{0,1:T(8,128)(2,1)} async-done(((bf16[1024,512]{0,1:T(8,128)(2,1)}), bf16[1024,2048]{0,1:T(8,128)(2,1)}) %all-gather.20.cloned.1.call-update) | async-done | bytes 4194320 | tf_op jit(solution)/shard_map/all_gather | solution.py:164
  297.1 81.3 %all-gather.32.cloned.1.call-done = bf16[5632,512]{1,0:T(8,128)(2,1)} async-done(((bf16[704,512]{1,0:T(8,128)(2,1)}), bf16[5632,512]{1,0:T(8,128)(2,1)}) %all-gather.32.cloned.1.call-update) | async-done | bytes 5767184 | tf_op jit(solution)/shard_map/all_gather | solution.py:171
  392.5 78.9 %all-gather.28.cloned.1.call-done = bf16[2048,1408]{1,0:T(8,128)(2,1)} async-done(((bf16[256,1408]{1,0:T(8,128)(2,1)}), bf16[2048,1408]{1,0:T(8,128)(2,1)}) %all-gather.28.cloned.1.call-update) | async-done | bytes 5767184 | tf_op jit(solution)/shard_map/all_gather | solution.py:170
  471.4 34.8 %all-gather.24.cloned.1.call-done = bf16[1024,2048]{0,1:T(8,128)(2,1)} async-done(((bf16[1024,512]{0,1:T(8,128)(2,1)}), bf16[1024,2048]{0,1:T(8,128)(2,1)}) %all-gather.24.cloned.1.call-update) | async-done | bytes 4194320 | tf_op jit(solution)/shard_map/all_gather | solution.py:109
  518.1 82.9 %all-gather.26.cloned.1.call-done = bf16[2048,1408]{1,0:T(8,128)(2,1)} async-done(((bf16[256,1408]{1,0:T(8,128)(2,1)}), bf16[2048,1408]{1,0:T(8,128)(2,1)}) %all-gather.26.cloned.1.call-update) | async-done | bytes 5767184 | tf_op jit(solution)/shard_map/all_gather | solution.py:169
  601.0 167.6 %reduce-scatter.12.cloned.1.call-done = f32[1024,1408]{1,0:T(8,128)} async-done(((f32[1024,5632]{1,0:T(8,128)}), f32[1024,1408]{1,0:T(8,128)}) %reduce-scatter.12.cloned.1.call-update) | async-done | bytes 5767184 | tf_op jit(solution)/shard_map/reduce_scatter | solution.py:181
  768.5 17.2 multiply_convert_fusion.1
  805.6 69.8 %reduce-scatter.14.cloned.1.call-done = f32[1024,512]{0,1:T(8,128)} async-done(((f32[1024,2048]{0,1:T(8,128)}), f32[1024,512]{0,1:T(8,128)}) %reduce-scatter.14.cloned.1.call-update) | async-done | bytes 2097168 | tf_op jit(solution)/shard_map/reduce_scatter | solution.py:113
  922.7 30.3 %all-gather.30.cloned.1.call-done = bf16[1024,5632]{1,0:T(8,128)(2,1)} async-done(((bf16[1024,1408]{1,0:T(8,128)(2,1)}), bf16[1024,5632]{1,0:T(8,128)(2,1)}) %all-gather.30.cloned.1.call-update) | async-done | bytes 11534352 | tf_op jit(solution)/shard_map/all_gather | solution.py:178
  965.6 61.6 %reduce-scatter.16.cloned.1.call-done = f32[1024,512]{1,0:T(8,128)} async-done(((f32[1024,2048]{1,0:T(8,128)}), f32[1024,512]{1,0:T(8,128)}) %reduce-scatter.16.cloned.1.call-update) | async-done | bytes 2097168 | tf_op jit(solution)/shard_map/reduce_scatter | solution.py:113
  1052.5 22.6 %multiply_reduce_fusion = (f32[8,1024]{1,0:T(8,128)S(1)}, f32[8,1024,1024]{1,2,0:T(8,128)}) fusion(f32[8,1024,1024]{1,2,0:T(8,128)} %get-tuple-element.143, f32[8,1024]{1,0:T(8,128)S(1)} %log_add_fusion, bf16[1024,8,64]{0,2,1:T(8,128)(2,1)S(1)} %bitcast.63, bf16[1024,8,64]{0,2,1:T(8,128)(2,1)} %bitcast.67), kind=kOutput, calls=%fused_computation.1 | convolution fusion | flops 1098899456 | bytes 69271552 | tf_op jit(solution)/shard_map/while/body/eval_jaxpr/qhe,khe->hqk/dot_general | solution.py:72
  1075.5 29.2 %multiply_convert_fusion = bf16[8,1024,1024]{1,2,0:T(8,128)(2,1)} fusion(f32[8,1024,1024]{1,2,0:T(8,128)} %get-tuple-element.146, f32[8,1024,1024]{1,2,0:T(8,128)} %get-tuple-element.143, f32[8,1024]{1,0:T(8,128)S(1)} %get-tuple-element.145, f32[8,1024]{1,0:T(8,128)S(1)} %log_add_fusion), kind=kLoop, calls=%fused_computation | loop fusion | flops 33554432 | bytes 83951616 | tf_op jit(solution)/shard_map/while/body/eval_jaxpr/convert_element_type | solution.py:77
  1158.0 96.9 %reduce-scatter.28.cloned.1.call-done = bf16[256,1408]{1,0:T(8,128)(2,1)} async-done(((bf16[2048,1408]{1,0:T(8,128)(2,1)}), bf16[256,1408]{1,0:T(8,128)(2,1)}) %reduce-scatter.28.cloned.1.call-update) | async-done | bytes 720912 | tf_op jit(solution)/shard_map/reduce_scatter | solution.py:191
  1269.6 56.5 %reduce-scatter.26.cloned.1.call-done = bf16[256,512]{1,0:T(8,128)(2,1)} async-done(((bf16[2048,512]{1,0:T(8,128)(2,1)}), bf16[256,512]{1,0:T(8,128)(2,1)}) %reduce-scatter.26.cloned.1.call-update) | async-done | bytes 262160 | tf_op jit(solution)/shard_map/reduce_scatter | solution.py:234
  1328.0 111.2 %reduce-scatter.32.cloned.1.call-done = bf16[704,512]{1,0:T(8,128)(2,1)} async-done(((bf16[5632,512]{1,0:T(8,128)(2,1)}), bf16[704,512]{1,0:T(8,128)(2,1)}) %reduce-scatter.32.cloned.1.call-update) | async-done | bytes 720912 | tf_op jit(solution)/shard_map/reduce_scatter | solution.py:197
  1441.9 69.0 %reduce-scatter.24.cloned.1.call-done = bf16[256,512]{1,0:T(8,128)(2,1)} async-done(((bf16[2048,512]{1,0:T(8,128)(2,1)}), bf16[256,512]{1,0:T(8,128)(2,1)}) %reduce-scatter.24.cloned.1.call-update) | async-done | bytes 262160 | tf_op jit(solution)/shard_map/reduce_scatter | solution.py:231
  1512.6 68.9 %reduce-scatter.22.cloned.1.call-done = bf16[256,512]{1,0:T(8,128)(2,1)} async-done(((bf16[2048,512]{1,0:T(8,128)(2,1)}), bf16[256,512]{1,0:T(8,128)(2,1)}) %reduce-scatter.22.cloned.1.call-update) | async-done | bytes 262160 | tf_op jit(solution)/shard_map/reduce_scatter | solution.py:228
  1583.4 69.0 %reduce-scatter.20.cloned.1.call-done = bf16[256,512]{1,0:T(8,128)(2,1)} async-done(((bf16[2048,512]{1,0:T(8,128)(2,1)}), bf16[256,512]{1,0:T(8,128)(2,1)}) %reduce-scatter.20.cloned.1.call-update) | async-done | bytes 262160 | tf_op jit(solution)/shard_map/reduce_scatter | solution.py:225
  1654.2 71.7 %reduce-scatter.18.cloned.1.call-done = f32[1024,512]{0,1:T(8,128)} async-done(((f32[1024,2048]{0,1:T(8,128)}), f32[1024,512]{0,1:T(8,128)}) %reduce-scatter.18.cloned.1.call-update) | async-done | bytes 2097168 | tf_op jit(solution)/shard_map/reduce_scatter | solution.py:113
  1740.7 37.3 %all-reduce = (f32[512]{0:T(512)}, f32[512]{0:T(512)}, f32[512]{0:T(512)}, f32[512]{0:T(512)}, f32[512]{0:T(512)}) all-reduce(f32[512]{0:T(512)S(1)} %get-tuple-element.95, f32[512]{0:T(512)S(1)} %reduce_sum.155, f32[512]{0:T(512)S(1)} %reduce_sum.157, f32[512]{0:T(512)S(1)} %reduce_sum.159, ...), channel_id=1, replica_groups=mesh['row'=8,'col'=4] {'row'}, use_global_device_ids=true, to_apply=%region_24.25 | all-reduce | flops 2560 | bytes 20480 | tf_op jit(solution)/shard_map/psum | solution.py:245
  (207 shorter events, 331.6 us)
Async XLA Ops:
  7.2 55.1 %all-gather.18.cloned.1.call-start = ((), (), s32[]{:S(2)}) async-start(), calls=%async_computation.14 | async-start | bytes 2359296 | tf_op jit(solution)/shard_map/all_gather | solution.py:146
  7.9 89.5 %all-gather.12.cloned.1.call-start = ((), (), s32[]{:S(2)}) async-start(), calls=%async_computation.11 | async-start | bytes 5242880 | tf_op jit(solution)/shard_map/all_gather | solution.py:109
  20.3 128.6 %all-gather.16.cloned.1.call-start = ((), (), s32[]{:S(2)}) async-start(), calls=%async_computation.13 | async-start | bytes 2359296 | tf_op jit(solution)/shard_map/all_gather | solution.py:145
  21.0 177.7 %all-gather.14.cloned.1.call-start = ((), (), s32[]{:S(2)}) async-start(), calls=%async_computation.12 | async-start | bytes 2359296 | tf_op jit(solution)/shard_map/all_gather | solution.py:147
  21.6 226.9 %all-gather.22.cloned.1.call-start = ((), (), s32[]{:S(2)}) async-start(), calls=%async_computation.16 | async-start | bytes 2359296 | tf_op jit(solution)/shard_map/all_gather | solution.py:148
  22.2 261.3 %all-gather.20.cloned.1.call-start = ((), (), s32[]{:S(2)}) async-start(), calls=%async_computation.15 | async-start | bytes 5242880 | tf_op jit(solution)/shard_map/all_gather | solution.py:164
  219.3 159.1 %all-gather.32.cloned.1.call-start = ((), (), s32[]{:S(2)}) async-start(), calls=%async_computation.21 | async-start | bytes 6488064 | tf_op jit(solution)/shard_map/all_gather | solution.py:171
  220.0 251.4 %all-gather.28.cloned.1.call-start = ((), (), s32[]{:S(2)}) async-start(), calls=%async_computation.19 | async-start | bytes 6488064 | tf_op jit(solution)/shard_map/all_gather | solution.py:170
  220.8 285.5 %all-gather.24.cloned.1.call-start = ((), (), s32[]{:S(2)}) async-start(), calls=%async_computation.17 | async-start | bytes 5242880 | tf_op jit(solution)/shard_map/all_gather | solution.py:109
  288.8 586.5 %copy-start.2 = (f32[1024,512]{0,1:T(8,128)}, f32[1024,512]{0,1:T(8,128)S(1)}, u32[]{:S(2)}) copy-start(f32[1024,512]{0,1:T(8,128)S(1)} %get-tuple-element.144) | copy-start | bytes 6291460
  296.4 304.5 %all-gather.26.cloned.1.call-start = ((), (), s32[]{:S(2)}) async-start(), calls=%async_computation.18 | async-start | bytes 6488064 | tf_op jit(solution)/shard_map/all_gather | solution.py:169
  297.0 471.5 %reduce-scatter.12.cloned.1.call-start = ((), (), s32[]{:S(2)}) async-start(), calls=%async_computation.22 | async-start | bytes 28835840 | tf_op jit(solution)/shard_map/reduce_scatter | solution.py:181
  392.4 482.9 %reduce-scatter.14.cloned.1.call-start = ((), (), s32[]{:S(2)}) async-start(), calls=%async_computation.23 | async-start | bytes 10485760 | tf_op jit(solution)/shard_map/reduce_scatter | solution.py:113
  803.5 149.6 %all-gather.30.cloned.1.call-start = ((), (), s32[]{:S(2)}) async-start(), calls=%async_computation.20 | async-start | bytes 14417920 | tf_op jit(solution)/shard_map/all_gather | solution.py:178
  804.2 223.0 %reduce-scatter.16.cloned.1.call-start = ((), (), s32[]{:S(2)}) async-start(), calls=%async_computation.24 | async-start | bytes 10485760 | tf_op jit(solution)/shard_map/reduce_scatter | solution.py:113
  894.5 261.2 %reduce-scatter.30.cloned.1.call-start = ((), (), s32[]{:S(2)}) async-start(), calls=%async_computation.31 | async-start | bytes 6488064 | tf_op jit(solution)/shard_map/reduce_scatter | solution.py:194
  905.5 349.5 %reduce-scatter.28.cloned.1.call-start = ((), (), s32[]{:S(2)}) async-start(), calls=%async_computation.30 | async-start | bytes 6488064 | tf_op jit(solution)/shard_map/reduce_scatter | solution.py:191
  916.4 409.8 %reduce-scatter.26.cloned.1.call-start = ((), (), s32[]{:S(2)}) async-start(), calls=%async_computation.29 | async-start | bytes 2359296 | tf_op jit(solution)/shard_map/reduce_scatter | solution.py:234
  922.5 516.7 %reduce-scatter.32.cloned.1.call-start = ((), (), s32[]{:S(2)}) async-start(), calls=%async_computation.32 | async-start | bytes 6488064 | tf_op jit(solution)/shard_map/reduce_scatter | solution.py:197
  965.5 545.3 %reduce-scatter.24.cloned.1.call-start = ((), (), s32[]{:S(2)}) async-start(), calls=%async_computation.28 | async-start | bytes 2359296 | tf_op jit(solution)/shard_map/reduce_scatter | solution.py:231
  1075.2 506.4 %reduce-scatter.22.cloned.1.call-start = ((), (), s32[]{:S(2)}) async-start(), calls=%async_computation.27 | async-start | bytes 2359296 | tf_op jit(solution)/shard_map/reduce_scatter | solution.py:228
  1136.9 515.5 %reduce-scatter.20.cloned.1.call-start = ((), (), s32[]{:S(2)}) async-start(), calls=%async_computation.26 | async-start | bytes 2359296 | tf_op jit(solution)/shard_map/reduce_scatter | solution.py:225
  1142.9 583.0 %reduce-scatter.18.cloned.1.call-start = ((), (), s32[]{:S(2)}) async-start(), calls=%async_computation.25 | async-start | bytes 10485760 | tf_op jit(solution)/shard_map/reduce_scatter | solution.py:113
  1269.6 456.3 %copy-start.34 = (f32[512]{0:T(512)S(1)}, f32[512]{0:T(512)}, u32[]{:S(2)}) copy-start(f32[512]{0:T(512)} %param.19) | copy-start | bytes 6148
  (44 other events, 2594.6 us)
Sparse Core Ops, SparseCore 0:
  10.2 52.1 all-gather.17
  64.5 32.9 all-gather.11
  99.6 49.2 all-gather.15
  150.9 47.7 all-gather.13
  200.7 47.7 all-gather.21
  250.5 32.9 all-gather.19
  285.7 92.6 all-gather.31
  380.5 90.8 all-gather.27
  473.5 32.6 all-gather.23
  508.3 92.6 all-gather.25
  603.5 164.9 reduce-scatter.11
  803.6 71.7 reduce-scatter.13
  876.9 76.0 all-gather.29
  955.5 71.7 reduce-scatter.15
  1031.2 110.0 reduce-scatter.29
  1145.2 109.7 reduce-scatter.27
  1258.8 67.3 reduce-scatter.25
  1330.1 109.0 reduce-scatter.31
  1443.2 67.6 reduce-scatter.23
  1514.6 66.9 reduce-scatter.21
  1585.5 66.8 reduce-scatter.19
  1655.2 70.7 reduce-scatter.17
where the time goes:
time: 1790 us
  waiting for transfers between devices  1350 us (75%)
  matrix products  256 us (14%)
  other arithmetic  81 us (5%)
  blocking collectives  64.2 us (4%)
    reduce_scatter x3, waiting for transfers between devices, scatter_cols(): return lax.psum_scatter(values, 'col', scatter_dimension=1, tiled=True)  203 us
    reduce_scatter x1, waiting for transfers between devices, per_device(): lax.psum_scatter(contract_cols(out_grad, down_all), 'col', scatter_dimens...  168 us
    reduce_scatter x1, waiting for transfers between devices, per_device(): lax.psum_scatter(grad_down.astype(jnp.bfloat16), 'row', scatter_dimension...  111 us
    reduce_scatter x1, waiting for transfers between devices, per_device(): lax.psum_scatter(grad_gate_weight.astype(jnp.bfloat16), 'row', scatter_di...  96.9 us
    all_gather x1, waiting for transfers between devices, per_device(): lax.all_gather(gate_weight, 'row', axis=0, tiled=True)  82.9 us
    all_gather x1, waiting for transfers between devices, per_device(): lax.all_gather(down_weight, 'row', axis=0, tiled=True)  81.3 us
    all_gather x1, waiting for transfers between devices, per_device(): lax.all_gather(up_weight, 'row', axis=0, tiled=True)  78.9 us
    all_gather x2, waiting for transfers between devices, gather_cols(): return lax.all_gather(values, 'col', axis=1, tiled=True)  70 us
  transfers between devices with their start and end apart: 22, of which 21 were waited for; matrix products, arithmetic and copies ran while one was open for 17% of the time, Pallas kernels for 0%

commit v1 on v0

v1 whole, which is shorter than its diff:
```python
import functools

import jax
import jax.numpy as jnp
from jax import lax
from jax.experimental import pallas as pl
from jax.experimental.pallas import tpu as pltpu
from jax.sharding import PartitionSpec as P

HEAD_DIM = 64
ROT = 16
SEQ = 1024
BASE = 10000.0
NEG = -1e30
F32 = jnp.float32
BF16 = jnp.bfloat16
SCALE = HEAD_DIM**-0.5
MESH = pl.DeviceIdType.MESH
QBLOCK = 256
PAIR = 2


def dot(left, right, left_dims=(1,), right_dims=(0,)):
    return lax.dot_general(
        left, right, ((left_dims, right_dims), ((), ())), preferred_element_type=F32
    )


def swap_pairs(values, lane):
    half = ROT // 2
    width = values.shape[1]
    ahead = pltpu.roll(values, width - half, 1)
    behind = pltpu.roll(values, half, 1)
    return jnp.where(lane < half, ahead, behind)


def attention_forward_kernel(
    q_ref, k_ref, v_ref, seg_col_ref, seg_row_ref, o_ref, lse_ref, acc_ref, lse_scratch
):
    width = q_ref.shape[1]
    heads = width // HEAD_DIM
    full_lane = lax.broadcasted_iota(jnp.int32, (1, width), 1)
    acc_ref[...] = jnp.zeros_like(acc_ref)
    lse_lane = lax.broadcasted_iota(jnp.int32, (1, lse_scratch.shape[1]), 1)

    @pl.loop(0, heads)
    def _(head):
        mask = full_lane // HEAD_DIM == head
        for start in range(0, SEQ, QBLOCK):
            keys = start + QBLOCK
            rows = slice(start, keys)
            queries = jnp.where(mask, q_ref[rows, :], jnp.zeros((), BF16))
            scores = dot(queries, k_ref[:keys, :], (1,), (1,))
            query_pos = start + lax.broadcasted_iota(jnp.int32, scores.shape, 0)
            key_pos = lax.broadcasted_iota(jnp.int32, scores.shape, 1)
            seen = (seg_col_ref[rows, :] == seg_row_ref[0, :, :keys]) & (key_pos <= query_pos)
            scores = jnp.where(seen, scores, NEG)
            peak = jnp.max(scores, axis=1, keepdims=True)
            weights = jnp.exp(scores - peak)
            total = jnp.sum(weights, axis=1, keepdims=True)
            probs = (weights * (1.0 / total)).astype(BF16)
            output = dot(probs, v_ref[:keys, :])
            acc_ref[rows, :] = jnp.where(mask, output, acc_ref[rows, :])
            lse_scratch[rows, :] = jnp.where(
                lse_lane == head, peak + jnp.log(total), lse_scratch[rows, :]
            )

    o_ref[...] = acc_ref[...].astype(BF16)
    lse_ref[0] = lse_scratch[...].T[: lse_ref.shape[1], :]


def attention_forward(queries, keys, values, segments):
    rows, width = queries.shape
    seqs = rows // SEQ
    block = lambda columns: pl.BlockSpec((SEQ, columns), lambda s: (s, 0))
    return pl.pallas_call(
        attention_forward_kernel,
        grid=(seqs,),
        in_specs=[block(width)] * 3 + [block(1), pl.BlockSpec((1, 1, SEQ), lambda s: (s, 0, 0))],
        out_specs=[block(width), pl.BlockSpec((1, 8, SEQ), lambda s: (s, 0, 0))],
        out_shape=[
            jax.ShapeDtypeStruct((rows, width), BF16),
            jax.ShapeDtypeStruct((seqs, 8, SEQ), F32),
        ],
        scratch_shapes=[pltpu.VMEM((SEQ, width), F32), pltpu.VMEM((SEQ, 128), F32)],
        compiler_params=pltpu.CompilerParams(vmem_limit_bytes=56 << 20),
        cost_estimate=pl.CostEstimate(
            flops=8 * rows * SEQ * width, bytes_accessed=10 * rows * width, transcendentals=0
        ),
        name="attention_forward",
    )(queries, keys, values, segments.reshape(rows, 1), segments.reshape(seqs, 1, SEQ))


def attention_backward_kernel(
    q_ref, k_ref, v_ref, do_ref, lse_ref, cos_ref, sin_ref, seg_col_ref, seg_row_ref,
    grad_ref, sums_ref, dq_ref, dk_ref, dv_ref,
):
    width = q_ref.shape[1]
    heads = width // HEAD_DIM
    full_lane = lax.broadcasted_iota(jnp.int32, (1, width), 1)
    in_head = full_lane % HEAD_DIM
    for ref in (dq_ref, dk_ref, dv_ref):
        ref[...] = jnp.zeros_like(ref)

    @pl.loop(0, heads)
    def _(head):
        mask = full_lane // HEAD_DIM == head
        nothing = jnp.zeros((), BF16)
        for start in range(0, SEQ, QBLOCK):
            keys = start + QBLOCK
            rows = slice(start, keys)
            queries = jnp.where(mask, q_ref[rows, :], nothing)
            grads = jnp.where(mask, do_ref[rows, :], nothing)
            scores = dot(k_ref[:keys, :], queries, (1,), (1,))
            key_pos = lax.broadcasted_iota(jnp.int32, scores.shape, 0)
            query_pos = start + lax.broadcasted_iota(jnp.int32, scores.shape, 1)
            seen = (seg_col_ref[:keys, :] == seg_row_ref[0, :, rows]) & (key_pos <= query_pos)
            probs = jnp.where(
                seen, jnp.exp(scores - lse_ref[0, pl.ds(head, 1), rows]), 0.0
            )
            dv_ref[:keys, :] += dot(probs.astype(BF16), grads)
            grad_probs = dot(v_ref[:keys, :], grads, (1,), (1,))
            delta = jnp.sum(probs * grad_probs, axis=0, keepdims=True)
            grad_scores = (probs * (grad_probs - delta)).astype(BF16)
            dk_ref[:keys, :] += dot(grad_scores, queries)
            masked_keys = jnp.where(mask, k_ref[:keys, :], nothing)
            dq_ref[rows, :] += dot(grad_scores, masked_keys, (0,), (0,))

    cosine = jnp.tile(cos_ref[...], (1, width // cos_ref.shape[1]))
    sine = jnp.tile(sin_ref[...], (1, width // sin_ref.shape[1]))
    for part, (ref, scale) in enumerate(((dq_ref, SCALE), (dk_ref, 1.0), (dv_ref, None))):
        grad = ref[...]
        if scale is not None:
            grad = grad * scale
            grad = grad * cosine - swap_pairs(grad, in_head) * sine
        low = grad.astype(BF16)
        columns = slice(part * width, (part + 1) * width)
        grad_ref[:, columns] = low
        sums_ref[0, :, columns] = jnp.sum(low.astype(F32), axis=0, keepdims=True)


def attention_backward(queries, keys, values, grad_out, lse, cosine, sine, segments):
    rows, width = queries.shape
    seqs = rows // SEQ
    block = lambda columns: pl.BlockSpec((SEQ, columns), lambda s: (s, 0))
    return pl.pallas_call(
        attention_backward_kernel,
        grid=(seqs,),
        in_specs=[block(width)] * 4
        + [
            pl.BlockSpec((1, 8, SEQ), lambda s: (s, 0, 0)),
            block(cosine.shape[1]),
            block(cosine.shape[1]),
            block(1),
            pl.BlockSpec((1, 1, SEQ), lambda s: (s, 0, 0)),
        ],
        out_specs=[block(3 * width), pl.BlockSpec((1, 1, 3 * width), lambda s: (s, 0, 0))],
        out_shape=[
            jax.ShapeDtypeStruct((rows, 3 * width), BF16),
            jax.ShapeDtypeStruct((seqs, 1, 3 * width), F32),
        ],
        scratch_shapes=[pltpu.VMEM((SEQ, width), F32)] * 3,
        compiler_params=pltpu.CompilerParams(vmem_limit_bytes=56 << 20),
        cost_estimate=pl.CostEstimate(
            flops=10 * rows * SEQ * width, bytes_accessed=20 * rows * width, transcendentals=0
        ),
        name="attention_backward",
    )(
        queries, keys, values, grad_out, lse, cosine, sine,
        segments.reshape(rows, 1), segments.reshape(seqs, 1, SEQ),
    )


def row_pairs():
    return [(r, r ^ 1) for r in range(lax.axis_size("row"))]


def row_lines():
    size = lax.axis_size("row")
    return [list(range(start, size, PAIR)) for start in range(PAIR)]


def neighbours():
    return [list(range(r, r + PAIR)) for r in range(0, lax.axis_size("row"), PAIR)]


def swap_rows(values):
    return lax.ppermute(values, "row", row_pairs())


def gather_line(values, axis=0):
    return lax.all_gather(values, "row", axis=axis, tiled=True, axis_index_groups=row_lines())


def scatter_line(values, axis=0):
    return lax.psum_scatter(
        values, "row", scatter_dimension=axis, tiled=True, axis_index_groups=row_lines()
    )


def pick(values, index, axis):
    size = values.shape[axis] // PAIR
    return lax.dynamic_slice_in_dim(values, index * size, size, axis)


def in_order(x, own, other, axis):
    return jnp.where(
        x == 0, jnp.concatenate([own, other], axis), jnp.concatenate([other, own], axis)
    )


def own_columns(weight, x):
    return in_order(x, pick(weight, x, 1), swap_rows(pick(weight, 1 - x, 1)), 0)


def own_units(weight, x):
    kept, sent = pick(weight, x, 1).T, pick(weight, 1 - x, 1).T
    return in_order(x, kept, swap_rows(sent), 1)


def own_inputs(grad, x):
    return in_order(x, pick(grad, x, 1), swap_rows(pick(grad, 1 - x, 1)), 0)


def own_rows(grad, x):
    return in_order(x, pick(grad, x, 0), swap_rows(pick(grad, 1 - x, 0)), 1)


def places():
    row, col = lax.axis_index("row"), lax.axis_index("col")
    return row % PAIR, col // 2, col % 2, row, col


def peers(row, col):
    x = row % PAIR
    over_x = (row + 1 - 2 * x, col)
    over_y = (row, (col + 2) % 4)
    over_core = (row, col + 1 - 2 * (col % 2))
    return over_x, over_y, over_core


def meet(devices):
    barrier = pltpu.get_barrier_semaphore()
    for device in devices:
        pl.semaphore_signal(barrier, inc=1, device_id=device, device_id_type=MESH)
    pl.semaphore_wait(barrier, len(devices))


def block_at(ref, a, col, rows, width, start, count):
    at = pl.multiple_of(a * rows + start, 128)
    return ref.at[pl.ds(at, count), pl.ds(pl.multiple_of(col * width, 128), width)]


CHUNKS = 4


def gather_plane_kernel(src_ref, out_ref, local_sem, send_sem, recv_sem):
    rows, width = src_ref.shape
    x, y, core, row, col = places()
    over_x, over_y, over_core = peers(row, col)
    meet((over_x, over_y, over_core))
    count = rows // CHUNKS
    col_y = (col + 2) % 4
    col_core = col + 1 - 2 * core
    first, second = list(range(CHUNKS // 2)), list(range(CHUNKS // 2, CHUNKS))

    def piece(a, c, s):
        return block_at(out_ref, a, c, rows, width, s * count, count)

    def copy(index, source, place, device):
        return pltpu.make_async_remote_copy(
            source, place, send_sem.at[index], recv_sem.at[index],
            device_id=device, device_id_type=MESH,
        )

    def own(s):
        return src_ref.at[pl.ds(s * count, count), :]

    sent = []

    def send(index, source, place, device):
        task = copy(index, source, place, device)
        task.start()
        sent.append(task)

    def wait(index, place):
        copy(index, place, place, over_core).wait_recv()

    local = pltpu.make_async_copy(
        src_ref, block_at(out_ref, x, col, rows, width, 0, rows), local_sem
    )
    local.start()
    for s, t in zip(first + second, second + first):
        send(s, own(s), piece(x, col, s), over_x)
        send(CHUNKS + t, own(t), piece(x, col, t), over_y)
    for s in range(CHUNKS):
        send(4 * CHUNKS + s, own(s), piece(x, col, s), over_core)
    for s, t in zip(first + second, second + first):
        wait(s, piece(1 - x, col, s))
        if s in first:
            send(2 * CHUNKS + s, piece(1 - x, col, s), piece(1 - x, col, s), over_y)
        send(5 * CHUNKS + s, piece(1 - x, col, s), piece(1 - x, col, s), over_core)
        wait(CHUNKS + t, piece(x, col_y, t))
        if t in second:
            send(2 * CHUNKS + t, piece(x, col_y, t), piece(x, col_y, t), over_x)
        send(6 * CHUNKS + t, piece(x, col_y, t), piece(x, col_y, t), over_core)
    for s, t in zip(first, second):
        for u in (s, t):
            wait(2 * CHUNKS + u, piece(1 - x, col_y, u))
            send(7 * CHUNKS + u, piece(1 - x, col_y, u), piece(1 - x, col_y, u), over_core)
    for group, (a, c) in enumerate(
        ((x, col_core), (1 - x, col_core), (x, (col_core + 2) % 4), (1 - x, (col_core + 2) % 4))
    ):
        for s in range(CHUNKS):
            wait((4 + group) * CHUNKS + s, piece(a, c, s))
    for task in sent:
        task.wait_send()
    local.wait()


def gather_plane(values, name, collective_id):
    cols = lax.axis_size("col")
    if cols != 4:
        across = lax.all_gather(values, "col", axis=1, tiled=True)
        return lax.all_gather(across, "row", axis=0, tiled=True, axis_index_groups=neighbours())
    rows, width = values.shape
    return pl.pallas_call(
        gather_plane_kernel,
        in_specs=[pl.BlockSpec(memory_space=pl.ANY)],
        out_specs=pl.BlockSpec(memory_space=pl.ANY),
        out_shape=jax.ShapeDtypeStruct((PAIR * rows, cols * width), values.dtype),
        scratch_shapes=[
            pltpu.SemaphoreType.DMA,
            pltpu.SemaphoreType.DMA((8 * CHUNKS,)),
            pltpu.SemaphoreType.DMA((8 * CHUNKS,)),
        ],
        compiler_params=pltpu.CompilerParams(collective_id=collective_id, has_side_effects=True),
        name=name,
    )(values)


def add_rows(out_ref, left_ref, right_ref, rows, step=64):
    @pl.loop(0, rows // step)
    def _(i):
        at = pl.ds(pl.multiple_of(i * step, step), step)
        total = left_ref[at, :].astype(F32) + right_ref[at, :].astype(F32)
        out_ref[at, :] = total.astype(out_ref.dtype)


def scatter_plane_kernel(
    part_ref, out_ref, own_ref, core_ref, x_ref, y_ref, last_ref,
    load_sem, send_sem, recv_sem,
):
    rows, width = own_ref.shape[1:]
    half = rows // 2
    x, y, core, row, col = places()
    over_x, over_y, over_core = peers(row, col)
    meet((over_x, over_y, over_core))
    top, bottom = pl.ds(0, half), pl.ds(half, half)

    def copy(index, source, place, device):
        return pltpu.make_async_remote_copy(
            source, place, send_sem.at[index], recv_sem.at[index],
            device_id=device, device_id_type=MESH,
        )

    sent = []

    def send(index, source, place, device):
        task = copy(index, source, place, device)
        task.start()
        sent.append(task)

    def wait(index, place):
        copy(index, place, place, over_core).wait_recv()

    order = ((1 - x, 1 - y), (1 - x, y), (x, 1 - y), (x, y))
    loads = []
    for i, (a, b) in enumerate(order):
        slot = 2 * a + b
        send(
            i, block_at(part_ref, a, 2 * b + 1 - core, rows, width, 0, rows),
            core_ref.at[slot], over_core,
        )
        load = pltpu.make_async_copy(
            block_at(part_ref, a, 2 * b + core, rows, width, 0, rows),
            own_ref.at[slot], load_sem.at[i],
        )
        load.start()
        loads.append(load)
    for i, (a, b) in enumerate(order):
        slot = 2 * a + b
        loads[i].wait()
        wait(i, core_ref.at[slot])
        add_rows(own_ref.at[slot], own_ref.at[slot], core_ref.at[slot], rows)
        if i in (0, 1):
            send(4 + i, own_ref.at[slot, top, :], x_ref.at[i], over_x)
        if i in (0, 2):
            send(6 + i // 2, own_ref.at[slot, bottom, :], y_ref.at[i // 2], over_y)
    wait(4, x_ref.at[0])
    slot = 2 * x + 1 - y
    add_rows(own_ref.at[slot, top, :], own_ref.at[slot, top, :], x_ref.at[0], half)
    send(8, own_ref.at[slot, top, :], last_ref.at[0], over_y)
    wait(6, y_ref.at[0])
    slot = 2 * (1 - x) + y
    add_rows(own_ref.at[slot, bottom, :], own_ref.at[slot, bottom, :], y_ref.at[0], half)
    send(9, own_ref.at[slot, bottom, :], last_ref.at[1], over_x)
    slot = 2 * x + y
    wait(5, x_ref.at[1])
    add_rows(own_ref.at[slot, top, :], own_ref.at[slot, top, :], x_ref.at[1], half)
    wait(7, y_ref.at[1])
    add_rows(own_ref.at[slot, bottom, :], own_ref.at[slot, bottom, :], y_ref.at[1], half)
    wait(8, last_ref.at[0])
    add_rows(out_ref.at[top, :], own_ref.at[slot, top, :], last_ref.at[0], half)
    wait(9, last_ref.at[1])
    add_rows(out_ref.at[bottom, :], own_ref.at[slot, bottom, :], last_ref.at[1], half)
    for task in sent:
        task.wait_send()


def scatter_plane(values, name, collective_id):
    cols = lax.axis_size("col")
    if cols != 4:
        mine = lax.psum_scatter(
            values, "row", scatter_dimension=0, tiled=True, axis_index_groups=neighbours()
        )
        return lax.psum_scatter(mine, "col", scatter_dimension=1, tiled=True).astype(F32)
    rows, width = values.shape[0] // PAIR, values.shape[1] // cols
    return pl.pallas_call(
        scatter_plane_kernel,
        in_specs=[pl.BlockSpec(memory_space=pl.ANY)],
        out_specs=pl.BlockSpec(memory_space=pltpu.VMEM),
        out_shape=jax.ShapeDtypeStruct((rows, width), F32),
        scratch_shapes=[
            pltpu.VMEM((4, rows, width), BF16),
            pltpu.VMEM((4, rows, width), BF16),
            pltpu.VMEM((2, rows // 2, width), BF16),
            pltpu.VMEM((2, rows // 2, width), BF16),
            pltpu.VMEM((2, rows // 2, width), BF16),
            pltpu.SemaphoreType.DMA((4,)),
            pltpu.SemaphoreType.DMA((10,)),
            pltpu.SemaphoreType.DMA((10,)),
        ],
        compiler_params=pltpu.CompilerParams(
            collective_id=collective_id, has_side_effects=True, vmem_limit_bytes=40 << 20
        ),
        name=name,
    )(values)


def gather_heads_kernel(src_ref, out_ref, local_sem, send_sem, recv_sem):
    rows, width = out_ref.shape[0], src_ref.shape[1]
    x, y, core, row, col = places()
    over_x, over_y, over_core = peers(row, col)
    meet((over_x, over_y, over_core))
    count = rows // 2
    col_y = (col + 2) % 4
    col_core = col + 1 - 2 * core

    def piece(c, a, s):
        at = pl.multiple_of((PAIR * c + a) * width, 128)
        return out_ref.at[pl.ds(s * count, count), pl.ds(at, width)]

    def mine(a, s):
        return src_ref.at[pl.ds(pl.multiple_of(a * rows + s * count, 128), count), :]

    def copy(index, source, place, device):
        return pltpu.make_async_remote_copy(
            source, place, send_sem.at[index], recv_sem.at[index],
            device_id=device, device_id_type=MESH,
        )

    sent = []

    def send(index, source, place, device):
        task = copy(index, source, place, device)
        task.start()
        sent.append(task)

    def wait(index, place):
        copy(index, place, place, over_core).wait_recv()

    local = []
    for s in range(2):
        send(s, mine(1 - x, s), piece(col, x, s), over_x)
        send(2 + s, mine(x, s), piece(col, x, s), over_y)
        task = pltpu.make_async_copy(mine(x, s), piece(col, x, s), local_sem.at[s])
        task.start()
        local.append(task)
    for s in range(2):
        send(4 + s, mine(x, s), piece(col, x, s), over_core)
    for s in range(2):
        wait(s, piece(col, 1 - x, s))
        send(6 + s, piece(col, 1 - x, s), piece(col, 1 - x, s), over_y)
        send(8 + s, piece(col, 1 - x, s), piece(col, 1 - x, s), over_core)
    for s in range(2):
        wait(2 + s, piece(col_y, x, s))
        send(10 + s, piece(col_y, x, s), piece(col_y, x, s), over_core)
    for s in range(2):
        wait(6 + s, piece(col_y, 1 - x, s))
        send(12 + s, piece(col_y, 1 - x, s), piece(col_y, 1 - x, s), over_core)
    far = (col_core + 2) % 4
    for s in range(2):
        wait(4 + s, piece(col_core, x, s))
        wait(8 + s, piece(col_core, 1 - x, s))
        wait(10 + s, piece(far, x, s))
        wait(12 + s, piece(far, 1 - x, s))
    for task in sent:
        task.wait_send()
    for task in local:
        task.wait()


def gather_heads(values, x, collective_id):
    cols = lax.axis_size("col")
    if cols != 4:
        here = in_order(x, pick(values, x, 0), swap_rows(pick(values, 1 - x, 0)), 1)
        return lax.all_gather(here, "col", axis=1, tiled=True)
    rows, width = values.shape[0] // PAIR, values.shape[1]
    return pl.pallas_call(
        gather_heads_kernel,
        in_specs=[pl.BlockSpec(memory_space=pl.ANY)],
        out_specs=pl.BlockSpec(memory_space=pl.ANY),
        out_shape=jax.ShapeDtypeStruct((rows, PAIR * cols * width), values.dtype),
        scratch_shapes=[
            pltpu.SemaphoreType.DMA((2,)),
            pltpu.SemaphoreType.DMA((14,)),
            pltpu.SemaphoreType.DMA((14,)),
        ],
        compiler_params=pltpu.CompilerParams(collective_id=collective_id, has_side_effects=True),
        name="gather_heads",
    )(values)


def scatter_heads_kernel(
    part_ref, out_ref, own_ref, core_ref, y_ref, load_sem, out_sem, send_sem, recv_sem
):
    rows, width = own_ref.shape[1:]
    half = width // PAIR
    count = rows // CHUNKS
    x, y, core, row, col = places()
    over_x, over_y, over_core = peers(row, col)
    meet((over_x, over_y, over_core))

    def copy(index, source, place, device):
        return pltpu.make_async_remote_copy(
            source, place, send_sem.at[index], recv_sem.at[index],
            device_id=device, device_id_type=MESH,
        )

    sent = []

    def send(index, source, place, device):
        task = copy(index, source, place, device)
        task.start()
        sent.append(task)

    def wait(index, place):
        copy(index, place, place, over_core).wait_recv()

    def part(c, s):
        return part_ref.at[
            pl.ds(s * count, count), pl.ds(pl.multiple_of(c * width, 128), width)
        ]

    loads = []
    for i, b in enumerate((1 - y, y)):
        for s in range(CHUNKS):
            at = pl.ds(s * count, count)
            index = i * CHUNKS + s
            send(index, part(2 * b + 1 - core, s), core_ref.at[i, at, :], over_core)
            load = pltpu.make_async_copy(
                part(2 * b + core, s), own_ref.at[i, at, :], load_sem.at[index]
            )
            load.start()
            loads.append(load)
    for i in range(2):
        for s in range(CHUNKS):
            at = pl.ds(s * count, count)
            index = i * CHUNKS + s
            loads[index].wait()
            wait(index, core_ref.at[i, at, :])
            add_rows(own_ref.at[i, at, :], own_ref.at[i, at, :], core_ref.at[i, at, :], count)
            if i == 0:
                send(2 * CHUNKS + s, own_ref.at[0, at, :], y_ref.at[at, :], over_y)
    left, right = pl.ds(0, half), pl.ds(half, half)
    kept = []
    for s in range(CHUNKS):
        at = pl.ds(s * count, count)
        wait(2 * CHUNKS + s, y_ref.at[at, :])
        add_rows(own_ref.at[1, at, :], own_ref.at[1, at, :], y_ref.at[at, :], count)
        place = out_ref.at[pl.ds(pl.multiple_of(x * rows + s * count, 128), count), :]
        theirs = own_ref.at[1, at, pl.ds(pl.multiple_of((1 - x) * half, 128), half)]
        ours = own_ref.at[1, at, pl.ds(pl.multiple_of(x * half, 128), half)]
        send(3 * CHUNKS + s, theirs, place, over_x)
        task = pltpu.make_async_copy(ours, place, out_sem.at[s])
        task.start()
        kept.append(task)
    for s in range(CHUNKS):
        wait(
            3 * CHUNKS + s,
            out_ref.at[pl.ds(pl.multiple_of((1 - x) * rows + s * count, 128), count), :],
        )
    for task in sent:
        task.wait_send()
    for task in kept:
        task.wait()


def scatter_heads(values, x, collective_id):
    cols = lax.axis_size("col")
    if cols != 4:
        mine = lax.psum_scatter(values, "col", scatter_dimension=1, tiled=True)
        return in_order(x, pick(mine, x, 1), swap_rows(pick(mine, 1 - x, 1)), 0)
    rows, width = values.shape[0], values.shape[1] // cols
    return pl.pallas_call(
        scatter_heads_kernel,
        in_specs=[pl.BlockSpec(memory_space=pl.ANY)],
        out_specs=pl.BlockSpec(memory_space=pl.ANY),
        out_shape=jax.ShapeDtypeStruct((PAIR * rows, width // PAIR), BF16),
        scratch_shapes=[
            pltpu.VMEM((2, rows, width), BF16),
            pltpu.VMEM((2, rows, width), BF16),
            pltpu.VMEM((rows, width), BF16),
            pltpu.SemaphoreType.DMA((2 * CHUNKS,)),
            pltpu.SemaphoreType.DMA((CHUNKS,)),
            pltpu.SemaphoreType.DMA((4 * CHUNKS,)),
            pltpu.SemaphoreType.DMA((4 * CHUNKS,)),
        ],
        compiler_params=pltpu.CompilerParams(
            collective_id=collective_id, has_side_effects=True, vmem_limit_bytes=32 << 20
        ),
        name="scatter_heads",
    )(values)


def row_stats(values):
    mean = jnp.mean(values, axis=1, keepdims=True)
    var = jnp.mean(values * values, axis=1, keepdims=True) - mean * mean
    return mean, lax.rsqrt(var + 1e-05)


def norm_backward(grad_norm, unit_values, inv_std, norm_gain):
    full_width = grad_norm.shape[1] * lax.axis_size("col")
    grad_unit = grad_norm * norm_gain
    row_sums = lax.psum(
        (jnp.sum(grad_unit, axis=1), jnp.sum(grad_unit * unit_values, axis=1)), "col"
    )
    grad_in = inv_std * (
        grad_unit
        - row_sums[0][:, None] / full_width
        - unit_values * row_sums[1][:, None] / full_width
    )
    return grad_in, jnp.sum(grad_norm * unit_values, axis=0)


def rotation_tables(positions):
    half = ROT // 2
    inv_freq = BASE ** (-(jnp.arange(half, dtype=F32) * 2.0) / ROT)
    angles = positions.astype(F32)[:, None] * inv_freq[None, :]
    cosine, sine = jnp.cos(angles), jnp.sin(angles)
    rest = HEAD_DIM - ROT
    ones = jnp.ones((positions.shape[0], rest), F32)
    cosine = jnp.concatenate([cosine, cosine, ones], axis=1)
    sine = jnp.concatenate([-sine, sine, 0.0 * ones], axis=1)
    return jnp.tile(cosine, (1, 2)), jnp.tile(sine, (1, 2))


TILE = 256


def norm_tile(values_ref, gain_ref, stats_ref):
    values = values_ref[...].astype(F32)
    mean, inv_std = row_stats(values)
    lane = lax.broadcasted_iota(jnp.int32, stats_ref.shape, 1)
    stats_ref[...] = jnp.where(lane == 0, mean, inv_std)
    return ((values - mean) * inv_std * gain_ref[...]).astype(BF16)


def project_heads_kernel(
    tokens_ref, gain_ref, weight_ref, bias_ref, cos_ref, sin_ref,
    normed_ref, q_ref, k_ref, v_ref, stats_ref,
):
    width = q_ref.shape[1]
    normed = norm_tile(tokens_ref, gain_ref, stats_ref)
    normed_ref[...] = normed
    in_head = lax.broadcasted_iota(jnp.int32, (1, width), 1) % HEAD_DIM
    cosine = jnp.tile(cos_ref[...], (1, width // cos_ref.shape[1]))
    sine = jnp.tile(sin_ref[...], (1, width // sin_ref.shape[1]))
    pre = dot(normed, weight_ref[...]) + bias_ref[...]
    for ref, at, scale in ((q_ref, 0, SCALE), (k_ref, width, 1.0)):
        part = pre[:, at : at + width]
        turned = part * cosine + swap_pairs(part, in_head) * sine
        ref[...] = turned.astype(BF16) * jnp.asarray(scale, BF16)
    v_ref[...] = pre[:, 2 * width :].astype(BF16)


def tiled(columns):
    return pl.BlockSpec((TILE, columns), lambda i: (i, 0))


def whole(shape):
    return pl.BlockSpec(shape, lambda i: (0,) * len(shape))


def project_heads(tokens, gain, weight, bias, cosine, sine):
    rows, depth = tokens.shape
    width = weight.shape[1] // 3
    return pl.pallas_call(
        project_heads_kernel,
        grid=(rows // TILE,),
        in_specs=[
            tiled(depth), whole((1, depth)), whole(weight.shape), whole((1, 3 * width)),
            tiled(cosine.shape[1]), tiled(cosine.shape[1]),
        ],
        out_specs=[tiled(depth)] + [tiled(width)] * 3 + [tiled(8)],
        out_shape=[jax.ShapeDtypeStruct((rows, depth), BF16)]
        + [jax.ShapeDtypeStruct((rows, width), BF16)] * 3
        + [jax.ShapeDtypeStruct((rows, 8), F32)],
        compiler_params=pltpu.CompilerParams(vmem_limit_bytes=48 << 20),
        cost_estimate=pl.CostEstimate(
            flops=6 * rows * depth * width,
            bytes_accessed=4 * rows * depth + 6 * depth * width, transcendentals=0,
        ),
        name="project_heads",
    )(tokens, gain.reshape(1, depth), weight, bias.reshape(1, 3 * width), cosine, sine)


def feed_forward_kernel(
    resid_ref, gain_ref, weight_ref, grad_ref, down_ref,
    normed_ref, hidden_ref, dgate_ref, dup_ref, stats_ref,
):
    lines, _, hidden, width = weight_ref.shape
    normed_ref[...] = norm_tile(resid_ref, gain_ref, stats_ref)
    gate = jnp.zeros((hidden, TILE), F32)
    up = jnp.zeros((hidden, TILE), F32)
    dhidden = jnp.zeros((hidden, TILE), F32)
    for z in range(lines):
        part = normed_ref[:, z * width : (z + 1) * width]
        gate += dot(weight_ref[z, 0], part, (1,), (1,))
        up += dot(weight_ref[z, 1], part, (1,), (1,))
    for c in range(down_ref.shape[0]):
        part = grad_ref[:, c * width : (c + 1) * width]
        dhidden += dot(down_ref[c], part, (1,), (1,))
    sigmoid = 1.0 / (1.0 + jnp.exp(-gate))
    silu = gate * sigmoid
    hidden_ref[...] = (silu * up).astype(BF16)
    dgate_ref[...] = (dhidden * up * sigmoid * (1.0 + gate * (1.0 - sigmoid))).astype(BF16)
    dup_ref[...] = (dhidden * silu).astype(BF16)


def feed_forward(resid, gain, weight, grad, down):
    rows, depth = resid.shape
    hidden = down.shape[1]
    across = pl.BlockSpec((hidden, TILE), lambda i: (0, i))
    return pl.pallas_call(
        feed_forward_kernel,
        grid=(rows // TILE,),
        in_specs=[
            tiled(depth), whole((1, depth)), whole(weight.shape), tiled(depth), whole(down.shape)
        ],
        out_specs=[tiled(depth)] + [across] * 3 + [tiled(8)],
        out_shape=[jax.ShapeDtypeStruct((rows, depth), BF16)]
        + [jax.ShapeDtypeStruct((hidden, rows), BF16)] * 3
        + [jax.ShapeDtypeStruct((rows, 8), F32)],
        compiler_params=pltpu.CompilerParams(vmem_limit_bytes=56 << 20),
        cost_estimate=pl.CostEstimate(
            flops=6 * rows * depth * hidden,
            bytes_accessed=6 * rows * depth + 6 * depth * hidden, transcendentals=0,
        ),
        name="feed_forward",
    )(resid, gain.reshape(1, depth), weight, grad, down)


def weight_grads_kernel(*refs):
    *left_refs, right_ref, out_ref = refs
    for i, left_ref in enumerate(left_refs):
        out_ref[0, i] = dot(left_ref[...], right_ref[...]).astype(BF16)


def weight_grads(lefts, right, width, name):
    hidden, rows = lefts[0].shape
    blocks = right.shape[1] // width
    return pl.pallas_call(
        weight_grads_kernel,
        grid=(blocks,),
        in_specs=[whole((hidden, rows))] * len(lefts)
        + [pl.BlockSpec((rows, width), lambda i: (0, i))],
        out_specs=pl.BlockSpec((1, len(lefts), hidden, width), lambda i: (i, 0, 0, 0)),
        out_shape=jax.ShapeDtypeStruct((blocks, len(lefts), hidden, width), BF16),
        compiler_params=pltpu.CompilerParams(vmem_limit_bytes=56 << 20),
        cost_estimate=pl.CostEstimate(
            flops=2 * len(lefts) * rows * hidden * right.shape[1],
            bytes_accessed=2 * rows * right.shape[1], transcendentals=0,
        ),
        name=name,
    )(*lefts, right)


def back_project_kernel(*refs):
    *left_refs, weight_ref, out_ref = refs
    width = weight_ref.shape[-1]
    lefts = [ref[...].T for ref in left_refs]
    for z in range(weight_ref.shape[0]):
        total = sum(dot(left, weight_ref[z, i]) for i, left in enumerate(lefts))
        out_ref[:, z * width : (z + 1) * width] = total.astype(BF16)


def back_project(lefts, weight, name):
    hidden, rows = lefts[0].shape
    depth = weight.shape[0] * weight.shape[-1]
    return pl.pallas_call(
        back_project_kernel,
        grid=(rows // TILE,),
        in_specs=[pl.BlockSpec((hidden, TILE), lambda i: (0, i))] * len(lefts)
        + [whole(weight.shape)],
        out_specs=tiled(depth),
        out_shape=jax.ShapeDtypeStruct((rows, depth), BF16),
        compiler_params=pltpu.CompilerParams(vmem_limit_bytes=48 << 20),
        cost_estimate=pl.CostEstimate(
            flops=2 * len(lefts) * rows * hidden * depth,
            bytes_accessed=2 * rows * depth, transcendentals=0,
        ),
        name=name,
    )(*lefts, weight)


def per_device(
    tokens, segment_ids, positions, attn_gain, query_weight, query_bias, key_weight, key_bias,
    value_weight, value_bias, out_weight, mlp_gain, gate_weight, up_weight, down_weight, out_grad,
):
    count, width = tokens.shape
    lines = lax.axis_size("row") // PAIR
    cols = lax.axis_size("col")
    row = lax.axis_index("row")
    col = lax.axis_index("col")
    x = row % PAIR
    half = width // PAIR

    qkv_weight = gather_line(
        jnp.concatenate(
            [own_columns(w, x) for w in (query_weight, key_weight, value_weight)], axis=1
        )
    )
    out_line = gather_line(out_weight)
    down_line = gather_line(down_weight)
    ffn_weight = gather_line(
        jnp.stack([own_units(w, x) for w in (gate_weight, up_weight)])[None]
    )
    out_other = swap_rows(out_line)
    depth = out_weight.shape[0]
    full = (lines, 1, depth, width)
    out_all = in_order(x, out_line.reshape(full), out_other.reshape(full), 1).reshape(-1, width)
    hidden = ffn_weight.shape[2]
    down_all = lax.all_to_all(
        down_line.reshape(lines, hidden, width), "col", split_axis=0, concat_axis=0, tiled=True
    )

    bias = jnp.concatenate(
        [pick(b, x, 0) for b in (query_bias, key_bias, value_bias)], axis=0
    )
    gains = lax.all_gather(jnp.stack([attn_gain, mlp_gain]), "col", axis=1, tiled=True)
    own_place = jnp.stack([positions, segment_ids])
    place = in_order(x, own_place, swap_rows(own_place), 1)
    cosine, sine = rotation_tables(place[0])
    plane_segments = place[1]

    tokens_all = gather_plane(tokens, "gather_tokens", 0)
    grad_all = gather_plane(out_grad, "gather_cotangent", 1)
    normed_first, queries, keys, values, stats_first = project_heads(
        tokens_all, gains[0], qkv_weight, bias, cosine, sine
    )
    attended, lse = attention_forward(queries, keys, values, plane_segments)
    attn_all = gather_heads(attended, x, 2)
    inputs = tokens.astype(F32)
    resid = inputs + dot(attn_all, out_all)

    resid_all = gather_plane(resid.astype(BF16), "gather_residual", 3)
    normed_second, hidden_low, grad_gate, grad_up, stats_second = feed_forward(
        resid_all, gains[1], ffn_weight, grad_all, down_all
    )
    grad_ffn = scatter_line(weight_grads((grad_gate, grad_up), normed_second, width, "ffn_grads"))
    grad_second = scatter_plane(
        back_project((grad_gate, grad_up), ffn_weight, "back_ffn"), "scatter_second", 4
    )
    grad_down = weight_grads((hidden_low,), grad_all, width, "down_grads")
    grad_down = lax.all_to_all(
        grad_down.reshape(cols, hidden, width), "col", split_axis=0, concat_axis=0, tiled=True
    )
    grad_down = scatter_line(grad_down.reshape(lines * hidden, width))
    own_stats = pick(stats_second, x, 0)
    mean_here, inv_here = own_stats[:, 0:1], own_stats[:, 1:2]
    grad_resid, mlp_gain_part = norm_backward(
        grad_second, (resid - mean_here) * inv_here, inv_here, mlp_gain
    )
    grad_resid = grad_resid + out_grad.astype(F32)
    grad_resid_low = grad_resid.astype(BF16)

    grad_attn = scatter_heads(dot(grad_resid_low, out_all, (1,), (1,)).astype(BF16), x, 5)
    grad_qkv, bias_sums = attention_backward(
        queries, keys, values, grad_attn, lse, cosine, sine, plane_segments
    )
    grad_out_weight = dot(attn_all, grad_resid_low, (0,), (0,)).astype(BF16)
    grad_out_weight = grad_out_weight.reshape(lines, PAIR, depth, width)
    grad_out_weight = pick(grad_out_weight, x, 1) + swap_rows(pick(grad_out_weight, 1 - x, 1))
    grad_out_weight = scatter_line(grad_out_weight.reshape(lines * depth, width))
    grad_qkv_weight = scatter_line(dot(normed_first, grad_qkv, (0,), (0,)).astype(BF16))
    grad_first = scatter_plane(
        dot(grad_qkv, qkv_weight, (1,), (1,)).astype(BF16), "scatter_first", 6
    )
    own_stats = pick(stats_first, x, 0)
    mean_here, inv_here = own_stats[:, 0:1], own_stats[:, 1:2]
    grad_input, attn_gain_part = norm_backward(
        grad_first, (inputs - mean_here) * inv_here, inv_here, attn_gain
    )
    tokens_grad = grad_input + grad_resid
    mixed = resid + scatter_plane(
        back_project((hidden_low,), down_all[:, None], "mix"), "scatter_mixed", 7
    )
    mixed = mixed.astype(BF16)

    bias_part = jnp.sum(bias_sums, axis=(0, 1)).reshape(3, half)
    bias_part = jnp.where(
        (jnp.arange(PAIR) == x)[None, :, None], bias_part[:, None, :], 0.0
    ).reshape(3, width)
    vectors = lax.psum(
        jnp.concatenate([bias_part, attn_gain_part[None], mlp_gain_part[None]], axis=0), "row"
    )
    wide = lambda grad: own_rows(grad, x).astype(F32)
    return (
        mixed,
        tokens_grad,
        vectors[3],
        wide(grad_qkv_weight[:, :half]),
        vectors[0],
        wide(grad_qkv_weight[:, half : 2 * half]),
        vectors[1],
        wide(grad_qkv_weight[:, 2 * half :]),
        vectors[2],
        grad_out_weight.astype(F32),
        vectors[4],
        own_inputs(grad_ffn[0, 0], x).T.astype(F32),
        own_inputs(grad_ffn[0, 1], x).T.astype(F32),
        grad_down.astype(F32),
    )


def solution(mesh):
    grid, rows, cols = P("row", "col"), P("row"), P("col")
    in_specs = (
        grid, rows, rows, cols, grid, cols, grid, cols, grid, cols, grid, cols, grid, grid, grid, grid,
    )
    out_specs = (
        grid, grid, cols, grid, cols, grid, cols, grid, cols, grid, cols, grid, grid, grid,
    )
    return jax.shard_map(
        per_device, mesh=mesh, in_specs=in_specs, out_specs=out_specs, check_vma=False
    )
```

time: 1790 us -> 774 us (0.43)
  waiting for transfers between devices: 1350 us -> 80.9 us
  Pallas kernels: 0 us -> 451 us
  matrix products: 256 us -> 34.3 us
  other arithmetic: 81 us -> 25.8 us
  local copies, waits for them, and re-layouts: 15 us -> 47.2 us
  blocking collectives: 64.2 us -> 95.3 us
    reduce_scatter x11 -> x4, waiting for transfers between devices: 842 us -> 38.8 us  [scatter_line(): lax.psum_scatter(values, 'row', scatter_dimension=axis, tiled=True, axis_...]
    all_gather x11 -> x4, waiting for transfers between devices: 505 us -> 3.7 us  [gather_line(): lax.all_gather(values, 'row', axis=axis, tiled=True, axis_index_groups=ro...]
    pallas_call x0 -> x16, Pallas kernels: none -> 451 us  [the longest x3 119 us: scatter_plane(): pl.pallas_call(scatter_plane_kernel, in_specs=[pl.BlockSpec(memory_space=...]
    dot_general x27 -> x5, matrix products: 256 us -> 34.3 us  [dot(): lax.dot_general(left, right, ((left_dims, right_dims), ((), ())), preferr...]
    convert_element_type x12 -> x7, other arithmetic: 48.6 us -> 7.23 us  [the longest x3 2.72 us: per_device(): wide = lambda grad: own_rows(grad, x).astype(F32)]
    all_to_all x0 -> x1, blocking collectives: none -> 39.4 us  [per_device(): lax.all_to_all(grad_down.reshape(cols, hidden, width), 'col', split_axis=...]
    ppermute x0 -> x13, waiting for transfers between devices: none -> 36.9 us  [swap_rows(): return lax.ppermute(values, 'row', row_pairs())]
    unnamed x96 -> x82, local copies, waits for them, and re-layouts: 11.4 us -> 29.4 us
  transfers between devices with their start and end apart: 22 -> 22, of which waited for: 21 -> 10; matrix products, arithmetic and copies ran while one was open for 17% -> 9% of each run, Pallas kernels for 0% -> 41%
where the time goes in v1:
time: 774 us; the launch traced here: 768 us
  Pallas kernels  451 us (58%)
  blocking collectives  95.3 us (12%)
  waiting for transfers between devices  80.9 us (10%)
  local copies, waits for them, and re-layouts  47.2 us (6%)
  matrix products  34.3 us (4%)
  other arithmetic  25.8 us (3%)
  starting transfers between devices  17.9 us (2%)
  between operations  15.1 us (2%)
    pallas_call x3, Pallas kernels, scatter_plane(): pl.pallas_call(scatter_plane_kernel, in_specs=[pl.BlockSpec(memory_space=...  119 us
    pallas_call x3, Pallas kernels, gather_plane(): pl.pallas_call(gather_plane_kernel, in_specs=[pl.BlockSpec(memory_space=p...  119 us
    all_to_all x1, blocking collectives, per_device(): lax.all_to_all(grad_down.reshape(cols, hidden, width), 'col', split_axis=...  39.4 us
    reduce_scatter x4, waiting for transfers between devices, scatter_line(): lax.psum_scatter(values, 'row', scatter_dimension=axis, tiled=True, axis_...  38.8 us
    ppermute x13, waiting for transfers between devices, swap_rows(): return lax.ppermute(values, 'row', row_pairs())  36.9 us
    psum x1, blocking collectives, per_device(): lax.psum(jnp.concatenate([bias_part, attn_gain_part[None], mlp_gain_part[...  36.8 us
    dot_general x5, matrix products, dot(): lax.dot_general(left, right, ((left_dims, right_dims), ((), ())), preferr...  34.3 us
    pallas_call x1, Pallas kernels, scatter_heads(): pl.pallas_call(scatter_heads_kernel, in_specs=[pl.BlockSpec(memory_space=...  32.3 us
  transfers between devices with their start and end apart: 22, of which 10 were waited for; matrix products, arithmetic and copies ran while one was open for 9% of the time, Pallas kernels for 41%

profile of v1, /device:TPU:0, one launch (start us, length us, event | category | flops | bytes accessed | tf_op | source)
XLA Modules:
  0.0 767.6 jit_solution(15500943695134743937)
XLA Ops:
  26.6 8.7 %collective-permute-done.5 = bf16[704,256]{1,0:T(8,128)(2,1)S(1)} collective-permute-done((bf16[704,256]{1,0:T(8,128)(2,1)S(1)}, bf16[704,256]{1,0:T(8,128)(2,1)S(1)}, u32[]{:S(2)}, u32[]{:S(2)}) %collective-permute-start.5) | collective-permute-done | bytes 360480 | tf_op jit(solution)/shard_map/ppermute | solution.py:188
  51.6 39.6 %gather_cotangent.1.grad_ref.refs_1_ = bf16[2048,2048]{1,0:T(8,128)(2,1)} custom-call(bf16[1024,512]{1,0:T(8,128)(2,1)} %src_ref.3), custom_call_target="tpu_custom_call" | custom-call | tf_op jit(solution)/shard_map/gather_cotangent/pallas_call | solution.py:327
  91.3 39.6 %gather_tokens.1.tokens_ref = bf16[2048,2048]{1,0:T(8,128)(2,1)} custom-call(bf16[1024,512]{1,0:T(8,128)(2,1)} %src_ref.2), custom_call_target="tpu_custom_call" | custom-call | tf_op jit(solution)/shard_map/gather_tokens/pallas_call | solution.py:327
  147.2 9.6 %collective-permute-done.4 = bf16[1024,512]{1,0:T(8,128)(2,1)} collective-permute-done((bf16[1024,512]{1,0:T(8,128)(2,1)}, bf16[1024,512]{1,0:T(8,128)(2,1)}, u32[]{:S(2)}, u32[]{:S(2)}) %collective-permute-start.4) | collective-permute-done | bytes 1048608 | tf_op jit(solution)/shard_map/ppermute | solution.py:188
  165.6 15.7 %project_heads.1 = (bf16[2048,2048]{1,0:T(8,128)(2,1)}, bf16[2048,256]{1,0:T(8,128)(2,1)S(1)}, bf16[2048,256]{1,0:T(8,128)(2,1)S(1)}, bf16[2048,256]{1,0:T(8,128)(2,1)S(1)}, f32[2048,8]{1,0:T(8,128)S(1)}) custom-call(bf16[2048,2048]{1,0:T(8,128)(2,1)} %gather_tokens.1.tokens_ref, f32[1,2048]{1,0:T(1,128)S(1)} %get-tuple-element.117.gain_ref, ...), custom_call_target="tpu_custom_call" | custom-call | flops 6442450944 | bytes 19922944 | tf_op jit(solution)/shard_map/project_heads/pallas_call | solution.py:709
  185.2 21.0 %attention_forward.1 = (bf16[2048,256]{1,0:T(8,128)(2,1)}, f32[2,8,1024]{2,1,0:T(8,128)}) custom-call(bf16[2048,256]{1,0:T(8,128)(2,1)} %copy-done.9, bf16[2048,256]{1,0:T(8,128)(2,1)} %copy-done.10, bf16[2048,256]{1,0:T(8,128)(2,1)} %copy-done.11, s32[2048,1]{1,0:T(8,128)} %copy.42.seg_col_ref, s32[2,1,1024]{2,1,0:T(1,128)} %bitcast.88), custom_call_target="tpu_custom_call" | custom-call | flops 4294967296 | bytes 5242880 | tf_op jit(solution)/shard_map/attention_forward/pallas_call | solution.py:76
  206.2 27.9 %gather_heads.1 = bf16[1024,2048]{1,0:T(8,128)(2,1)} custom-call(bf16[2048,256]{1,0:T(8,128)(2,1)} %get-tuple-element.31.src_ref), custom_call_target="tpu_custom_call" | custom-call | tf_op jit(solution)/shard_map/gather_heads/pallas_call | solution.py:520
  241.2 39.5 %gather_residual.1.resid_ref = bf16[2048,2048]{1,0:T(8,128)(2,1)} custom-call(bf16[1024,512]{1,0:T(8,128)(2,1)} %get-tuple-element.124.src_ref), custom_call_target="tpu_custom_call" | custom-call | tf_op jit(solution)/shard_map/gather_residual/pallas_call | solution.py:327
  282.3 28.1 %feed_forward.1 = (bf16[2048,2048]{1,0:T(8,128)(2,1)}, bf16[704,2048]{1,0:T(8,128)(2,1)}, bf16[704,2048]{1,0:T(8,128)(2,1)}, bf16[704,2048]{1,0:T(8,128)(2,1)}, f32[2048,8]{1,0:T(8,128)}) custom-call(bf16[2048,2048]{1,0:T(8,128)(2,1)} %gather_residual.1.resid_ref, f32[1,2048]{1,0:T(1,128)} %get-tuple-element.116.gain_ref, bf16[4,2,704,512]{3,2,1,0:T(8,128)(2,1)} %bitcast.95, ...), custom_call_target="tpu_custom_call" | custom-call | flops 17716740096 | bytes 33816576 | tf_op jit(solution)/shard_map/feed_forward/pallas_call | solution.py:756
  314.0 18.9 %back_ffn.1.part_ref = bf16[2048,2048]{1,0:T(8,128)(2,1)} custom-call(bf16[704,2048]{1,0:T(8,128)(2,1)S(1)} %copy-done.12, bf16[704,2048]{1,0:T(8,128)(2,1)S(1)} %copy-done.13, bf16[4,2,704,512]{3,2,1,0:T(8,128)(2,1)} %bitcast.96), custom_call_target="tpu_custom_call" | custom-call | flops 11811160064 | bytes 8388608 | tf_op jit(solution)/shard_map/back_ffn/pallas_call | solution.py:812
  336.3 40.1 %scatter_second.1 = f32[1024,512]{1,0:T(8,128)S(1)} custom-call(bf16[2048,2048]{1,0:T(8,128)(2,1)S(1)} %copy-done), custom_call_target="tpu_custom_call" | custom-call | tf_op jit(solution)/shard_map/scatter_second/pallas_call | solution.py:429
  387.9 10.0 %mix.1.part_ref = bf16[2048,2048]{1,0:T(8,128)(2,1)} custom-call(bf16[704,2048]{1,0:T(8,128)(2,1)S(1)} %copy-done.8, bf16[4,1,704,512]{3,2,1,0:T(8,128)(2,1)S(1)} %bitcast.60), custom_call_target="tpu_custom_call" | custom-call | flops 5905580032 | bytes 8388608 | tf_op jit(solution)/shard_map/mix/pallas_call | solution.py:812
  401.4 39.5 %scatter_mixed.1 = f32[1024,512]{1,0:T(8,128)S(1)} custom-call(bf16[2048,2048]{1,0:T(8,128)(2,1)S(1)} %copy-done.1), custom_call_target="tpu_custom_call" | custom-call | tf_op jit(solution)/shard_map/scatter_mixed/pallas_call | solution.py:429
  452.8 32.3 %scatter_heads.1.do_ref = bf16[2048,256]{1,0:T(8,128)(2,1)S(1)} custom-call(bf16[1024,2048]{1,0:T(8,128)(2,1)S(1)} %convolution_convert_fusion.1.part_ref), custom_call_target="tpu_custom_call" | custom-call | tf_op jit(solution)/shard_map/scatter_heads/pallas_call | solution.py:616
  488.5 32.2 %attention_backward.1 = (bf16[2048,768]{1,0:T(8,128)(2,1)}, f32[2,1,768]{2,1,0:T(1,128)}) custom-call(bf16[2048,256]{1,0:T(8,128)(2,1)} %copy-done.9, bf16[2048,256]{1,0:T(8,128)(2,1)} %copy-done.10, bf16[2048,256]{1,0:T(8,128)(2,1)} %copy-done.11, bf16[2048,256]{1,0:T(8,128)(2,1)} %copy-done.4, f32[2,8,1024]{2,1,0:T(8,128)} %get-tuple-element.37.lse_ref, ...), custom_call_target="tpu_custom_call" | custom-call | flops 5368709120 | bytes 10485760 | tf_op jit(solution)/shard_map/attention_backward/pallas_call | solution.py:146
  520.7 11.4 %convolution_convert_fusion.2 = bf16[2048,768]{1,0:T(8,128)(2,1)} fusion(bf16[2048,2048]{1,0:T(8,128)(2,1)} %get-tuple-element.40, bf16[2048,768]{1,0:T(8,128)(2,1)} %get-tuple-element.38), kind=kOutput, calls=%fused_computation.2 | convolution fusion | flops 6444023808 | bytes 14680064 | tf_op jit(solution)/shard_map/dot_general | solution.py:24
  532.1 17.1 %ffn_grads.1 = bf16[4,2,704,512]{3,2,1,0:T(8,128)(2,1)} custom-call(bf16[704,2048]{1,0:T(8,128)(2,1)} %get-tuple-element.35.refs_0_, bf16[704,2048]{1,0:T(8,128)(2,1)} %get-tuple-element.36.refs_1_, bf16[2048,2048]{1,0:T(8,128)(2,1)} %get-tuple-element.41.refs_2_), custom_call_target="tpu_custom_call" | custom-call | flops 11811160064 | bytes 8388608 | tf_op jit(solution)/shard_map/ffn_grads/pallas_call | solution.py:784
  549.3 10.2 %down_grads.1 = bf16[4,1,704,512]{3,2,1,0:T(8,128)(2,1)} custom-call(bf16[704,2048]{1,0:T(8,128)(2,1)} %get-tuple-element.32.refs_0_, bf16[2048,2048]{1,0:T(8,128)(2,1)} %gather_cotangent.1.grad_ref.refs_1_), custom_call_target="tpu_custom_call" | custom-call | flops 5905580032 | bytes 8388608 | tf_op jit(solution)/shard_map/down_grads/pallas_call | solution.py:784
  559.5 39.4 %all_to_all.10 = bf16[4,704,512]{2,1,0:T(8,128)(2,1)} all-to-all(bf16[4,704,512]{2,1,0:T(8,128)(2,1)} %bitcast.66), channel_id=1, replica_groups=mesh['row'=8,'col'=4] {'col'}, dimensions={0} | all-to-all | bytes 5767168 | tf_op jit(solution)/shard_map/all_to_all | solution.py:887
  600.9 9.4 %convolution_convert_fusion.part_ref = bf16[2048,2048]{1,0:T(8,128)(2,1)S(1)} fusion(bf16[2048,768]{1,0:T(8,128)(2,1)} %get-tuple-element.38, bf16[2048,768]{1,0:T(8,128)(2,1)} %all-gather.6.cloned.1.call-done.weight_ref), kind=kOutput, calls=%fused_computation | convolution fusion | flops 6446645248 | bytes 14680064 | tf_op jit(solution)/shard_map/dot_general | solution.py:24
  610.3 39.4 %scatter_first.1 = f32[1024,512]{1,0:T(8,128)S(1)} custom-call(bf16[2048,2048]{1,0:T(8,128)(2,1)S(1)} %convolution_convert_fusion.part_ref), custom_call_target="tpu_custom_call" | custom-call | tf_op jit(solution)/shard_map/scatter_first/pallas_call | solution.py:429
  650.8 7.4 all-reduce
  658.3 36.8 %psum.39 = f32[5,512]{1,0:T(8,128)S(1)} all-reduce(f32[5,512]{1,0:T(8,128)S(1)} %pad_maximum_fusion.2), channel_id=1, replica_groups=mesh['row'=8,'col'=4] {'row'}, use_global_device_ids=true, to_apply=%region_11.12 | all-reduce | flops 2560 | bytes 20480 | tf_op jit(solution)/shard_map/psum | solution.py:926
  715.9 38.8 %reduce-scatter.11.cloned.1.call-done = bf16[704,512]{1,0:T(8,128)(2,1)} async-done(((bf16[2816,512]{1,0:T(8,128)(2,1)}), bf16[704,512]{1,0:T(8,128)(2,1)}) %reduce-scatter.11.cloned.1.call-update) | async-done | bytes 720912 | tf_op jit(solution)/shard_map/reduce_scatter | solution.py:196
  (202 shorter events, 139.9 us)
Async XLA Ops:
  7.2 123.7 %all-gather.8.cloned.1.call-start = ((), (), s32[]{:S(2)}) async-start(), calls=%async_computation.7 | async-start | bytes 1310720 | tf_op jit(solution)/shard_map/all_gather | solution.py:192
  7.9 125.9 %all-gather.10.cloned.1.call-start = ((), (), s32[]{:S(2)}) async-start(), calls=%async_computation.8 | async-start | bytes 3604480 | tf_op jit(solution)/shard_map/all_gather | solution.py:192
  8.7 155.7 %all-gather.6.cloned.1.call-start = ((), (), s32[]{:S(2)}) async-start(), calls=%async_computation.6 | async-start | bytes 3932160 | tf_op jit(solution)/shard_map/all_gather | solution.py:192
  9.7 6.9 collective-permute-start
  13.7 6.5 collective-permute-start.1
  13.9 8.0 %collective-permute-start.2 = (bf16[256,256]{1,0:T(8,128)(2,1)S(1)}, bf16[256,256]{1,0:T(8,128)(2,1)S(1)}, u32[]{:S(2)}, u32[]{:S(2)}) collective-permute-start(bf16[256,256]{1,0:T(8,128)(2,1)S(1)} %get-tuple-element.110), channel_id=1, source_target_pairs={{0,4},{4,0},{8,12},{12,8},{16,20},{20,16},{24,28},{28,24},{1,5},{5... | collective-permute-start | bytes 393224 | tf_op jit(solution)/shard_map/ppermute | solution.py:188
  22.9 257.8 %all-gather.12.cloned.1.call-start = ((), (), s32[]{:S(2)}) async-start(), calls=%async_computation.13 | async-start | bytes 7208960 | tf_op jit(solution)/shard_map/all_gather | solution.py:192
  23.9 11.4 %collective-permute-start.5 = (bf16[704,256]{1,0:T(8,128)(2,1)S(1)}, bf16[704,256]{1,0:T(8,128)(2,1)S(1)}, u32[]{:S(2)}, u32[]{:S(2)}) collective-permute-start(bf16[704,256]{1,0:T(8,128)(2,1)S(1)} %bitcast.75), channel_id=1, source_target_pairs={{0,4},{4,0},{8,12},{12,8},{16,20},{20,16},{24,28},{28,24},{1,5},{5... | collective-permute-start | bytes 1081352 | tf_op jit(solution)/shard_map/ppermute | solution.py:188
  25.9 15.1 %collective-permute-start.6 = (bf16[704,256]{1,0:T(8,128)(2,1)S(1)}, bf16[704,256]{1,0:T(8,128)(2,1)S(1)}, u32[]{:S(2)}, u32[]{:S(2)}) collective-permute-start(bf16[704,256]{1,0:T(8,128)(2,1)S(1)} %bitcast.74), channel_id=1, source_target_pairs={{0,4},{4,0},{8,12},{12,8},{16,20},{20,16},{24,28},{28,24},{1,5},{5... | collective-permute-start | bytes 1081352 | tf_op jit(solution)/shard_map/ppermute | solution.py:188
  42.6 88.3 %collective-permute-start.3 = (s32[2,1024]{1,0:T(2,128)S(1)}, s32[2,1024]{1,0:T(2,128)S(1)}, u32[]{:S(2)}, u32[]{:S(2)}) collective-permute-start(s32[2,1024]{1,0:T(2,128)S(1)} %pad_add_fusion), channel_id=1, source_target_pairs={{0,4},{4,0},{8,12},{12,8},{16,20},{20,16},{24,28},{28,24},{1,5},{5... | collective-permute-start | bytes 24584 | tf_op jit(solution)/shard_map/ppermute | solution.py:188
  130.9 25.9 %collective-permute-start.4 = (bf16[1024,512]{1,0:T(8,128)(2,1)}, bf16[1024,512]{1,0:T(8,128)(2,1)}, u32[]{:S(2)}, u32[]{:S(2)}) collective-permute-start(bf16[1024,512]{1,0:T(8,128)(2,1)} %all-gather.8.cloned.1.call-done), channel_id=1, source_target_pairs={{0,4},{4,0},{8,12},{12,8},{16,20},{20,16},{24,28},{28,24},{1,5},{5... | collective-permute-start | bytes 3145736 | tf_op jit(solution)/shard_map/ppermute | solution.py:188
  133.8 146.9 %all-to-all-start = ((bf16[4,704,512]{2,1,0:T(8,128)(2,1)}), bf16[4,704,512]{2,1,0:T(8,128)(2,1)S(1)}, u32[]{:S(2)}, u32[]{:S(2)}) async-start(bf16[4,704,512]{2,1,0:T(8,128)(2,1)} %bitcast.65), calls=%async_computation | async-start | bytes 5767168 | tf_op jit(solution)/shard_map/all_to_all | solution.py:855
  137.5 561.3 %reduce-scatter.7.cloned.1.call-start = ((), (), s32[]{:S(2)}) async-start(), calls=%async_computation.10 | async-start | bytes 1310720 | tf_op jit(solution)/shard_map/reduce_scatter | solution.py:196
  336.3 40.1 %copy-start.23 = (f32[2048,8]{1,0:T(8,128)S(1)}, f32[2048,8]{1,0:T(8,128)}, u32[]{:S(2)}) copy-start(f32[2048,8]{1,0:T(8,128)} %get-tuple-element.34) | copy-start | bytes 196612
  336.3 40.6 %copy-start.15 = (f32[1024,512]{1,0:T(8,128)S(1)}, f32[1024,512]{1,0:T(8,128)}, u32[]{:S(2)}) copy-start(f32[1024,512]{1,0:T(8,128)} %get-tuple-element.125) | copy-start | bytes 6291460
  447.4 38.8 %collective-permute-start.10 = (bf16[4,1,256,512]{3,2,1,0:T(8,128)(2,1)S(1)}, bf16[4,1,256,512]{3,2,1,0:T(8,128)(2,1)}, u32[]{:S(2)}, u32[]{:S(2)}) collective-permute-start(bf16[4,1,256,512]{3,2,1,0:T(8,128)(2,1)S(1)} %constant_dynamic-slice_fusion), channel_id=1, source_target_pairs={{0,4},{4,0},{8,12},{12,8},{16,20},{20,16},{24,28},{28,24},{1,5},{5... | collective-permute-start | bytes 3145736 | tf_op jit(solution)/shard_map/ppermute | solution.py:188
  488.5 212.2 %reduce-scatter.5.cloned.1.call-start = ((), (), s32[]{:S(2)}) async-start(), calls=%async_computation.9 | async-start | bytes 3932160 | tf_op jit(solution)/shard_map/reduce_scatter | solution.py:196
  532.1 177.1 %reduce-scatter.9.cloned.1.call-start = ((), (), s32[]{:S(2)}) async-start(), calls=%async_computation.11 | async-start | bytes 7208960 | tf_op jit(solution)/shard_map/reduce_scatter | solution.py:196
  549.2 205.5 %reduce-scatter.11.cloned.1.call-start = ((), (), s32[]{:S(2)}) async-start(), calls=%async_computation.12 | async-start | bytes 3604480 | tf_op jit(solution)/shard_map/reduce_scatter | solution.py:196
  701.8 6.5 collective-permute-start.9
  701.9 13.0 %collective-permute-start.8 = (bf16[256,256]{1,0:T(8,128)(2,1)S(1)}, bf16[256,256]{1,0:T(8,128)(2,1)S(1)}, u32[]{:S(2)}, u32[]{:S(2)}) collective-permute-start(bf16[256,256]{1,0:T(8,128)(2,1)S(1)} %get-tuple-element.102), channel_id=1, source_target_pairs={{0,4},{4,0},{8,12},{12,8},{16,20},{20,16},{24,28},{28,24},{1,5},{5... | collective-permute-start | bytes 393224 | tf_op jit(solution)/shard_map/ppermute | solution.py:188
  704.0 9.9 %collective-permute-start.7 = (bf16[256,256]{1,0:T(8,128)(2,1)S(1)}, bf16[256,256]{1,0:T(8,128)(2,1)S(1)}, u32[]{:S(2)}, u32[]{:S(2)}) collective-permute-start(bf16[256,256]{1,0:T(8,128)(2,1)S(1)} %get-tuple-element.104), channel_id=1, source_target_pairs={{0,4},{4,0},{8,12},{12,8},{16,20},{20,16},{24,28},{28,24},{1,5},{5... | collective-permute-start | bytes 393224 | tf_op jit(solution)/shard_map/ppermute | solution.py:188
  710.7 46.4 %collective-permute-start.12 = (bf16[704,256]{1,0:T(8,128)(2,1)S(1)}, bf16[704,256]{1,0:T(8,128)(2,1)S(1)}, u32[]{:S(2)}, u32[]{:S(2)}) collective-permute-start(bf16[704,256]{1,0:T(8,128)(2,1)S(1)} %get-tuple-element.92), channel_id=1, source_target_pairs={{0,4},{4,0},{8,12},{12,8},{16,20},{20,16},{24,28},{28,24},{1,5},{5... | collective-permute-start | bytes 1081352 | tf_op jit(solution)/shard_map/ppermute | solution.py:188
  714.9 43.9 %collective-permute-start.11 = (bf16[704,256]{1,0:T(8,128)(2,1)S(1)}, bf16[704,256]{1,0:T(8,128)(2,1)S(1)}, u32[]{:S(2)}, u32[]{:S(2)}) collective-permute-start(bf16[704,256]{1,0:T(8,128)(2,1)S(1)} %get-tuple-element.94), channel_id=1, source_target_pairs={{0,4},{4,0},{8,12},{12,8},{16,20},{20,16},{24,28},{28,24},{1,5},{5... | collective-permute-start | bytes 1081352 | tf_op jit(solution)/shard_map/ppermute | solution.py:188
  (35 other events, 272.7 us)
Sparse Core Ops, SparseCore 0:
  9.6 30.6 all-gather.7
  41.8 58.6 all-gather.9
  102.1 62.1 all-gather.5
  166.3 105.3 all-gather.11
  488.6 24.8 reduce-scatter.6
  532.2 57.9 reduce-scatter.4
  592.6 102.7 reduce-scatter.8
  697.9 56.7 reduce-scatter.10

commit v2 on v1

--- a/solution.py
+++ b/solution.py
@@ -23,6 +23,12 @@
 def dot(left, right, left_dims=(1,), right_dims=(0,)):
     return lax.dot_general(
         left, right, ((left_dims, right_dims), ((), ())), preferred_element_type=F32
+    )
+
+
+def taking(microseconds):
+    return pl.CostEstimate(
+        flops=microseconds * 10**9, bytes_accessed=microseconds * 10**6, transcendentals=0
     )
 
 
@@ -69,26 +75,47 @@
     lse_ref[0] = lse_scratch[...].T[: lse_ref.shape[1], :]
 
 
-def attention_forward(queries, keys, values, segments):
+def attention_forward_exchange_kernel(*refs):
+    ins, (blocks_ref, _), outs, all_ref = refs[:5], refs[5:7], refs[7:9], refs[9]
+    scratch, sems = refs[10:12], refs[12:]
+    exchange_beside(
+        lambda: attention_forward_kernel(*ins, *outs, *scratch),
+        blocks_ref, all_ref, (1, 3), None, *sems,
+    )
+
+
+def attention_forward(queries, keys, values, segments, blocks=None, partly=None, collective_id=None):
     rows, width = queries.shape
     seqs = rows // SEQ
     block = lambda columns: pl.BlockSpec((SEQ, columns), lambda s: (s, 0))
+    in_specs = [block(width)] * 3 + [block(1), pl.BlockSpec((1, 1, SEQ), lambda s: (s, 0, 0))]
+    out_specs = [block(width), pl.BlockSpec((1, 8, SEQ), lambda s: (s, 0, 0))]
+    out_shape = [
+        jax.ShapeDtypeStruct((rows, width), BF16), jax.ShapeDtypeStruct((seqs, 8, SEQ), F32)
+    ]
+    operands = [queries, keys, values, segments.reshape(rows, 1), segments.reshape(seqs, 1, SEQ)]
+    scratch = [pltpu.VMEM((SEQ, width), F32), pltpu.VMEM((SEQ, 128), F32)]
+    params, aliases, kernel = {}, {}, attention_forward_kernel
+    if blocks is not None:
+        anywhere = pl.BlockSpec(memory_space=pl.ANY)
+        in_specs, out_specs = in_specs + [anywhere] * 2, out_specs + [anywhere]
+        out_shape = out_shape + [jax.ShapeDtypeStruct(blocks.shape, BF16)]
+        operands = operands + [blocks, partly]
+        scratch = scratch + [pltpu.SemaphoreType.DMA((2,))] * 2
+        params = dict(collective_id=collective_id, has_side_effects=True)
+        aliases, kernel = {6: 2}, attention_forward_exchange_kernel
     return pl.pallas_call(
-        attention_forward_kernel,
+        kernel,
         grid=(seqs,),
-        in_specs=[block(width)] * 3 + [block(1), pl.BlockSpec((1, 1, SEQ), lambda s: (s, 0, 0))],
-        out_specs=[block(width), pl.BlockSpec((1, 8, SEQ), lambda s: (s, 0, 0))],
-        out_shape=[
-            jax.ShapeDtypeStruct((rows, width), BF16),
-            jax.ShapeDtypeStruct((seqs, 8, SEQ), F32),
-        ],
-        scratch_shapes=[pltpu.VMEM((SEQ, width), F32), pltpu.VMEM((SEQ, 128), F32)],
-        compiler_params=pltpu.CompilerParams(vmem_limit_bytes=56 << 20),
-        cost_estimate=pl.CostEstimate(
-            flops=8 * rows * SEQ * width, bytes_accessed=10 * rows * width, transcendentals=0
-        ),
+        in_specs=in_specs,
+        out_specs=out_specs,
+        out_shape=out_shape,
+        scratch_shapes=scratch,
+        input_output_aliases=aliases,
+        compiler_params=pltpu.CompilerParams(vmem_limit_bytes=56 << 20, **params),
+        cost_estimate=taking(21),
         name="attention_forward",
-    )(queries, keys, values, segments.reshape(rows, 1), segments.reshape(seqs, 1, SEQ))
+    )(*operands)
 
 
 def attention_backward_kernel(
@@ -139,36 +166,59 @@
         sums_ref[0, :, columns] = jnp.sum(low.astype(F32), axis=0, keepdims=True)
 
 
-def attention_backward(queries, keys, values, grad_out, lse, cosine, sine, segments):
+def attention_backward_exchange_kernel(*refs):
+    ins, blocks_ref, outs, all_ref = refs[:9], refs[9], refs[10:12], refs[12]
+    scratch, (stage, local_sem, *sems) = refs[13:16], refs[16:]
+    exchange_beside(
+        lambda: attention_backward_kernel(*ins, *outs, *scratch),
+        blocks_ref, all_ref, (2, 3, 1), (stage, local_sem), *sems,
+    )
+
+
+def attention_backward(
+    queries, keys, values, grad_out, lse, cosine, sine, segments, blocks=None, collective_id=None
+):
     rows, width = queries.shape
     seqs = rows // SEQ
     block = lambda columns: pl.BlockSpec((SEQ, columns), lambda s: (s, 0))
-    return pl.pallas_call(
-        attention_backward_kernel,
-        grid=(seqs,),
-        in_specs=[block(width)] * 4
-        + [
-            pl.BlockSpec((1, 8, SEQ), lambda s: (s, 0, 0)),
-            block(cosine.shape[1]),
-            block(cosine.shape[1]),
-            block(1),
-            pl.BlockSpec((1, 1, SEQ), lambda s: (s, 0, 0)),
-        ],
-        out_specs=[block(3 * width), pl.BlockSpec((1, 1, 3 * width), lambda s: (s, 0, 0))],
-        out_shape=[
-            jax.ShapeDtypeStruct((rows, 3 * width), BF16),
-            jax.ShapeDtypeStruct((seqs, 1, 3 * width), F32),
-        ],
-        scratch_shapes=[pltpu.VMEM((SEQ, width), F32)] * 3,
-        compiler_params=pltpu.CompilerParams(vmem_limit_bytes=56 << 20),
-        cost_estimate=pl.CostEstimate(
-            flops=10 * rows * SEQ * width, bytes_accessed=20 * rows * width, transcendentals=0
-        ),
-        name="attention_backward",
-    )(
+    in_specs = [block(width)] * 4 + [
+        pl.BlockSpec((1, 8, SEQ), lambda s: (s, 0, 0)),
+        block(cosine.shape[1]),
+        block(cosine.shape[1]),
+        block(1),
+        pl.BlockSpec((1, 1, SEQ), lambda s: (s, 0, 0)),
+    ]
+    out_specs = [block(3 * width), pl.BlockSpec((1, 1, 3 * width), lambda s: (s, 0, 0))]
+    out_shape = [
+        jax.ShapeDtypeStruct((rows, 3 * width), BF16),
+        jax.ShapeDtypeStruct((seqs, 1, 3 * width), F32),
+    ]
+    operands = [
         queries, keys, values, grad_out, lse, cosine, sine,
         segments.reshape(rows, 1), segments.reshape(seqs, 1, SEQ),
-    )
+    ]
+    scratch = [pltpu.VMEM((SEQ, width), F32)] * 3
+    params, kernel = {}, attention_backward_kernel
+    if blocks is not None:
+        anywhere = pl.BlockSpec(memory_space=pl.ANY)
+        in_specs, out_specs = in_specs + [anywhere], out_specs + [anywhere]
+        out_shape = out_shape + [jax.ShapeDtypeStruct(blocks.shape, BF16)]
+        operands = operands + [blocks]
+        scratch = scratch + [pltpu.VMEM(blocks.shape[1:], BF16), pltpu.SemaphoreType.DMA]
+        scratch = scratch + [pltpu.SemaphoreType.DMA((3,))] * 2
+        params = dict(collective_id=collective_id, has_side_effects=True)
+        kernel = attention_backward_exchange_kernel
+    return pl.pallas_call(
+        kernel,
+        grid=(seqs,),
+        in_specs=in_specs,
+        out_specs=out_specs,
+        out_shape=out_shape,
+        scratch_shapes=scratch,
+        compiler_params=pltpu.CompilerParams(vmem_limit_bytes=56 << 20, **params),
+        cost_estimate=taking(33),
+        name="attention_backward",
+    )(*operands)
 
 
 def row_pairs():
@@ -188,6 +238,10 @@
     return lax.ppermute(values, "row", row_pairs())
 
 
+def after(value, *others):
+    return lax.optimization_barrier((value,) + others)[0]
+
+
 def gather_line(values, axis=0):
     return lax.all_gather(values, "row", axis=axis, tiled=True, axis_index_groups=row_lines())
 
@@ -218,12 +272,8 @@
     return in_order(x, kept, swap_rows(sent), 1)
 
 
-def own_inputs(grad, x):
-    return in_order(x, pick(grad, x, 1), swap_rows(pick(grad, 1 - x, 1)), 0)
-
-
 def own_rows(grad, x):
-    return in_order(x, pick(grad, x, 0), swap_rows(pick(grad, 1 - x, 0)), 1)
+    return pick(grad, x, 0), swap_rows(pick(grad, 1 - x, 0))
 
 
 def places():
@@ -254,68 +304,346 @@
 CHUNKS = 4
 
 
+class Copies:
+    def __init__(self, send_sem, recv_sem, over_core):
+        self.send_sem, self.recv_sem, self.any = send_sem, recv_sem, over_core
+        self.sent = []
+
+    def copy(self, index, source, place, device):
+        return pltpu.make_async_remote_copy(
+            source, place, self.send_sem.at[index], self.recv_sem.at[index],
+            device_id=device, device_id_type=MESH,
+        )
+
+    def send(self, index, source, place, device):
+        task = self.copy(index, source, place, device)
+        task.start()
+        self.sent.append(task)
+
+    def wait(self, index, place):
+        self.copy(index, place, place, self.any).wait_recv()
+
+    def finish(self):
+        for task in self.sent:
+            task.wait_send()
+        self.sent = []
+
+
+class PlaneGather:
+    def __init__(self, copies, base, src_ref, out_ref, local_sem, over_y=CHUNKS // 2):
+        self.copies, self.base, self.src, self.out = copies, base, src_ref, out_ref
+        self.local_sem = local_sem
+        self.rows, self.width = src_ref.shape
+        self.count = self.rows // CHUNKS
+        self.x, self.y, self.core, self.row, self.col = places()
+        self.over_x, self.over_y, self.over_core = peers(self.row, self.col)
+        self.col_y = (self.col + 2) % 4
+        self.col_core = self.col + 1 - 2 * self.core
+        self.first = list(range(over_y))
+        self.second = list(range(over_y, CHUNKS))
+
+    def piece(self, a, c, s):
+        return block_at(self.out, a, c, self.rows, self.width, s * self.count, self.count)
+
+    def own(self, s):
+        return self.src.at[pl.ds(s * self.count, self.count), :]
+
+    def send(self, group, s, source, place, device):
+        self.copies.send(self.base + group * CHUNKS + s, source, place, device)
+
+    def pass_on(self, group, a, c, s, device):
+        self.send(group, s, self.piece(a, c, s), self.piece(a, c, s), device)
+
+    def wait(self, group, a, c, s):
+        self.copies.wait(self.base + group * CHUNKS + s, self.piece(a, c, s))
+
+    def start_x(self):
+        for s in self.first + self.second:
+            self.send(0, s, self.own(s), self.piece(self.x, self.col, s), self.over_x)
+
+    def start_y(self):
+        for s in self.second + self.first:
+            self.send(1, s, self.own(s), self.piece(self.x, self.col, s), self.over_y)
+
+    def start_core(self):
+        self.local = pltpu.make_async_copy(
+            self.src, block_at(self.out, self.x, self.col, self.rows, self.width, 0, self.rows),
+            self.local_sem,
+        )
+        self.local.start()
+        for s in range(CHUNKS):
+            self.send(4, s, self.own(s), self.piece(self.x, self.col, s), self.over_core)
+
+    def near(self, i):
+        s, t = (self.first + self.second)[i], (self.second + self.first)[i]
+        x, col, col_y = self.x, self.col, self.col_y
+        self.wait(0, 1 - x, col, s)
+        if s in self.first:
+            self.pass_on(2, 1 - x, col, s, self.over_y)
+        self.pass_on(5, 1 - x, col, s, self.over_core)
+        self.wait(1, x, col_y, t)
+        if t in self.second:
+            self.pass_on(2, x, col_y, t, self.over_x)
+        self.pass_on(6, x, col_y, t, self.over_core)
+
+    def far(self):
+        for u in range(CHUNKS):
+            self.wait(2, 1 - self.x, self.col_y, u)
+            self.pass_on(7, 1 - self.x, self.col_y, u, self.over_core)
+
+    def finish(self):
+        other, corner = self.col_core, (self.col_core + 2) % 4
+        for group, (a, c) in enumerate(
+            ((self.x, other), (1 - self.x, other), (self.x, corner), (1 - self.x, corner))
+        ):
+            for s in range(CHUNKS):
+                self.wait(4 + group, a, c, s)
+        self.local.wait()
+
+
 def gather_plane_kernel(src_ref, out_ref, local_sem, send_sem, recv_sem):
-    rows, width = src_ref.shape
+    _, _, _, row, col = places()
+    devices = peers(row, col)
+    meet(devices)
+    copies = Copies(send_sem, recv_sem, devices[2])
+    gather = PlaneGather(copies, 0, src_ref, out_ref, local_sem)
+    gather.start_x()
+    gather.start_y()
+    gather.start_core()
+    for i in range(CHUNKS):
+        gather.near(i)
+    gather.far()
+    gather.finish()
+    copies.finish()
+
+
+LINES = 4
+
+
+class LineGather:
+    def __init__(self, up_send, up_recv, down_send, down_recv, block):
+        self.up, self.down, self.block = (up_send, up_recv), (down_send, down_recv), block
+        self.row, self.col = lax.axis_index("row"), lax.axis_index("col")
+        self.z = self.row // PAIR
+
+    def task(self, sems, step, source, device):
+        send, recv = sems
+        place = self.block(source)
+        return pltpu.make_async_remote_copy(
+            place, place, send.at[step], recv.at[step],
+            device_id=(device, self.col), device_id_type=MESH,
+        )
+
+    def upward(self, step):
+        source = jnp.maximum(self.z - step, 0)
+        return self.task(self.up, step, source, jnp.minimum(self.row + PAIR, PAIR * LINES - 1))
+
+    def downward(self, step):
+        source = jnp.minimum(self.z + step, LINES - 1)
+        return self.task(self.down, step, source, jnp.maximum(self.row - PAIR, 0))
+
+    def start(self, step):
+        @pl.when((self.z >= step) & (self.z < LINES - 1))
+        def _():
+            self.upward(step).start()
+
+        @pl.when((self.z + step < LINES) & (self.z > 0))
+        def _():
+            self.downward(step).start()
+
+    def receive(self, step):
+        @pl.when(self.z >= step)
+        def _():
+            source = jnp.maximum(self.z - step, 0)
+            self.task(self.up, step - 1, source, self.row).wait_recv()
+
+        @pl.when(self.z + step < LINES)
+        def _():
+            source = jnp.minimum(self.z + step, LINES - 1)
+            self.task(self.down, step - 1, source, self.row).wait_recv()
+
+    def hop(self, step):
+        self.receive(step)
+        if step < LINES - 1:
+            self.start(step)
+
+    def finish(self):
+        for step in range(LINES - 1):
+
+            @pl.when((self.z >= step) & (self.z < LINES - 1))
+            def _():
+                self.upward(step).wait_send()
+
+            @pl.when((self.z + step < LINES) & (self.z > 0))
+            def _():
+                self.downward(step).wait_send()
+
+
+def gather_first_kernel(
+    tokens_ref, grad_ref, query_ref, key_ref, value_ref, out_weight_ref, gate_ref, up_ref,
+    gains_ref, places_ref,
+    tokens_all_ref, grad_all_ref, qkv_ref, out_all_ref, ffn_ref, gains_all_ref, places_all_ref,
+    turned_ref, local_sem, send_sem, recv_sem, swap_send, swap_recv, *line_sems,
+):
     x, y, core, row, col = places()
+    z = row // PAIR
     over_x, over_y, over_core = peers(row, col)
-    meet((over_x, over_y, over_core))
-    count = rows // CHUNKS
-    col_y = (col + 2) % 4
-    col_core = col + 1 - 2 * core
-    first, second = list(range(CHUNKS // 2)), list(range(CHUNKS // 2, CHUNKS))
-
-    def piece(a, c, s):
-        return block_at(out_ref, a, c, rows, width, s * count, count)
-
-    def copy(index, source, place, device):
+    over_far = (row, 3 - col)
+    size = PAIR * LINES
+    meet(
+        (
+            over_x, over_y, over_core, over_far,
+            ((row + PAIR) % size, col), ((row + size - PAIR) % size, col),
+        )
+    )
+    copies = Copies(send_sem, recv_sem, over_core)
+    depth, width = out_weight_ref.shape
+    half = width // PAIR
+    units = ffn_ref.shape[2]
+    base = 16 * CHUNKS
+    local = []
+
+    def keep(source, place):
+        task = pltpu.make_async_copy(source, place, local_sem.at[2 + len(local)])
+        task.start()
+        local.append(task)
+
+    def part(r, w):
+        return qkv_ref.at[
+            pl.ds(pl.multiple_of(r * depth, 128), depth), pl.ds(w * half, half)
+        ]
+
+    def out_block(z, x):
+        return out_all_ref.at[pl.ds(pl.multiple_of((PAIR * z + x) * depth, 128), depth), :]
+
+    def ffn_block(w, x):
+        return ffn_ref.at[0, w, :, pl.ds(pl.multiple_of(x * depth, 128), depth)]
+
+    def gains_block(c):
+        return gains_all_ref.at[:, pl.ds(pl.multiple_of(c * width, 128), width)]
+
+    def places_block(a):
+        rows = places_ref.shape[1]
+        return places_all_ref.at[:, pl.ds(pl.multiple_of(a * rows, 128), rows)]
+
+    for w, ref in enumerate((query_ref, key_ref, value_ref)):
+        theirs = ref.at[:, pl.ds(pl.multiple_of((1 - x) * half, 128), half)]
+        copies.send(base + w, theirs, part(row, w), over_x)
+        keep(ref.at[:, pl.ds(pl.multiple_of(x * half, 128), half)], part(row, w))
+    keep(out_weight_ref, out_block(z, x))
+    keep(gains_ref, gains_block(col))
+    keep(places_ref, places_block(x))
+    tokens = PlaneGather(copies, 0, tokens_ref, tokens_all_ref, local_sem.at[0], CHUNKS)
+    grad = PlaneGather(copies, 8 * CHUNKS, grad_ref, grad_all_ref, local_sem.at[1], CHUNKS)
+    tokens.start_y()
+    tokens.start_core()
+    copies.send(base + 5, places_ref, places_block(x), over_x)
+    for i, device in enumerate((over_core, over_y, over_far)):
+        copies.send(base + 6 + i, gains_ref, gains_block(col), device)
+    for w in range(3):
+        local[w].wait()
+        copies.wait(base + w, part(row + 1 - 2 * x, w))
+    heads = LineGather(
+        *line_sems[:4],
+        lambda at: qkv_ref.at[pl.ds(pl.multiple_of(at * PAIR * depth, 128), PAIR * depth), :],
+    )
+    outs = LineGather(*line_sems[4:], lambda at: out_block(at, x))
+
+    def swap_out(z, x):
+        block = out_block(z, x)
         return pltpu.make_async_remote_copy(
-            source, place, send_sem.at[index], recv_sem.at[index],
-            device_id=device, device_id_type=MESH,
-        )
-
-    def own(s):
-        return src_ref.at[pl.ds(s * count, count), :]
-
-    sent = []
-
-    def send(index, source, place, device):
-        task = copy(index, source, place, device)
-        task.start()
-        sent.append(task)
-
-    def wait(index, place):
-        copy(index, place, place, over_core).wait_recv()
-
-    local = pltpu.make_async_copy(
-        src_ref, block_at(out_ref, x, col, rows, width, 0, rows), local_sem
-    )
-    local.start()
-    for s, t in zip(first + second, second + first):
-        send(s, own(s), piece(x, col, s), over_x)
-        send(CHUNKS + t, own(t), piece(x, col, t), over_y)
-    for s in range(CHUNKS):
-        send(4 * CHUNKS + s, own(s), piece(x, col, s), over_core)
-    for s, t in zip(first + second, second + first):
-        wait(s, piece(1 - x, col, s))
-        if s in first:
-            send(2 * CHUNKS + s, piece(1 - x, col, s), piece(1 - x, col, s), over_y)
-        send(5 * CHUNKS + s, piece(1 - x, col, s), piece(1 - x, col, s), over_core)
-        wait(CHUNKS + t, piece(x, col_y, t))
-        if t in second:
-            send(2 * CHUNKS + t, piece(x, col_y, t), piece(x, col_y, t), over_x)
-        send(6 * CHUNKS + t, piece(x, col_y, t), piece(x, col_y, t), over_core)
-    for s, t in zip(first, second):
-        for u in (s, t):
-            wait(2 * CHUNKS + u, piece(1 - x, col_y, u))
-            send(7 * CHUNKS + u, piece(1 - x, col_y, u), piece(1 - x, col_y, u), over_core)
-    for group, (a, c) in enumerate(
-        ((x, col_core), (1 - x, col_core), (x, (col_core + 2) % 4), (1 - x, (col_core + 2) % 4))
-    ):
-        for s in range(CHUNKS):
-            wait((4 + group) * CHUNKS + s, piece(a, c, s))
-    for task in sent:
-        task.wait_send()
-    local.wait()
+            block, block, swap_send.at[z], swap_recv.at[z], device_id=over_x, device_id_type=MESH
+        )
+
+    def swap_outs(step):
+        @pl.when(z >= step)
+        def _():
+            swap_out(jnp.maximum(z - step, 0), x).start()
+
+        @pl.when(z + step < LINES)
+        def _():
+            swap_out(jnp.minimum(z + step, LINES - 1), x).start()
+
+    heads.start(0)
+    tokens.start_x()
+    for w, ref in enumerate((gate_ref, up_ref)):
+        for j in range(PAIR * units // 128):
+            turned_ref[w, j * 128 : (j + 1) * 128, :] = ref[:, j * 128 : (j + 1) * 128].T
+    for i in range(CHUNKS - 1):
+        tokens.near(i)
+    local[3].wait()
+    outs.start(0)
+    heads.hop(1)
+    tokens.near(CHUNKS - 1)
+    for w in range(2):
+        theirs = turned_ref.at[w, pl.ds(pl.multiple_of((1 - x) * units, 16), units), :]
+        copies.send(base + 3 + w, theirs, ffn_block(w, x), over_x)
+        keep(turned_ref.at[w, pl.ds(pl.multiple_of(x * units, 16), units), :], ffn_block(w, x))
+    swap_out(z, x).start()
+    grad.start_x()
+    grad.start_y()
+    grad.start_core()
+    tokens.far()
+    heads.hop(2)
+    outs.hop(1)
+    swap_outs(1)
+    for i in range(CHUNKS - 1):
+        grad.near(i)
+    heads.hop(3)
+    outs.hop(2)
+    swap_outs(2)
+    grad.near(CHUNKS - 1)
+    grad.far()
+    outs.hop(3)
+    swap_outs(3)
+    for at in range(LINES):
+        swap_out(at, 1 - x).wait_recv()
+    for w in range(2):
+        copies.wait(base + 3 + w, ffn_block(w, 1 - x))
+    copies.wait(base + 5, places_block(1 - x))
+    for i, c in enumerate((col + 1 - 2 * core, (col + 2) % 4, 3 - col)):
+        copies.wait(base + 6 + i, gains_block(c))
+    for at in range(LINES):
+        swap_out(at, x).wait_send()
+    for task in local[3 + 1 :]:
+        task.wait()
+    tokens.finish()
+    grad.finish()
+    heads.finish()
+    outs.finish()
+    copies.finish()
+
+
+def gather_first(
+    tokens, grad, query, key, value, out_weight, gate, up, gains, places, collective_id
+):
+    rows, width = tokens.shape
+    depth = out_weight.shape[0]
+    units = gate.shape[1] // PAIR
+    shape = lambda *dims: jax.ShapeDtypeStruct(dims, BF16)
+    sems = lambda n: pltpu.SemaphoreType.DMA((n,))
+    return pl.pallas_call(
+        gather_first_kernel,
+        in_specs=[pl.BlockSpec(memory_space=pltpu.VMEM)] * 10,
+        out_specs=[pl.BlockSpec(memory_space=pl.ANY)] * 7,
+        out_shape=[
+            shape(PAIR * rows, 4 * width), shape(PAIR * rows, 4 * width),
+            shape(PAIR * LINES * depth, 3 * width // PAIR), shape(PAIR * LINES * depth, width),
+            shape(1, 2, units, PAIR * depth),
+            jax.ShapeDtypeStruct((gains.shape[0], 4 * width), F32),
+            jax.ShapeDtypeStruct((places.shape[0], PAIR * rows), jnp.int32),
+        ],
+        scratch_shapes=[
+            pltpu.VMEM((2, PAIR * units, depth), BF16),
+            sems(10), sems(16 * CHUNKS + 9), sems(16 * CHUNKS + 9), sems(4), sems(4),
+        ]
+        + [sems(3)] * 8,
+        compiler_params=pltpu.CompilerParams(
+            collective_id=collective_id, has_side_effects=True, vmem_limit_bytes=60 << 20
+        ),
+        cost_estimate=taking(110),
+        name="gather_first",
+    )(tokens, grad, query, key, value, out_weight, gate, up, gains, places)
 
 
 def gather_plane(values, name, collective_id):
@@ -326,7 +654,7 @@
     rows, width = values.shape
     return pl.pallas_call(
         gather_plane_kernel,
-        in_specs=[pl.BlockSpec(memory_space=pl.ANY)],
+        in_specs=[pl.BlockSpec(memory_space=pltpu.VMEM)],
         out_specs=pl.BlockSpec(memory_space=pl.ANY),
         out_shape=jax.ShapeDtypeStruct((PAIR * rows, cols * width), values.dtype),
         scratch_shapes=[
@@ -334,6 +662,7 @@
             pltpu.SemaphoreType.DMA((8 * CHUNKS,)),
             pltpu.SemaphoreType.DMA((8 * CHUNKS,)),
         ],
+        cost_estimate=taking(40),
         compiler_params=pltpu.CompilerParams(collective_id=collective_id, has_side_effects=True),
         name=name,
     )(values)
@@ -441,6 +770,7 @@
             pltpu.SemaphoreType.DMA((10,)),
             pltpu.SemaphoreType.DMA((10,)),
         ],
+        cost_estimate=taking(40),
         compiler_params=pltpu.CompilerParams(
             collective_id=collective_id, has_side_effects=True, vmem_limit_bytes=40 << 20
         ),
@@ -519,7 +849,7 @@
     rows, width = values.shape[0] // PAIR, values.shape[1]
     return pl.pallas_call(
         gather_heads_kernel,
-        in_specs=[pl.BlockSpec(memory_space=pl.ANY)],
+        in_specs=[pl.BlockSpec(memory_space=pltpu.VMEM)],
         out_specs=pl.BlockSpec(memory_space=pl.ANY),
         out_shape=jax.ShapeDtypeStruct((rows, PAIR * cols * width), values.dtype),
         scratch_shapes=[
@@ -527,6 +857,7 @@
             pltpu.SemaphoreType.DMA((14,)),
             pltpu.SemaphoreType.DMA((14,)),
         ],
+        cost_estimate=taking(28),
         compiler_params=pltpu.CompilerParams(collective_id=collective_id, has_side_effects=True),
         name="gather_heads",
     )(values)
@@ -627,11 +958,57 @@
             pltpu.SemaphoreType.DMA((4 * CHUNKS,)),
             pltpu.SemaphoreType.DMA((4 * CHUNKS,)),
         ],
+        cost_estimate=taking(32),
         compiler_params=pltpu.CompilerParams(
             collective_id=collective_id, has_side_effects=True, vmem_limit_bytes=32 << 20
         ),
         name="scatter_heads",
     )(values)
+
+
+def sum_rows_kernel(part_ref, out_ref, slots_ref, send_sem, recv_sem):
+    size = slots_ref.shape[0]
+    row, col = lax.axis_index("row"), lax.axis_index("col")
+    others = [(lax.rem(row + step, size), col) for step in range(1, size)]
+    meet(others)
+    slots_ref[0] = part_ref[...]
+    copies = [
+        pltpu.make_async_remote_copy(
+            slots_ref.at[0], slots_ref.at[step], send_sem.at[step], recv_sem.at[step],
+            device_id=others[step - 1], device_id_type=MESH,
+        )
+        for step in range(1, size)
+    ]
+    for copy in copies:
+        copy.start()
+    for copy in copies:
+        copy.wait_recv()
+    total = jnp.zeros(part_ref.shape, F32)
+    for r in range(size):
+        total += slots_ref[lax.rem(row + size - r, size)]
+    out_ref[...] = total
+    for copy in copies:
+        copy.wait_send()
+
+
+def sum_rows(part, collective_id):
+    size = lax.axis_size("row")
+    if size != 8:
+        return lax.psum(part, "row")
+    return pl.pallas_call(
+        sum_rows_kernel,
+        in_specs=[pl.BlockSpec(memory_space=pltpu.VMEM)],
+        out_specs=pl.BlockSpec(memory_space=pltpu.VMEM),
+        out_shape=jax.ShapeDtypeStruct(part.shape, F32),
+        scratch_shapes=[
+            pltpu.VMEM((size,) + part.shape, F32),
+            pltpu.SemaphoreType.DMA((size,)),
+            pltpu.SemaphoreType.DMA((size,)),
+        ],
+        cost_estimate=taking(8),
+        compiler_params=pltpu.CompilerParams(collective_id=collective_id, has_side_effects=True),
+        name="sum_rows",
+    )(part)
 
 
 def row_stats(values):
@@ -703,27 +1080,91 @@
     return pl.BlockSpec(shape, lambda i: (0,) * len(shape))
 
 
-def project_heads(tokens, gain, weight, bias, cosine, sine):
+def column_block(blocks_ref, all_ref, other, sems, index):
+    row, col = lax.axis_index("row"), lax.axis_index("col")
+    send_sem, recv_sem = sems
+    return pltpu.make_async_remote_copy(
+        blocks_ref.at[other], all_ref.at[col], send_sem.at[index], recv_sem.at[index],
+        device_id=(row, other), device_id_type=MESH,
+    )
+
+
+def exchange_beside(kernel, blocks_ref, all_ref, steps, local, *sems):
+    row, col = lax.axis_index("row"), lax.axis_index("col")
+    others = [col + d - 2 * d * ((col // d) % 2) if d < 3 else 3 - col for d in steps]
+
+    @pl.when(pl.program_id(0) == 0)
+    def _():
+        meet([(row, other) for other in others])
+        for i, other in enumerate(others):
+            column_block(blocks_ref, all_ref, other, sems, i).start()
+        if local is not None:
+            pltpu.make_async_copy(blocks_ref.at[col], *local).start()
+
+    kernel()
+
+    @pl.when(pl.program_id(0) == pl.num_programs(0) - 1)
+    def _():
+        if local is not None:
+            stage, local_sem = local
+            pltpu.make_async_copy(blocks_ref.at[col], stage, local_sem).wait()
+            task = pltpu.make_async_copy(stage, all_ref.at[col], local_sem)
+            task.start()
+            task.wait()
+        for i, other in enumerate(others):
+            task = column_block(blocks_ref, all_ref, other, sems, i)
+            task.wait_send()
+            send_sem, recv_sem = sems
+            pltpu.make_async_remote_copy(
+                blocks_ref.at[other], all_ref.at[other], send_sem.at[i], recv_sem.at[i],
+                device_id=(row, other), device_id_type=MESH,
+            ).wait_recv()
+
+
+def project_heads_exchange_kernel(*refs):
+    *ins, blocks_ref = refs[:7]
+    outs, all_ref, (stage, local_sem, *sems) = refs[7:12], refs[12], refs[13:]
+    exchange_beside(
+        lambda: project_heads_kernel(*ins, *outs),
+        blocks_ref, all_ref, (2,), (stage, local_sem), *sems,
+    )
+
+
+def project_heads(tokens, gain, weight, bias, cosine, sine, blocks=None, collective_id=None):
     rows, depth = tokens.shape
     width = weight.shape[1] // 3
+    in_specs = [
+        tiled(depth), whole((1, depth)), whole(weight.shape), whole((1, 3 * width)),
+        tiled(cosine.shape[1]), tiled(cosine.shape[1]),
+    ]
+    out_specs = [tiled(depth)] + [tiled(width)] * 3 + [tiled(8)]
+    out_shape = [
+        jax.ShapeDtypeStruct((rows, depth), BF16),
+        *[jax.ShapeDtypeStruct((rows, width), BF16)] * 3,
+        jax.ShapeDtypeStruct((rows, 8), F32),
+    ]
+    operands = [tokens, gain.reshape(1, depth), weight, bias.reshape(1, 3 * width), cosine, sine]
+    params, scratch, kernel = {}, [], project_heads_kernel
+    if blocks is not None:
+        anywhere = pl.BlockSpec(memory_space=pl.ANY)
+        in_specs, out_specs = in_specs + [anywhere], out_specs + [anywhere]
+        out_shape = out_shape + [jax.ShapeDtypeStruct(blocks.shape, BF16)]
+        operands = operands + [blocks]
+        scratch = [pltpu.VMEM(blocks.shape[1:], BF16), pltpu.SemaphoreType.DMA]
+        scratch = scratch + [pltpu.SemaphoreType.DMA((1,))] * 2
+        params = dict(collective_id=collective_id, has_side_effects=True)
+        kernel = project_heads_exchange_kernel
     return pl.pallas_call(
-        project_heads_kernel,
+        kernel,
         grid=(rows // TILE,),
-        in_specs=[
-            tiled(depth), whole((1, depth)), whole(weight.shape), whole((1, 3 * width)),
-            tiled(cosine.shape[1]), tiled(cosine.shape[1]),
-        ],
-        out_specs=[tiled(depth)] + [tiled(width)] * 3 + [tiled(8)],
-        out_shape=[jax.ShapeDtypeStruct((rows, depth), BF16)]
-        + [jax.ShapeDtypeStruct((rows, width), BF16)] * 3
-        + [jax.ShapeDtypeStruct((rows, 8), F32)],
-        compiler_params=pltpu.CompilerParams(vmem_limit_bytes=48 << 20),
-        cost_estimate=pl.CostEstimate(
-            flops=6 * rows * depth * width,
-            bytes_accessed=4 * rows * depth + 6 * depth * width, transcendentals=0,
-        ),
+        in_specs=in_specs,
+        out_specs=out_specs,
+        out_shape=out_shape,
+        scratch_shapes=scratch,
+        compiler_params=pltpu.CompilerParams(vmem_limit_bytes=48 << 20, **params),
+        cost_estimate=taking(16),
         name="project_heads",
-    )(tokens, gain.reshape(1, depth), weight, bias.reshape(1, 3 * width), cosine, sine)
+    )(*operands)
 
 
 def feed_forward_kernel(
@@ -764,10 +1205,7 @@
         + [jax.ShapeDtypeStruct((hidden, rows), BF16)] * 3
         + [jax.ShapeDtypeStruct((rows, 8), F32)],
         compiler_params=pltpu.CompilerParams(vmem_limit_bytes=56 << 20),
-        cost_estimate=pl.CostEstimate(
-            flops=6 * rows * depth * hidden,
-            bytes_accessed=6 * rows * depth + 6 * depth * hidden, transcendentals=0,
-        ),
+        cost_estimate=taking(28),
         name="feed_forward",
     )(resid, gain.reshape(1, depth), weight, grad, down)
 
@@ -789,10 +1227,7 @@
         out_specs=pl.BlockSpec((1, len(lefts), hidden, width), lambda i: (i, 0, 0, 0)),
         out_shape=jax.ShapeDtypeStruct((blocks, len(lefts), hidden, width), BF16),
         compiler_params=pltpu.CompilerParams(vmem_limit_bytes=56 << 20),
-        cost_estimate=pl.CostEstimate(
-            flops=2 * len(lefts) * rows * hidden * right.shape[1],
-            bytes_accessed=2 * rows * right.shape[1], transcendentals=0,
-        ),
+        cost_estimate=taking(9 * len(lefts)),
         name=name,
     )(*lefts, right)
 
@@ -817,12 +1252,346 @@
         out_specs=tiled(depth),
         out_shape=jax.ShapeDtypeStruct((rows, depth), BF16),
         compiler_params=pltpu.CompilerParams(vmem_limit_bytes=48 << 20),
-        cost_estimate=pl.CostEstimate(
-            flops=2 * len(lefts) * rows * hidden * depth,
-            bytes_accessed=2 * rows * depth, transcendentals=0,
-        ),
+        cost_estimate=taking(10 * len(lefts)),
         name=name,
     )(*lefts, weight)
+
+
+class PlaneScatter:
+    SEMS = 14
+
+    def __init__(self, copies, base, fill, sent_ref, own_ref, core_ref, x_ref, y_ref, last_ref):
+        self.copies, self.base, self.fill = copies, base, fill
+        self.sent, self.own, self.core_part = sent_ref, own_ref, core_ref
+        self.x_ref, self.y_ref, self.last = x_ref, y_ref, last_ref
+        self.x, self.y, self.core, row, col = places()
+        self.over_x, self.over_y, self.over_core = peers(row, col)
+        x, y = self.x, self.y
+        self.order = ((1 - x, 1 - y), (1 - x, y), (x, 1 - y), (x, y))
+        self.half = sent_ref.shape[1] // 2
+        self.rows = (pl.ds(0, self.half), pl.ds(self.half, self.half))
+
+    def send(self, index, source, place, device):
+        self.copies.send(self.base + index, source, place, device)
+
+    def wait(self, index, place):
+        self.copies.wait(self.base + index, place)
+
+    def give(self, i, h):
+        a, b = self.order[i]
+        self.fill(self.sent.at[i], a, 2 * b + 1 - self.core, h, None)
+        at = self.rows[h]
+        self.send(2 * i + h, self.sent.at[i, at, :], self.core_part.at[i, at, :], self.over_core)
+
+    def keep(self, i, h):
+        a, b = self.order[i]
+        at = self.rows[h]
+        self.wait(2 * i + h, self.core_part.at[i, at, :])
+        self.fill(self.own.at[i], a, 2 * b + self.core, h, self.core_part.at[i])
+        if h == 0 and i in (0, 1):
+            self.send(8 + i, self.own.at[i, at, :], self.x_ref.at[i], self.over_x)
+        if h == 1 and i in (0, 2):
+            self.send(10 + i // 2, self.own.at[i, at, :], self.y_ref.at[i // 2], self.over_y)
+
+    def first(self):
+        self.give(0, 0)
+        self.give(0, 1)
+        self.keep(0, 0)
+        self.keep(0, 1)
+        for h in range(2):
+            self.give(1, h)
+            self.give(2, h)
+        self.keep(1, 0)
+        self.keep(2, 1)
+        self.keep(2, 0)
+        self.keep(1, 1)
+        for h in range(2):
+            self.give(3, h)
+        for h in range(2):
+            self.keep(3, h)
+
+    def add(self, i, h, ref):
+        at = self.own.at[i, self.rows[h], :]
+        add_rows(at, at, ref, self.half)
+
+    def second(self):
+        self.wait(8, self.x_ref.at[0])
+        self.add(2, 0, self.x_ref.at[0])
+        self.send(12, self.own.at[2, self.rows[0], :], self.last.at[0], self.over_y)
+        self.wait(10, self.y_ref.at[0])
+        self.add(1, 1, self.y_ref.at[0])
+        self.send(13, self.own.at[1, self.rows[1], :], self.last.at[1], self.over_x)
+        self.wait(9, self.x_ref.at[1])
+        self.add(3, 0, self.x_ref.at[1])
+        self.wait(11, self.y_ref.at[1])
+        self.add(3, 1, self.y_ref.at[1])
+
+    def third(self):
+        self.wait(12, self.last.at[0])
+        self.wait(13, self.last.at[1])
+
+    def result(self, start, count):
+        h, other = divmod(start, self.half)
+        return self.own[3, pl.ds(start, count), :].astype(F32) + self.last[
+            h, pl.ds(other, count), :
+        ].astype(F32)
+
+
+STEP = 128
+
+
+class NormBack:
+    def __init__(
+        self, copies, base, values_ref, stats_ref, gain_ref, base_ref, out_ref, low_ref, dgain_ref,
+        sums_ref,
+    ):
+        self.copies, self.base = copies, base
+        self.values, self.stats, self.gain, self.more = values_ref, stats_ref, gain_ref, base_ref
+        self.out, self.low, self.dgain, self.sums = out_ref, low_ref, dgain_ref, sums_ref
+
+    def unit_of(self, at):
+        stats = self.stats[at, :]
+        return (self.values[at, :].astype(F32) - stats[:, 0:1]) * stats[:, 1:2]
+
+    def start(self, result, devices):
+        lane = lax.broadcasted_iota(jnp.int32, (1, 128), 1)
+        self.dgain[...] = jnp.zeros_like(self.dgain)
+        for start in range(0, self.out.shape[0], STEP):
+            at = pl.ds(start, STEP)
+            grad = result(start, STEP)
+            self.out[at, :] = grad
+            unit = self.unit_of(at)
+            self.dgain[...] += jnp.sum(grad * unit, axis=0, keepdims=True)
+            grad = grad * self.gain[...]
+            first = jnp.sum(grad, axis=1, keepdims=True)
+            second = jnp.sum(grad * unit, axis=1, keepdims=True)
+            both = jnp.where(lane == 0, first, jnp.where(lane == 1, second, 0.0))
+            self.sums[0, :, start : start + STEP] = both.T[:8]
+        for i, device in enumerate(devices):
+            self.copies.send(self.base + i, self.sums.at[0], self.sums.at[1 + i], device)
+
+    def finish(self):
+        rows, width = self.out.shape
+        for i in range(3):
+            self.copies.wait(self.base + i, self.sums.at[1 + i])
+        for start in range(0, rows, STEP):
+            at = pl.ds(start, STEP)
+            columns = slice(start, start + STEP)
+            total = (self.sums[0, :, columns] + self.sums[1, :, columns]) + (
+                self.sums[2, :, columns] + self.sums[3, :, columns]
+            )
+            total = jnp.concatenate([total, jnp.zeros((STEP - 8, STEP), F32)], axis=0).T
+            total = total * (1.0 / (4 * width))
+            unit = self.unit_of(at)
+            grad = self.out[at, :] * self.gain[...]
+            grad = self.stats[at, 1:2] * (grad - total[:, 0:1] - unit * total[:, 1:2])
+            grad = grad + self.more[at, :].astype(F32)
+            self.out[at, :] = grad
+            if self.low is not None:
+                self.low[at, :] = grad.astype(BF16)
+
+
+def scatter_scratch(rows, width):
+    block = lambda n, r: pltpu.VMEM((n, r, width), BF16)
+    return [
+        block(4, rows), block(4, rows), block(4, rows),
+        block(2, rows // 2), block(2, rows // 2), block(2, rows // 2),
+    ]
+
+
+def around():
+    _, _, _, row, col = places()
+    over_x, over_y, over_core = peers(row, col)
+    return over_x, over_y, over_core, (row, 3 - col)
+
+
+def filling(rows, product):
+    half = rows // 2
+
+    def fill(ref, a, c, h, more):
+        @pl.loop(0, half // TILE)
+        def _(i):
+            start = h * half + i * TILE
+            total = product(pl.ds(pl.multiple_of(a * rows + start, TILE), TILE), c)
+            at = pl.ds(pl.multiple_of(start, TILE), TILE)
+            if more is not None:
+                total = total + more[at, :].astype(F32)
+            ref[at, :] = total.astype(BF16)
+
+    return fill
+
+
+def turn_rows(left_ref, source_ref, a, rows):
+    @pl.loop(0, rows // TILE)
+    def _(i):
+        at = pl.ds(pl.multiple_of(a * rows + i * TILE, TILE), TILE)
+        left_ref[at, :] = source_ref[:, at].T
+
+
+def back_second_kernel(
+    gate_ref, up_ref, weight_ref, values_ref, stats_ref, gain_ref, base_ref,
+    out_ref, low_ref, dgain_ref,
+    gate_vmem, up_vmem, weight_vmem, left_ref, sums_ref, load_sem, send_sem, recv_sem, *scratch,
+):
+    rows, width = out_ref.shape
+    x, y, core, _, _ = places()
+    devices = around()
+
+    def load_left(i, a):
+        at = pl.ds(pl.multiple_of(a * rows, TILE), rows)
+        return [
+            pltpu.make_async_copy(ref.at[:, at], vmem.at[:, at], load_sem.at[2 * i + j])
+            for j, (ref, vmem) in enumerate(((gate_ref, gate_vmem), (up_ref, up_vmem)))
+        ]
+
+    def load_weight(i, c):
+        return pltpu.make_async_copy(weight_ref.at[c], weight_vmem.at[c], load_sem.at[4 + i])
+
+    lefts = [load_left(0, 1 - x), load_left(1, x)]
+    columns = (2 * (1 - y) + 1 - core, 2 * (1 - y) + core, 2 * y + 1 - core, 2 * y + core)
+    weights = [load_weight(i, c) for i, c in enumerate(columns)]
+    for task in (*lefts[0], *weights, *lefts[1]):
+        task.start()
+    meet(devices)
+    copies = Copies(send_sem, recv_sem, devices[2])
+
+    def turn(i, a):
+        for j, (task, vmem) in enumerate(zip(lefts[i], (gate_vmem, up_vmem))):
+            task.wait()
+            turn_rows(left_ref.at[j], vmem, a, rows)
+
+    def product(at, c):
+        return dot(left_ref[0, at, :], weight_vmem[c, 0]) + dot(
+            left_ref[1, at, :], weight_vmem[c, 1]
+        )
+
+    scatter = PlaneScatter(copies, 0, filling(rows, product), *scratch)
+    turn(0, 1 - x)
+    weights[0].wait()
+    scatter.give(0, 0)
+    scatter.give(0, 1)
+    weights[1].wait()
+    scatter.keep(0, 0)
+    scatter.keep(0, 1)
+    weights[2].wait()
+    scatter.give(1, 0)
+    scatter.give(1, 1)
+    weights[3].wait()
+    scatter.keep(1, 0)
+    turn(1, x)
+    scatter.give(2, 1)
+    scatter.give(2, 0)
+    scatter.keep(2, 1)
+    scatter.keep(2, 0)
+    scatter.keep(1, 1)
+    scatter.give(3, 0)
+    scatter.give(3, 1)
+    scatter.keep(3, 0)
+    scatter.keep(3, 1)
+    scatter.second()
+    scatter.third()
+    norm = NormBack(
+        copies, PlaneScatter.SEMS, values_ref, stats_ref, gain_ref, base_ref, out_ref, low_ref,
+        dgain_ref, sums_ref,
+    )
+    norm.start(scatter.result, devices[1:])
+    norm.finish()
+    copies.finish()
+
+
+def back_second(gate, up, weight, values, stats, gain, base, collective_id):
+    rows, width = values.shape
+    hidden, tokens = gate.shape
+    vmem, anywhere = pl.BlockSpec(memory_space=pltpu.VMEM), pl.BlockSpec(memory_space=pl.ANY)
+    sems = lambda n: pltpu.SemaphoreType.DMA((n,))
+    return pl.pallas_call(
+        back_second_kernel,
+        in_specs=[anywhere] * 3 + [vmem] * 4,
+        out_specs=[vmem] * 3,
+        out_shape=[
+            jax.ShapeDtypeStruct((rows, width), F32),
+            jax.ShapeDtypeStruct((rows, width), BF16),
+            jax.ShapeDtypeStruct((1, width), F32),
+        ],
+        scratch_shapes=[
+            pltpu.VMEM(gate.shape, BF16), pltpu.VMEM(up.shape, BF16),
+            pltpu.VMEM(weight.shape, BF16), pltpu.VMEM((2, tokens, hidden), BF16),
+            pltpu.VMEM((4, 8, rows), F32),
+            sems(8), sems(PlaneScatter.SEMS + 3), sems(PlaneScatter.SEMS + 3),
+            *scatter_scratch(rows, width),
+        ],
+        compiler_params=pltpu.CompilerParams(
+            collective_id=collective_id, has_side_effects=True, vmem_limit_bytes=60 << 20
+        ),
+        cost_estimate=taking(50),
+        name="back_second",
+    )(gate, up, weight, values, stats, gain.reshape(1, width), base)
+
+
+def back_first_kernel(
+    grad_ref, weight_ref, hidden_ref, down_ref, values_ref, stats_ref, gain_ref, base_ref, resid_ref,
+    out_ref, dgain_ref, mixed_ref,
+    left_ref, sums_ref, send_sem, recv_sem, *scratch,
+):
+    rows, width = out_ref.shape
+    x, _, _, _, _ = places()
+    devices = around()
+    meet(devices)
+    copies = Copies(send_sem, recv_sem, devices[2])
+
+    def product(at, c):
+        weight = weight_ref[pl.ds(pl.multiple_of(c * width, 128), width), :]
+        return dot(grad_ref[at, :], weight, (1,), (1,))
+
+    def mix(at, c):
+        return dot(left_ref[at, :], down_ref[c])
+
+    scatter = PlaneScatter(copies, 0, filling(rows, product), *scratch[:6])
+    mixing = PlaneScatter(copies, PlaneScatter.SEMS + 3, filling(rows, mix), *scratch[6:])
+    norm = NormBack(
+        copies, PlaneScatter.SEMS, values_ref, stats_ref, gain_ref, base_ref, out_ref, None,
+        dgain_ref, sums_ref,
+    )
+    scatter.first()
+    for a in range(PAIR):
+        turn_rows(left_ref, hidden_ref, a, rows)
+    mixing.first()
+    scatter.second()
+    scatter.third()
+    norm.start(scatter.result, devices[1:])
+    mixing.second()
+    norm.finish()
+    mixing.third()
+    for start in range(0, rows, STEP):
+        at = pl.ds(start, STEP)
+        mixed_ref[at, :] = (resid_ref[at, :] + mixing.result(start, STEP)).astype(BF16)
+    copies.finish()
+
+
+def back_first(grad, weight, hidden, down, values, stats, gain, base, resid, collective_id):
+    rows, width = values.shape
+    vmem = pl.BlockSpec(memory_space=pltpu.VMEM)
+    sems = lambda n: pltpu.SemaphoreType.DMA((n,))
+    return pl.pallas_call(
+        back_first_kernel,
+        in_specs=[vmem] * 9,
+        out_specs=[vmem] * 3,
+        out_shape=[
+            jax.ShapeDtypeStruct((rows, width), F32),
+            jax.ShapeDtypeStruct((1, width), F32),
+            jax.ShapeDtypeStruct((rows, width), BF16),
+        ],
+        scratch_shapes=[
+            pltpu.VMEM(hidden.shape[::-1], BF16), pltpu.VMEM((4, 8, rows), F32),
+            sems(2 * PlaneScatter.SEMS + 3), sems(2 * PlaneScatter.SEMS + 3),
+            *scatter_scratch(rows, width), *scatter_scratch(rows, width),
+        ],
+        compiler_params=pltpu.CompilerParams(
+            collective_id=collective_id, has_side_effects=True, vmem_limit_bytes=62 << 20
+        ),
+        cost_estimate=taking(80),
+        name="back_first",
+    )(grad, weight, hidden, down, values, stats, gain.reshape(1, width), base, resid)
 
 
 def per_device(
@@ -837,40 +1606,54 @@
     x = row % PAIR
     half = width // PAIR
 
-    qkv_weight = gather_line(
-        jnp.concatenate(
-            [own_columns(w, x) for w in (query_weight, key_weight, value_weight)], axis=1
-        )
-    )
-    out_line = gather_line(out_weight)
-    down_line = gather_line(down_weight)
-    ffn_weight = gather_line(
-        jnp.stack([own_units(w, x) for w in (gate_weight, up_weight)])[None]
-    )
-    out_other = swap_rows(out_line)
-    depth = out_weight.shape[0]
-    full = (lines, 1, depth, width)
-    out_all = in_order(x, out_line.reshape(full), out_other.reshape(full), 1).reshape(-1, width)
-    hidden = ffn_weight.shape[2]
-    down_all = lax.all_to_all(
-        down_line.reshape(lines, hidden, width), "col", split_axis=0, concat_axis=0, tiled=True
-    )
-
+    fast = cols == 4 and lines == LINES
     bias = jnp.concatenate(
         [pick(b, x, 0) for b in (query_bias, key_bias, value_bias)], axis=0
     )
-    gains = lax.all_gather(jnp.stack([attn_gain, mlp_gain]), "col", axis=1, tiled=True)
-    own_place = jnp.stack([positions, segment_ids])
-    place = in_order(x, own_place, swap_rows(own_place), 1)
-    cosine, sine = rotation_tables(place[0])
-    plane_segments = place[1]
-
-    tokens_all = gather_plane(tokens, "gather_tokens", 0)
-    grad_all = gather_plane(out_grad, "gather_cotangent", 1)
-    normed_first, queries, keys, values, stats_first = project_heads(
-        tokens_all, gains[0], qkv_weight, bias, cosine, sine
-    )
-    attended, lse = attention_forward(queries, keys, values, plane_segments)
+    depth = out_weight.shape[0]
+    hidden = down_weight.shape[0]
+    down_line = gather_line(down_weight)
+    if fast:
+        tokens_all, grad_all, qkv_weight, out_all, ffn_part, gains, places_all = gather_first(
+            tokens, out_grad, query_weight, key_weight, value_weight, out_weight,
+            gate_weight, up_weight,
+            jnp.pad(jnp.stack([attn_gain, mlp_gain]), ((0, 6), (0, 0))),
+            jnp.pad(jnp.stack([positions, segment_ids]), ((0, 6), (0, 0))), 0,
+        )
+    else:
+        qkv_weight = gather_line(
+            jnp.concatenate(
+                [own_columns(w, x) for w in (query_weight, key_weight, value_weight)], axis=1
+            )
+        )
+        tokens_all = gather_plane(tokens, "gather_tokens", 0)
+        grad_all = gather_plane(out_grad, "gather_cotangent", 1)
+        out_line = gather_line(out_weight)
+        full = (lines, 1, depth, width)
+        out_all = in_order(
+            x, out_line.reshape(full), swap_rows(out_line).reshape(full), 1
+        ).reshape(-1, width)
+        ffn_part = jnp.stack([own_units(w, x) for w in (gate_weight, up_weight)])[None]
+        gains = lax.all_gather(jnp.stack([attn_gain, mlp_gain]), "col", axis=1, tiled=True)
+        own_place = jnp.stack([positions, segment_ids])
+        places_all = in_order(x, own_place, swap_rows(own_place), 1)
+    cosine, sine = rotation_tables(places_all[0])
+    plane_segments = places_all[1]
+    down_blocks = after(down_line, tokens_all).reshape(lines, hidden, width)
+    ffn_weight = gather_line(after(ffn_part, down_blocks))
+
+    projections = (tokens_all, gains[0], qkv_weight, bias, cosine, sine)
+    if fast:
+        normed_first, queries, keys, values, stats_first, down_partly = project_heads(
+            *projections, down_blocks, 1
+        )
+        attended, lse, down_all = attention_forward(
+            queries, keys, values, plane_segments, down_blocks, down_partly, 8
+        )
+    else:
+        normed_first, queries, keys, values, stats_first = project_heads(*projections)
+        attended, lse = attention_forward(queries, keys, values, plane_segments)
+        down_all = lax.all_to_all(down_blocks, "col", split_axis=0, concat_axis=0, tiled=True)
     attn_all = gather_heads(attended, x, 2)
     inputs = tokens.astype(F32)
     resid = inputs + dot(attn_all, out_all)
@@ -879,68 +1662,104 @@
     normed_second, hidden_low, grad_gate, grad_up, stats_second = feed_forward(
         resid_all, gains[1], ffn_weight, grad_all, down_all
     )
-    grad_ffn = scatter_line(weight_grads((grad_gate, grad_up), normed_second, width, "ffn_grads"))
-    grad_second = scatter_plane(
-        back_project((grad_gate, grad_up), ffn_weight, "back_ffn"), "scatter_second", 4
-    )
-    grad_down = weight_grads((hidden_low,), grad_all, width, "down_grads")
-    grad_down = lax.all_to_all(
-        grad_down.reshape(cols, hidden, width), "col", split_axis=0, concat_axis=0, tiled=True
-    )
-    grad_down = scatter_line(grad_down.reshape(lines * hidden, width))
+    grad_ffn = weight_grads((grad_gate, grad_up), normed_second, width, "ffn_grads")
     own_stats = pick(stats_second, x, 0)
-    mean_here, inv_here = own_stats[:, 0:1], own_stats[:, 1:2]
-    grad_resid, mlp_gain_part = norm_backward(
-        grad_second, (resid - mean_here) * inv_here, inv_here, mlp_gain
-    )
-    grad_resid = grad_resid + out_grad.astype(F32)
-    grad_resid_low = grad_resid.astype(BF16)
-
-    grad_attn = scatter_heads(dot(grad_resid_low, out_all, (1,), (1,)).astype(BF16), x, 5)
-    grad_qkv, bias_sums = attention_backward(
-        queries, keys, values, grad_attn, lse, cosine, sine, plane_segments
-    )
+    if fast:
+        grad_resid, grad_resid_low, mlp_gain_part = back_second(
+            after(grad_gate, grad_ffn), grad_up, ffn_weight,
+            resid, own_stats, mlp_gain, out_grad, 4,
+        )
+        mlp_gain_part = mlp_gain_part[0]
+    else:
+        grad_second = scatter_plane(
+            back_project((grad_gate, grad_up), ffn_weight, "back_ffn"), "scatter_second", 4
+        )
+        mean_here, inv_here = own_stats[:, 0:1], own_stats[:, 1:2]
+        grad_resid, mlp_gain_part = norm_backward(
+            grad_second, (resid - mean_here) * inv_here, inv_here, mlp_gain
+        )
+        grad_resid = grad_resid + out_grad.astype(F32)
+        grad_resid_low = grad_resid.astype(BF16)
+    grad_ffn = scatter_line(grad_ffn)
+
     grad_out_weight = dot(attn_all, grad_resid_low, (0,), (0,)).astype(BF16)
     grad_out_weight = grad_out_weight.reshape(lines, PAIR, depth, width)
-    grad_out_weight = pick(grad_out_weight, x, 1) + swap_rows(pick(grad_out_weight, 1 - x, 1))
-    grad_out_weight = scatter_line(grad_out_weight.reshape(lines * depth, width))
-    grad_qkv_weight = scatter_line(dot(normed_first, grad_qkv, (0,), (0,)).astype(BF16))
-    grad_first = scatter_plane(
-        dot(grad_qkv, qkv_weight, (1,), (1,)).astype(BF16), "scatter_first", 6
-    )
+    grad_out_other = swap_rows(pick(grad_out_weight, 1 - x, 1))
+    grad_attn = scatter_heads(dot(grad_resid_low, out_all, (1,), (1,)).astype(BF16), x, 5)
+    grad_out_weight = pick(grad_out_weight, x, 1) + grad_out_other
+    grad_attn = after(grad_attn, grad_out_weight)
+    grad_down = weight_grads((after(hidden_low, grad_attn),), grad_all, width, "down_grads")
+    grad_down = grad_down.reshape(cols, hidden, width)
+    backward = (queries, keys, values, grad_attn, lse, cosine, sine, plane_segments)
+    if fast:
+        grad_qkv, bias_sums, grad_down = attention_backward(*backward, grad_down, 9)
+    else:
+        grad_qkv, bias_sums = attention_backward(*backward)
+        grad_down = lax.all_to_all(grad_down, "col", split_axis=0, concat_axis=0, tiled=True)
+    grad_qkv_weight = dot(normed_first, grad_qkv, (0,), (0,)).astype(BF16)
+    grad_out_weight = scatter_line(
+        after(grad_out_weight, grad_ffn).reshape(lines * depth, width)
+    )
+    grad_down = scatter_line(
+        after(grad_down, grad_out_weight).reshape(lines * hidden, width)
+    )
+    grad_qkv_later = after(grad_qkv, grad_qkv_weight)
+    grad_qkv_weight = scatter_line(grad_qkv_weight)
     own_stats = pick(stats_first, x, 0)
-    mean_here, inv_here = own_stats[:, 0:1], own_stats[:, 1:2]
-    grad_input, attn_gain_part = norm_backward(
-        grad_first, (inputs - mean_here) * inv_here, inv_here, attn_gain
-    )
-    tokens_grad = grad_input + grad_resid
-    mixed = resid + scatter_plane(
-        back_project((hidden_low,), down_all[:, None], "mix"), "scatter_mixed", 7
-    )
-    mixed = mixed.astype(BF16)
+    if fast:
+        tokens_grad, attn_gain_part, mixed = back_first(
+            grad_qkv_later, qkv_weight, hidden_low, down_all,
+            tokens, own_stats, attn_gain, grad_resid, resid, 6,
+        )
+        attn_gain_part = attn_gain_part[0]
+    else:
+        grad_first = scatter_plane(
+            dot(grad_qkv_later, qkv_weight, (1,), (1,)).astype(BF16), "scatter_first", 6
+        )
+        mean_here, inv_here = own_stats[:, 0:1], own_stats[:, 1:2]
+        grad_input, attn_gain_part = norm_backward(
+            grad_first, (inputs - mean_here) * inv_here, inv_here, attn_gain
+        )
+        tokens_grad = grad_input + grad_resid
+        mixed = resid + scatter_plane(
+            back_project((hidden_low,), down_all[:, None], "mix"), "scatter_mixed", 10
+        )
+        mixed = mixed.astype(BF16)
+    kept, other = pick(grad_ffn[0], x, 2), swap_rows(pick(grad_ffn[0], 1 - x, 2))
+    gate_grad, up_grad = (
+        in_order(x, kept[i], other[i], 0).T.astype(F32) for i in range(2)
+    )
 
     bias_part = jnp.sum(bias_sums, axis=(0, 1)).reshape(3, half)
     bias_part = jnp.where(
         (jnp.arange(PAIR) == x)[None, :, None], bias_part[:, None, :], 0.0
     ).reshape(3, width)
-    vectors = lax.psum(
-        jnp.concatenate([bias_part, attn_gain_part[None], mlp_gain_part[None]], axis=0), "row"
-    )
-    wide = lambda grad: own_rows(grad, x).astype(F32)
+    vectors = sum_rows(
+        jnp.concatenate(
+            [bias_part, attn_gain_part[None], mlp_gain_part[None], jnp.zeros((3, width), F32)]
+        ),
+        7,
+    )
+    grad_qkv_weight = own_rows(grad_qkv_weight, x)
+    wide = lambda w: jnp.where(
+        x == 0,
+        jnp.concatenate([grad_qkv_weight[0][:, w], grad_qkv_weight[1][:, w]], axis=1),
+        jnp.concatenate([grad_qkv_weight[1][:, w], grad_qkv_weight[0][:, w]], axis=1),
+    ).astype(F32)
     return (
         mixed,
         tokens_grad,
         vectors[3],
-        wide(grad_qkv_weight[:, :half]),
+        wide(slice(0, half)),
         vectors[0],
-        wide(grad_qkv_weight[:, half : 2 * half]),
+        wide(slice(half, 2 * half)),
         vectors[1],
-        wide(grad_qkv_weight[:, 2 * half :]),
+        wide(slice(2 * half, 3 * half)),
         vectors[2],
         grad_out_weight.astype(F32),
         vectors[4],
-        own_inputs(grad_ffn[0, 0], x).T.astype(F32),
-        own_inputs(grad_ffn[0, 1], x).T.astype(F32),
+        gate_grad,
+        up_grad,
         grad_down.astype(F32),
     )
 

time: 774 us -> 631 us (0.82)
  blocking collectives: 95.3 us -> 0 us
  Pallas kernels: 451 us -> 530 us
  waiting for transfers between devices: 80.9 us -> 15.9 us
  local copies, waits for them, and re-layouts: 47.2 us -> 21.8 us
  starting transfers between devices: 17.9 us -> 4.08 us
  other arithmetic: 25.8 us -> 12.9 us
  matrix products: 34.3 us -> 25.6 us
    pallas_call x8 -> x7, Pallas kernels: 217 us -> 371 us  [the longest x1 139 us: gather_first(): pl.pallas_call(gather_first_kernel, in_specs=[pl.BlockSpec(memory_space=p...]
    pallas_call x3 -> x1, Pallas kernels: 119 us -> 40.7 us  [gather_plane(): pl.pallas_call(gather_plane_kernel, in_specs=[pl.BlockSpec(memory_space=p...]
    psum x3 -> x0, blocking collectives: 50.7 us -> none  [the longest x1 36.8 us: per_device(): lax.psum(jnp.concatenate([bias_part, attn_gain_part[None], mlp_gain_part[...]
    all_to_all x1 -> x0, blocking collectives: 39.4 us -> none  [per_device(): lax.all_to_all(grad_down.reshape(cols, hidden, width), 'col', split_axis=...]
    reduce_scatter x4, waiting for transfers between devices: 38.8 us -> 0.03 us  [scatter_line(): lax.psum_scatter(values, 'row', scatter_dimension=axis, tiled=True, axis_...]
    ppermute x13 -> x3, waiting for transfers between devices: 36.9 us -> 15.1 us  [swap_rows(): return lax.ppermute(values, 'row', row_pairs())]
    unnamed x82 -> x42, local copies, waits for them, and re-layouts: 29.4 us -> 10.5 us
    ppermute x13 -> x3, starting transfers between devices: 13.9 us -> 3.63 us  [swap_rows(): return lax.ppermute(values, 'row', row_pairs())]
  transfers between devices with their start and end apart: 22 -> 9, of which waited for: 10 -> 2; matrix products, arithmetic and copies ran while one was open for 9% -> 8% of each run, Pallas kernels for 41% -> 78%
where the time goes in v2:
time: 631 us; the launch traced here: 625 us
  Pallas kernels  530 us (84%)
  matrix products  25.6 us (4%)
  local copies, waits for them, and re-layouts  21.8 us (3%)
  waiting for transfers between devices  15.9 us (3%)
  between operations  14.8 us (2%)
  other arithmetic  12.9 us (2%)
    pallas_call x1, Pallas kernels, gather_first(): pl.pallas_call(gather_first_kernel, in_specs=[pl.BlockSpec(memory_space=p...  139 us
    pallas_call x1, Pallas kernels, back_first(): pl.pallas_call(back_first_kernel, in_specs=[vmem] * 9, out_specs=[vmem] *...  89.6 us
    pallas_call x1, Pallas kernels, back_second(): pl.pallas_call(back_second_kernel, in_specs=[anywhere] * 3 + [vmem] * 4,...  54.4 us
    pallas_call x1, Pallas kernels, gather_plane(): pl.pallas_call(gather_plane_kernel, in_specs=[pl.BlockSpec(memory_space=p...  40.7 us
    pallas_call x1, Pallas kernels, attention_backward(): pl.pallas_call(kernel, grid=(seqs,), in_specs=in_specs, out_specs=out_spe...  37 us
    pallas_call x1, Pallas kernels, scatter_heads(): pl.pallas_call(scatter_heads_kernel, in_specs=[pl.BlockSpec(memory_space=...  33.5 us
    pallas_call x1, Pallas kernels, gather_heads(): pl.pallas_call(gather_heads_kernel, in_specs=[pl.BlockSpec(memory_space=p...  29.5 us
    pallas_call x1, Pallas kernels, feed_forward(): pl.pallas_call(feed_forward_kernel, grid=(rows // TILE,), in_specs=[tiled...  28.1 us
  transfers between devices with their start and end apart: 9, of which 2 were waited for; matrix products, arithmetic and copies ran while one was open for 8% of the time, Pallas kernels for 78%

profile of v2, /device:TPU:0, one launch (start us, length us, event | category | flops | bytes accessed | tf_op | source)
XLA Modules:
  0.0 625.5 jit_solution(8015815168589664456)
XLA Ops:
  10.6 139.0 %gather_first.1 = (bf16[2048,2048]{1,0:T(8,128)(2,1)}, bf16[2048,2048]{1,0:T(8,128)(2,1)}, bf16[2048,768]{1,0:T(8,128)(2,1)}, bf16[2048,512]{1,0:T(8,128)(2,1)},...) custom-call(bf16[1024,512]{1,0:T(8,128)(2,1)} %values_ref.1, bf16[1024,512]{1,0:T(8,128)(2,1)} %base_ref.1, ...), custom_call_target="tpu_custom_call" | custom-call | flops 109999996928 | bytes 110000000 | tf_op jit(solution)/shard_map/gather_first/pallas_call | solution.py:625
  150.1 1.5 fusion.7
  157.1 19.3 %project_heads.1 = (bf16[2048,2048]{1,0:T(8,128)(2,1)}, bf16[2048,256]{1,0:T(8,128)(2,1)S(1)}, bf16[2048,256]{1,0:T(8,128)(2,1)S(1)}, bf16[2048,256]{1,0:T(8,128...) custom-call(bf16[2048,2048]{1,0:T(8,128)(2,1)} %get-tuple-element.52.refs_0_, ...), custom_call_target="tpu_custom_call" | custom-call | flops 16000000000 | bytes 16000000 | tf_op jit(solution)/shard_map/project_heads/pallas_call | solution.py:1157
  179.3 21.1 %attention_forward.1 = (bf16[2048,256]{1,0:T(8,128)(2,1)}, f32[2,8,1024]{2,1,0:T(8,128)}, bf16[4,704,512]{2,1,0:T(8,128)(2,1)}) custom-call(bf16[2048,256]{1,0:T(8,128)(2,1)} %copy-done.1, bf16[2048,256]{1,0:T(8,128)(2,1)} %copy-done.2, bf16[2048,256]{1,0:T(8,128)(2,1)} %copy-done.3, ...), custom_call_target="tpu_custom_call", output_to_operand_aliasing={{2}: (6, {})} | custom-call | flops 20999999488 | bytes 21000000 | tf_op jit(solution)/shard_map/attention_forward/pallas_call | solution.py:107
  200.4 29.5 %gather_heads.1 = bf16[1024,2048]{1,0:T(8,128)(2,1)} custom-call(bf16[2048,256]{1,0:T(8,128)(2,1)} %get-tuple-element.61.src_ref), custom_call_target="tpu_custom_call" | custom-call | flops 28000000000 | bytes 28000000 | tf_op jit(solution)/shard_map/gather_heads/pallas_call | solution.py:850
  230.0 6.9 %fusion.9 = (bf16[1024,512]{1,0:T(8,128)(2,1)}, f32[1024,512]{1,0:T(8,128)}) fusion(bf16[1024,2048]{1,0:T(8,128)(2,1)} %gather_heads.1, bf16[2048,512]{1,0:T(8,128)(2,1)} %get-tuple-element.62, bf16[1024,512]{1,0:T(8,128)(2,1)S(1)} %copy-done.15), kind=kOutput, calls=%fused_computation.46 | convolution fusion | flops 2149056512 | bytes 10485760 | tf_op jit(solution)/shard_map/dot_general | solution.py:24
  236.9 40.7 %gather_residual.1.resid_ref = bf16[2048,2048]{1,0:T(8,128)(2,1)} custom-call(bf16[1024,512]{1,0:T(8,128)(2,1)} %get-tuple-element.155.src_ref), custom_call_target="tpu_custom_call" | custom-call | flops 40000000000 | bytes 40000000 | tf_op jit(solution)/shard_map/gather_residual/pallas_call | solution.py:655
  277.6 28.1 %feed_forward.1 = (bf16[2048,2048]{1,0:T(8,128)(2,1)}, bf16[704,2048]{1,0:T(8,128)(2,1)}, bf16[704,2048]{1,0:T(8,128)(2,1)}, bf16[704,2048]{1,0:T(8,128)(2,1)}, f32[2048,8]{1,0:T(8,128)}) custom-call(bf16[2048,2048]{1,0:T(8,128)(2,1)} %gather_residual.1.resid_ref, f32[1,2048]{1,0:T(1,128)} %get-tuple-element.142.gain_ref, ...), custom_call_target="tpu_custom_call" | custom-call | flops 28000000000 | bytes 28000000 | tf_op jit(solution)/shard_map/feed_forward/pallas_call | solution.py:1197
  305.7 17.1 %ffn_grads.1 = bf16[4,2,704,512]{3,2,1,0:T(8,128)(2,1)} custom-call(bf16[704,2048]{1,0:T(8,128)(2,1)} %get-tuple-element.70.refs_0_.gate_ref, bf16[704,2048]{1,0:T(8,128)(2,1)} %get-tuple-element.68.refs_1_.up_ref, bf16[2048,2048]{1,0:T(8,128)(2,1)} %get-tuple-element.69.refs_2_), custom_call_target="tpu_custom_call" | custom-call | flops 17999998976 | bytes 18000000 | tf_op jit(solution)/shard_map/ffn_grads/pallas_call | solution.py:1222
  324.8 54.4 %back_second.1 = (f32[1024,512]{1,0:T(8,128)}, bf16[1024,512]{1,0:T(8,128)(2,1)}, f32[1,512]{1,0:T(1,128)}) custom-call(bf16[704,2048]{1,0:T(8,128)(2,1)} %get-tuple-element.70.refs_0_.gate_ref, bf16[704,2048]{1,0:T(8,128)(2,1)} %get-tuple-element.68.refs_1_.up_ref, bf16[4,2,704,512]{3,2,1,0:T(8,128)(2,1)} %all-gather.5.cloned.1.call-done.weight_ref, ...), custom_call_target="tpu_custom_call" | custom-call | flops 49999998976 | bytes 50000000 | tf_op jit(solution)/shard_map/back_second/pallas_call | solution.py:1507
  379.3 5.0 convolution_convert_fusion.2
  385.9 2.4 convolution_convert_fusion.part_ref
  388.2 33.5 %scatter_heads.1.refs_3_ = bf16[2048,256]{1,0:T(8,128)(2,1)S(1)} custom-call(bf16[1024,2048]{1,0:T(8,128)(2,1)S(1)} %convolution_convert_fusion.part_ref), custom_call_target="tpu_custom_call" | custom-call | flops 32000000000 | bytes 32000000 | tf_op jit(solution)/shard_map/scatter_heads/pallas_call | solution.py:947
  423.9 10.3 %down_grads.1 = bf16[4,1,704,512]{3,2,1,0:T(8,128)(2,1)} custom-call(bf16[704,2048]{1,0:T(8,128)(2,1)} %get-tuple-element.76.refs_0_.hidden_ref, bf16[2048,2048]{1,0:T(8,128)(2,1)} %get-tuple-element.65.grad_ref.refs_1_), custom_call_target="tpu_custom_call" | custom-call | flops 8999999488 | bytes 9000000 | tf_op jit(solution)/shard_map/down_grads/pallas_call | solution.py:1222
  434.2 37.0 %attention_backward.1 = (bf16[2048,768]{1,0:T(8,128)(2,1)}, f32[2,1,768]{2,1,0:T(1,128)}, bf16[4,704,512]{2,1,0:T(8,128)(2,1)}) custom-call(bf16[2048,256]{1,0:T(8,128)(2,1)} %copy-done.1, bf16[2048,256]{1,0:T(8,128)(2,1)} %copy-done.2, bf16[2048,256]{1,0:T(8,128)(2,1)} %copy-done.3, bf16[2048,256]{1,0:T(8,128)(2,1)} %copy-done.4, ...), custom_call_target="tpu_custom_call" | custom-call | flops 32999999488 | bytes 33000000 | tf_op jit(solution)/shard_map/attention_backward/pallas_call | solution.py:211
  471.2 11.4 %convolution_convert_fusion.1 = bf16[2048,768]{1,0:T(8,128)(2,1)} fusion(bf16[2048,2048]{1,0:T(8,128)(2,1)} %get-tuple-element.78, bf16[2048,768]{1,0:T(8,128)(2,1)} %get-tuple-element.79.grad_ref), kind=kOutput, calls=%fused_computation.1 | convolution fusion | flops 6444023808 | bytes 14680064 | tf_op jit(solution)/shard_map/dot_general | solution.py:24
  483.7 89.6 %back_first.1 = (f32[1024,512]{1,0:T(8,128)}, f32[1,512]{1,0:T(1,128)}, bf16[1024,512]{1,0:T(8,128)(2,1)}) custom-call(bf16[2048,768]{1,0:T(8,128)(2,1)} %get-tuple-element.79.grad_ref, bf16[2048,768]{1,0:T(8,128)(2,1)} %get-tuple-element.54.refs_2_.weight_ref, bf16[704,2048]{1,0:T(8,128)(2,1)} %get-tuple-element.76.refs_0_.hidden_ref, ...), custom_call_target="tpu_custom_call" | custom-call | flops 80000000000 | bytes 80000000 | tf_op jit(solution)/shard_map/back_first/pallas_call | solution.py:1575
  574.7 10.7 %sum_rows.1 = f32[8,512]{1,0:T(8,128)} custom-call(f32[8,512]{1,0:T(8,128)} %pad_maximum_fusion.part_ref), custom_call_target="tpu_custom_call" | custom-call | flops 8000000000 | bytes 8000000 | tf_op jit(solution)/shard_map/sum_rows/pallas_call | solution.py:998
  586.5 1.7 collective-permute-start.1
  591.3 7.3 %collective-permute-done.1 = bf16[256,768]{1,0:T(8,128)(2,1)S(1)} collective-permute-done((bf16[256,768]{1,0:T(8,128)(2,1)S(1)}, bf16[256,768]{1,0:T(8,128)(2,1)S(1)}, u32[]{:S(2)}, u32[]{:S(2)}) %collective-permute-start.1) | collective-permute-done | bytes 393248 | tf_op jit(solution)/shard_map/ppermute | solution.py:238
  601.4 7.8 %collective-permute-done.2 = bf16[2,704,256]{2,1,0:T(8,128)(2,1)S(1)} collective-permute-done((bf16[2,704,256]{2,1,0:T(8,128)(2,1)S(1)}, bf16[2,704,256]{2,1,0:T(8,128)(2,1)S(1)}, u32[]{:S(2)}, u32[]{:S(2)}) %collective-permute-start.2) | collective-permute-done | bytes 720928 | tf_op jit(solution)/shard_map/ppermute | solution.py:238
  609.4 1.5 copy.48
  611.1 1.5 copy.47
  613.5 2.6 convert_element_type.69
  (107 shorter events, 30.7 us)
Async XLA Ops:
  7.2 149.6 %all-gather.3.cloned.1.call-start = ((), (), s32[]{:S(2)}) async-start(), calls=%async_computation.4 | async-start | bytes 3604480 | tf_op jit(solution)/shard_map/all_gather | solution.py:246
  7.9 269.7 %all-gather.5.cloned.1.call-start = ((), (), s32[]{:S(2)}) async-start(), calls=%async_computation.5 | async-start | bytes 7208960 | tf_op jit(solution)/shard_map/all_gather | solution.py:246
  10.6 139.2 %copy-start.12 = (f32[512]{0:T(512)S(1)}, f32[512]{0:T(512)}, u32[]{:S(2)}) copy-start(f32[512]{0:T(512)} %param.21) | copy-start | bytes 6148
  10.6 139.3 %copy-start.13 = (f32[512]{0:T(512)S(1)}, f32[512]{0:T(512)}, u32[]{:S(2)}) copy-start(f32[512]{0:T(512)} %param.23) | copy-start | bytes 6148
  10.6 139.4 %copy-start.14 = (f32[512]{0:T(512)S(1)}, f32[512]{0:T(512)}, u32[]{:S(2)}) copy-start(f32[512]{0:T(512)} %param.25) | copy-start | bytes 6148
  152.5 4.6 copy-start
  156.8 277.3 %reduce-scatter.7.cloned.1.call-start = ((), (), s32[]{:S(2)}) async-start(), calls=%async_computation.7 | async-start | bytes 7208960 | tf_op jit(solution)/shard_map/reduce_scatter | solution.py:250
  200.4 29.5 %copy-start.15 = (bf16[1024,512]{1,0:T(8,128)(2,1)S(1)}, bf16[1024,512]{1,0:T(8,128)(2,1)}, u32[]{:S(2)}) copy-start(bf16[1024,512]{1,0:T(8,128)(2,1)} %values_ref.1) | copy-start | bytes 3145732
  322.8 1.2 copy-start.9
  322.8 160.8 %reduce-scatter.9.cloned.1.call-start = ((), (), s32[]{:S(2)}) async-start(), calls=%async_computation.8 | async-start | bytes 1310720 | tf_op jit(solution)/shard_map/reduce_scatter | solution.py:250
  379.3 6.5 %copy-start.17 = (bf16[1024,512]{1,0:T(8,128)(2,1)S(1)}, bf16[1024,512]{1,0:T(8,128)(2,1)}, u32[]{:S(2)}) copy-start(bf16[1024,512]{1,0:T(8,128)(2,1)} %get-tuple-element.72) | copy-start | bytes 3145732
  384.3 1.6 copy-start.16
  384.4 38.4 %collective-permute-start = (bf16[4,1,256,512]{3,2,1,0:T(8,128)(2,1)S(1)}, bf16[4,1,256,512]{3,2,1,0:T(8,128)(2,1)S(1)}, u32[]{:S(2)}, u32[]{:S(2)}) collective-permute-start(bf16[4,1,256,512]{3,2,1,0:T(8,128)(2,1)S(1)} %constant_dynamic-slice_fusion.3), channel_id=1, source_target_pairs={{0,4},{4,0},{8,12},{12,8},{16,20},{20,16},{24,28},{28,24},{1,5},{5... | collective-permute-start | bytes 3145736 | tf_op jit(solution)/shard_map/ppermute | solution.py:238
  421.7 1.0 copy-start.4
  434.2 151.3 %reduce-scatter.5.cloned.1.call-start = ((), (), s32[]{:S(2)}) async-start(), calls=%async_computation.6 | async-start | bytes 3932160 | tf_op jit(solution)/shard_map/reduce_scatter | solution.py:250
  482.7 130.9 %reduce-scatter.11.cloned.1.call-start = ((), (), s32[]{:S(2)}) async-start(), calls=%async_computation.9 | async-start | bytes 3604480 | tf_op jit(solution)/shard_map/reduce_scatter | solution.py:250
  483.7 89.6 %copy-start.10 = (f32[2,1,768]{2,1,0:T(1,128)S(1)}, f32[2,1,768]{2,1,0:T(1,128)}, u32[]{:S(2)}) copy-start(f32[2,1,768]{2,1,0:T(1,128)} %get-tuple-element.84) | copy-start | bytes 18436
  483.7 89.7 %copy-start.11 = (f32[1,512]{1,0:T(1,128)S(1)}, f32[1,512]{1,0:T(1,128)}, u32[]{:S(2)}) copy-start(f32[1,512]{1,0:T(1,128)} %get-tuple-element.86) | copy-start | bytes 6148
  574.7 16.1 %copy-start.6 = (bf16[1,2,704,512]{3,2,1,0:T(8,128)(2,1)S(1)}, bf16[1,2,704,512]{3,2,1,0:T(8,128)(2,1)}, u32[]{:S(2)}) copy-start(bf16[1,2,704,512]{3,2,1,0:T(8,128)(2,1)} %reduce-scatter.7.cloned.1.call-done) | copy-start | bytes 4325380
  586.5 12.1 %collective-permute-start.1 = (bf16[256,768]{1,0:T(8,128)(2,1)S(1)}, bf16[256,768]{1,0:T(8,128)(2,1)S(1)}, u32[]{:S(2)}, u32[]{:S(2)}) collective-permute-start(bf16[256,768]{1,0:T(8,128)(2,1)S(1)} %constant_dynamic-slice_fusion.1), channel_id=1, source_target_pairs={{0,4},{4,0},{8,12},{12,8},{16,20},{20,16},{24,28},{28,24},{1,5},{5... | collective-permute-start | bytes 1179656 | tf_op jit(solution)/shard_map/ppermute | solution.py:238
  590.8 18.4 %collective-permute-start.2 = (bf16[2,704,256]{2,1,0:T(8,128)(2,1)S(1)}, bf16[2,704,256]{2,1,0:T(8,128)(2,1)S(1)}, u32[]{:S(2)}, u32[]{:S(2)}) collective-permute-start(bf16[2,704,256]{2,1,0:T(8,128)(2,1)S(1)} %dynamic-slice_bitcast_fusion), channel_id=1, source_target_pairs={{0,4},{4,0},{8,12},{12,8},{16,20},{20,16},{24,28},{28,24},{1,5},{5... | collective-permute-start | bytes 2162696 | tf_op jit(solution)/shard_map/ppermute | solution.py:238
  611.0 1.7 copy-start.8
  612.7 3.4 copy-start.7
  613.5 3.5 copy-start.5
  (3 other events, 2.9 us)
Sparse Core Ops, SparseCore 0:
  9.6 80.2 all-gather.2
  157.0 104.2 all-gather.4
  322.9 100.4 reduce-scatter.6
  434.3 24.8 reduce-scatter.8
  482.8 57.9 reduce-scatter.4
  543.1 58.2 reduce-scatter.10

commit v3 on v2

--- a/solution.py
+++ b/solution.py
@@ -120,7 +120,7 @@
 
 def attention_backward_kernel(
     q_ref, k_ref, v_ref, do_ref, lse_ref, cos_ref, sin_ref, seg_col_ref, seg_row_ref,
-    grad_ref, sums_ref, dq_ref, dk_ref, dv_ref,
+    grad_ref, sums_ref, dq_ref, dk_ref, dv_ref, halfway=None,
 ):
     width = q_ref.shape[1]
     heads = width // HEAD_DIM
@@ -129,12 +129,11 @@
     for ref in (dq_ref, dk_ref, dv_ref):
         ref[...] = jnp.zeros_like(ref)
 
-    @pl.loop(0, heads)
-    def _(head):
+    def one_head(head):
         mask = full_lane // HEAD_DIM == head
         nothing = jnp.zeros((), BF16)
-        for start in range(0, SEQ, QBLOCK):
-            keys = start + QBLOCK
+        for start in range(0, SEQ, 2 * QBLOCK):
+            keys = start + 2 * QBLOCK
             rows = slice(start, keys)
             queries = jnp.where(mask, q_ref[rows, :], nothing)
             grads = jnp.where(mask, do_ref[rows, :], nothing)
@@ -153,6 +152,11 @@
             masked_keys = jnp.where(mask, k_ref[:keys, :], nothing)
             dq_ref[rows, :] += dot(grad_scores, masked_keys, (0,), (0,))
 
+    pl.loop(0, heads // 2)(one_head)
+    if halfway is not None:
+        halfway()
+    pl.loop(heads // 2, heads)(one_head)
+
     cosine = jnp.tile(cos_ref[...], (1, width // cos_ref.shape[1]))
     sine = jnp.tile(sin_ref[...], (1, width // sin_ref.shape[1]))
     for part, (ref, scale) in enumerate(((dq_ref, SCALE), (dk_ref, 1.0), (dv_ref, None))):
@@ -166,17 +170,46 @@
         sums_ref[0, :, columns] = jnp.sum(low.astype(F32), axis=0, keepdims=True)
 
 
-def attention_backward_exchange_kernel(*refs):
-    ins, blocks_ref, outs, all_ref = refs[:9], refs[9], refs[10:12], refs[12]
-    scratch, (stage, local_sem, *sems) = refs[13:16], refs[16:]
-    exchange_beside(
-        lambda: attention_backward_kernel(*ins, *outs, *scratch),
-        blocks_ref, all_ref, (2, 3, 1), (stage, local_sem), *sems,
-    )
+def attention_backward_sums_kernel(*refs):
+    ins, parts_ref, resid_ref = refs[:9], refs[9], refs[10]
+    outs, mixed_ref, scratch = refs[11:13], refs[13], refs[14:17]
+    load_sem, send_sem, recv_sem, *blocks = refs[17:]
+    devices = peers(lax.axis_index("row"), lax.axis_index("col"))
+    copies = Copies(send_sem, recv_sem, devices[2])
+    mixing = PartsScatter(copies, 0, parts_ref, load_sem, *blocks)
+    step = pl.program_id(0)
+
+    @pl.when(step == 0)
+    def _():
+        meet(devices)
+        mixing.start()
+        mixing.keep(0, 0)
+        mixing.keep(0, 1)
+
+    def halfway():
+        @pl.when(step == 0)
+        def _():
+            for i, h in ((1, 0), (2, 0), (2, 1), (1, 1), (3, 0), (3, 1)):
+                mixing.keep(i, h)
+
+        @pl.when(step == 1)
+        def _():
+            mixing.second()
+
+    attention_backward_kernel(*ins, *outs, *scratch, halfway=halfway)
+
+    @pl.when(step == 1)
+    def _():
+        mixing.third()
+        for start in range(0, mixed_ref.shape[0], STEP):
+            at = pl.ds(start, STEP)
+            mixed_ref[at, :] = (resid_ref[at, :] + mixing.result(start, STEP)).astype(BF16)
+        mixing.drain()
 
 
 def attention_backward(
-    queries, keys, values, grad_out, lse, cosine, sine, segments, blocks=None, collective_id=None
+    queries, keys, values, grad_out, lse, cosine, sine, segments,
+    parts=None, resid=None, collective_id=None,
 ):
     rows, width = queries.shape
     seqs = rows // SEQ
@@ -199,15 +232,16 @@
     ]
     scratch = [pltpu.VMEM((SEQ, width), F32)] * 3
     params, kernel = {}, attention_backward_kernel
-    if blocks is not None:
-        anywhere = pl.BlockSpec(memory_space=pl.ANY)
-        in_specs, out_specs = in_specs + [anywhere], out_specs + [anywhere]
-        out_shape = out_shape + [jax.ShapeDtypeStruct(blocks.shape, BF16)]
-        operands = operands + [blocks]
-        scratch = scratch + [pltpu.VMEM(blocks.shape[1:], BF16), pltpu.SemaphoreType.DMA]
-        scratch = scratch + [pltpu.SemaphoreType.DMA((3,))] * 2
+    if parts is not None:
+        in_specs = in_specs + [pl.BlockSpec(memory_space=pl.ANY), whole(resid.shape)]
+        out_specs = out_specs + [whole(resid.shape)]
+        out_shape = out_shape + [jax.ShapeDtypeStruct(resid.shape, BF16)]
+        operands = operands + [parts, resid]
+        sems = lambda n: pltpu.SemaphoreType.DMA((n,))
+        scratch = scratch + [sems(4), sems(PlaneScatter.SEMS), sems(PlaneScatter.SEMS)]
+        scratch = scratch + scatter_scratch(*resid.shape)[1:]
         params = dict(collective_id=collective_id, has_side_effects=True)
-        kernel = attention_backward_exchange_kernel
+        kernel = attention_backward_sums_kernel
     return pl.pallas_call(
         kernel,
         grid=(seqs,),
@@ -215,8 +249,8 @@
         out_specs=out_specs,
         out_shape=out_shape,
         scratch_shapes=scratch,
-        compiler_params=pltpu.CompilerParams(vmem_limit_bytes=56 << 20, **params),
-        cost_estimate=taking(33),
+        compiler_params=pltpu.CompilerParams(vmem_limit_bytes=60 << 20, **params),
+        cost_estimate=taking(42),
         name="attention_backward",
     )(*operands)
 
@@ -863,107 +897,9 @@
     )(values)
 
 
-def scatter_heads_kernel(
-    part_ref, out_ref, own_ref, core_ref, y_ref, load_sem, out_sem, send_sem, recv_sem
-):
-    rows, width = own_ref.shape[1:]
-    half = width // PAIR
-    count = rows // CHUNKS
-    x, y, core, row, col = places()
-    over_x, over_y, over_core = peers(row, col)
-    meet((over_x, over_y, over_core))
-
-    def copy(index, source, place, device):
-        return pltpu.make_async_remote_copy(
-            source, place, send_sem.at[index], recv_sem.at[index],
-            device_id=device, device_id_type=MESH,
-        )
-
-    sent = []
-
-    def send(index, source, place, device):
-        task = copy(index, source, place, device)
-        task.start()
-        sent.append(task)
-
-    def wait(index, place):
-        copy(index, place, place, over_core).wait_recv()
-
-    def part(c, s):
-        return part_ref.at[
-            pl.ds(s * count, count), pl.ds(pl.multiple_of(c * width, 128), width)
-        ]
-
-    loads = []
-    for i, b in enumerate((1 - y, y)):
-        for s in range(CHUNKS):
-            at = pl.ds(s * count, count)
-            index = i * CHUNKS + s
-            send(index, part(2 * b + 1 - core, s), core_ref.at[i, at, :], over_core)
-            load = pltpu.make_async_copy(
-                part(2 * b + core, s), own_ref.at[i, at, :], load_sem.at[index]
-            )
-            load.start()
-            loads.append(load)
-    for i in range(2):
-        for s in range(CHUNKS):
-            at = pl.ds(s * count, count)
-            index = i * CHUNKS + s
-            loads[index].wait()
-            wait(index, core_ref.at[i, at, :])
-            add_rows(own_ref.at[i, at, :], own_ref.at[i, at, :], core_ref.at[i, at, :], count)
-            if i == 0:
-                send(2 * CHUNKS + s, own_ref.at[0, at, :], y_ref.at[at, :], over_y)
-    left, right = pl.ds(0, half), pl.ds(half, half)
-    kept = []
-    for s in range(CHUNKS):
-        at = pl.ds(s * count, count)
-        wait(2 * CHUNKS + s, y_ref.at[at, :])
-        add_rows(own_ref.at[1, at, :], own_ref.at[1, at, :], y_ref.at[at, :], count)
-        place = out_ref.at[pl.ds(pl.multiple_of(x * rows + s * count, 128), count), :]
-        theirs = own_ref.at[1, at, pl.ds(pl.multiple_of((1 - x) * half, 128), half)]
-        ours = own_ref.at[1, at, pl.ds(pl.multiple_of(x * half, 128), half)]
-        send(3 * CHUNKS + s, theirs, place, over_x)
-        task = pltpu.make_async_copy(ours, place, out_sem.at[s])
-        task.start()
-        kept.append(task)
-    for s in range(CHUNKS):
-        wait(
-            3 * CHUNKS + s,
-            out_ref.at[pl.ds(pl.multiple_of((1 - x) * rows + s * count, 128), count), :],
-        )
-    for task in sent:
-        task.wait_send()
-    for task in kept:
-        task.wait()
-
-
-def scatter_heads(values, x, collective_id):
-    cols = lax.axis_size("col")
-    if cols != 4:
-        mine = lax.psum_scatter(values, "col", scatter_dimension=1, tiled=True)
-        return in_order(x, pick(mine, x, 1), swap_rows(pick(mine, 1 - x, 1)), 0)
-    rows, width = values.shape[0], values.shape[1] // cols
-    return pl.pallas_call(
-        scatter_heads_kernel,
-        in_specs=[pl.BlockSpec(memory_space=pl.ANY)],
-        out_specs=pl.BlockSpec(memory_space=pl.ANY),
-        out_shape=jax.ShapeDtypeStruct((PAIR * rows, width // PAIR), BF16),
-        scratch_shapes=[
-            pltpu.VMEM((2, rows, width), BF16),
-            pltpu.VMEM((2, rows, width), BF16),
-            pltpu.VMEM((rows, width), BF16),
-            pltpu.SemaphoreType.DMA((2 * CHUNKS,)),
-            pltpu.SemaphoreType.DMA((CHUNKS,)),
-            pltpu.SemaphoreType.DMA((4 * CHUNKS,)),
-            pltpu.SemaphoreType.DMA((4 * CHUNKS,)),
-        ],
-        cost_estimate=taking(32),
-        compiler_params=pltpu.CompilerParams(
-            collective_id=collective_id, has_side_effects=True, vmem_limit_bytes=32 << 20
-        ),
-        name="scatter_heads",
-    )(values)
+def scatter_heads(values, x):
+    mine = lax.psum_scatter(values, "col", scatter_dimension=1, tiled=True)
+    return in_order(x, pick(mine, x, 1), swap_rows(pick(mine, 1 - x, 1)), 0)
 
 
 def sum_rows_kernel(part_ref, out_ref, slots_ref, send_sem, recv_sem):
@@ -1089,13 +1025,13 @@
     )
 
 
-def exchange_beside(kernel, blocks_ref, all_ref, steps, local, *sems):
+def exchange_beside(kernel, blocks_ref, all_ref, steps, local, *sems, more=()):
     row, col = lax.axis_index("row"), lax.axis_index("col")
     others = [col + d - 2 * d * ((col // d) % 2) if d < 3 else 3 - col for d in steps]
 
     @pl.when(pl.program_id(0) == 0)
     def _():
-        meet([(row, other) for other in others])
+        meet([(row, other) for other in others] + list(more))
         for i, other in enumerate(others):
             column_block(blocks_ref, all_ref, other, sems, i).start()
         if local is not None:
@@ -1268,8 +1204,11 @@
         self.over_x, self.over_y, self.over_core = peers(row, col)
         x, y = self.x, self.y
         self.order = ((1 - x, 1 - y), (1 - x, y), (x, 1 - y), (x, y))
-        self.half = sent_ref.shape[1] // 2
+        self.theirs = [2 * b + 1 - self.core for _, b in self.order]
+        self.ours = [2 * b + self.core for _, b in self.order]
+        self.half = own_ref.shape[1] // 2
         self.rows = (pl.ds(0, self.half), pl.ds(self.half, self.half))
+        self.given = Copies(copies.send_sem, copies.recv_sem, self.over_core)
 
     def send(self, index, source, place, device):
         self.copies.send(self.base + index, source, place, device)
@@ -1278,16 +1217,22 @@
         self.copies.wait(self.base + index, place)
 
     def give(self, i, h):
-        a, b = self.order[i]
-        self.fill(self.sent.at[i], a, 2 * b + 1 - self.core, h, None)
+        a, _ = self.order[i]
+        self.fill(self.sent.at[i], a, self.theirs[i], h, None)
         at = self.rows[h]
-        self.send(2 * i + h, self.sent.at[i, at, :], self.core_part.at[i, at, :], self.over_core)
+        self.given.send(
+            self.base + 2 * i + h, self.sent.at[i, at, :], self.core_part.at[i, at, :], self.over_core
+        )
 
     def keep(self, i, h):
-        a, b = self.order[i]
+        a, _ = self.order[i]
         at = self.rows[h]
         self.wait(2 * i + h, self.core_part.at[i, at, :])
-        self.fill(self.own.at[i], a, 2 * b + self.core, h, self.core_part.at[i])
+        self.fill(self.own.at[i], a, self.ours[i], h, self.core_part.at[i])
+        self.part_done(i, h)
+
+    def part_done(self, i, h):
+        at = self.rows[h]
         if h == 0 and i in (0, 1):
             self.send(8 + i, self.own.at[i, at, :], self.x_ref.at[i], self.over_x)
         if h == 1 and i in (0, 2):
@@ -1310,6 +1255,14 @@
         for h in range(2):
             self.keep(3, h)
 
+    def settle(self):
+        self.given.finish()
+
+    def drain(self):
+        view = self.own.at[0, self.rows[0], :]
+        for index in range(self.SEMS):
+            self.copies.copy(self.base + index, view, view, self.over_core).wait_send()
+
     def add(self, i, h, ref):
         at = self.own.at[i, self.rows[h], :]
         add_rows(at, at, ref, self.half)
@@ -1335,6 +1288,112 @@
         return self.own[3, pl.ds(start, count), :].astype(F32) + self.last[
             h, pl.ds(other, count), :
         ].astype(F32)
+
+
+class PartsScatter(PlaneScatter):
+    def __init__(self, copies, base, parts_ref, load_sem, *scratch):
+        super().__init__(copies, base, None, None, *scratch)
+        blocks = [a * 4 for a, _ in self.order]
+        self.parts, self.load_sem = parts_ref, load_sem
+        self.sources = [parts_ref.at[at + c] for at, c in zip(blocks, self.theirs)]
+        self.loads = [
+            pltpu.make_async_copy(parts_ref.at[at + c], self.own.at[i], load_sem.at[i])
+            for i, (at, c) in enumerate(zip(blocks, self.ours))
+        ]
+
+    def start(self):
+        for i, load in enumerate(self.loads):
+            load.start()
+            for h, at in enumerate(self.rows):
+                self.given.send(
+                    self.base + 2 * i + h, self.sources[i].at[at, :],
+                    self.core_part.at[i, at, :], self.over_core,
+                )
+
+    def keep(self, i, h):
+        if h == 0:
+            self.loads[i].wait()
+        at = self.rows[h]
+        self.wait(2 * i + h, self.core_part.at[i, at, :])
+        self.add(i, h, self.core_part.at[i, at, :])
+        self.part_done(i, h)
+
+
+class LineScatter:
+    def __init__(self, up_send, up_recv, down_send, down_recv, part, up_ref, down_ref):
+        self.part, self.row, self.col = part, lax.axis_index("row"), lax.axis_index("col")
+        self.z = self.row // PAIR
+        last = LINES - 1
+        self.ways = (
+            (self.z, lambda n: n, up_ref, up_send, up_recv, jnp.minimum(self.row + PAIR, PAIR * last + PAIR - 1)),
+            (last - self.z, lambda n: last - n, down_ref, down_send, down_recv, jnp.maximum(self.row - PAIR, 0)),
+        )
+
+    def clear(self):
+        for n, _, slots, _, _, _ in self.ways:
+
+            @pl.when(n == 0)
+            def _():
+                slots[LINES - 2] = jnp.zeros(slots.shape[1:], slots.dtype)
+
+    def task(self, way, step, source):
+        _, _, slots, send, recv, device = way
+        return pltpu.make_async_remote_copy(
+            source, slots.at[step], send.at[step], recv.at[step],
+            device_id=(device, self.col), device_id_type=MESH,
+        )
+
+    def sends(self, way, step, act):
+        n, place, slots, _, _, _ = way
+
+        @pl.when(n == 0)
+        def _():
+            act(self.task(way, step, self.part(place(LINES - 1 - step))))
+
+        if step > 0:
+
+            @pl.when((n > 0) & (n <= step))
+            def _():
+                act(self.task(way, step, slots.at[step - 1]))
+
+    def start(self):
+        for way in self.ways:
+            self.sends(way, 0, lambda task: task.start())
+
+    def hop(self, step):
+        for way in self.ways:
+            n, place, slots, _, _, _ = way
+
+            @pl.when((n >= 1) & (n <= step + 1))
+            def _():
+                self.task(way, step, slots.at[step]).wait_recv()
+                add_rows(
+                    slots.at[step], slots.at[step], self.part(place(LINES - 2 - step + n)),
+                    slots.shape[1],
+                )
+
+            self.sends(way, step + 1, lambda task: task.start())
+
+    def receive(self):
+        last = LINES - 2
+        for way in self.ways:
+            n, _, slots, _, _, _ = way
+
+            @pl.when(n >= 1)
+            def _():
+                self.task(way, last, slots.at[last]).wait_recv()
+
+    def total(self, at):
+        last = LINES - 2
+        result = self.part(self.z)[at, :].astype(F32)
+        for _, _, slots, _, _, _ in self.ways:
+            result = result + slots[last, at, :].astype(F32)
+        return result
+
+    def finish(self):
+        for way in self.ways:
+            for step in range(LINES - 1):
+                self.sends(way, step, lambda task: task.wait_send())
 
 
 STEP = 128
@@ -1429,9 +1488,9 @@
 
 
 def back_second_kernel(
-    gate_ref, up_ref, weight_ref, values_ref, stats_ref, gain_ref, base_ref,
-    out_ref, low_ref, dgain_ref,
-    gate_vmem, up_vmem, weight_vmem, left_ref, sums_ref, load_sem, send_sem, recv_sem, *scratch,
+    gate_ref, up_ref, weight_ref, hidden_hbm, grad_hbm, values_ref, stats_ref, gain_ref, base_ref,
+    out_ref, low_ref, dgain_ref, down_ref,
+    hidden_ref, grad_ref, gate_vmem, up_vmem, weight_vmem, left_ref, sums_ref, load_sem, send_sem, recv_sem, *scratch,
 ):
     rows, width = out_ref.shape
     x, y, core, _, _ = places()
@@ -1450,7 +1509,11 @@
     lefts = [load_left(0, 1 - x), load_left(1, x)]
     columns = (2 * (1 - y) + 1 - core, 2 * (1 - y) + core, 2 * y + 1 - core, 2 * y + core)
     weights = [load_weight(i, c) for i, c in enumerate(columns)]
-    for task in (*lefts[0], *weights, *lefts[1]):
+    others = [
+        pltpu.make_async_copy(hidden_hbm, hidden_ref, load_sem.at[8]),
+        pltpu.make_async_copy(grad_hbm, grad_ref, load_sem.at[9]),
+    ]
+    for task in (*lefts[0], *weights, *lefts[1], *others):
         task.start()
     meet(devices)
     copies = Copies(send_sem, recv_sem, devices[2])
@@ -1488,7 +1551,13 @@
     scatter.give(3, 1)
     scatter.keep(3, 0)
     scatter.keep(3, 1)
+    scatter.settle()
     scatter.second()
+    for task in others:
+        task.wait()
+    for c in range(down_ref.shape[0]):
+        right = grad_ref[:, c * width : (c + 1) * width]
+        down_ref[c] = dot(hidden_ref[...], right).astype(BF16)
     scatter.third()
     norm = NormBack(
         copies, PlaneScatter.SEMS, values_ref, stats_ref, gain_ref, base_ref, out_ref, low_ref,
@@ -1499,99 +1568,324 @@
     copies.finish()
 
 
-def back_second(gate, up, weight, values, stats, gain, base, collective_id):
+def back_second(gate, up, weight, hidden, grad, values, stats, gain, base, collective_id):
     rows, width = values.shape
-    hidden, tokens = gate.shape
+    units, tokens = gate.shape
     vmem, anywhere = pl.BlockSpec(memory_space=pltpu.VMEM), pl.BlockSpec(memory_space=pl.ANY)
     sems = lambda n: pltpu.SemaphoreType.DMA((n,))
     return pl.pallas_call(
         back_second_kernel,
-        in_specs=[anywhere] * 3 + [vmem] * 4,
-        out_specs=[vmem] * 3,
+        in_specs=[anywhere] * 5 + [vmem] * 4,
+        out_specs=[vmem] * 4,
         out_shape=[
             jax.ShapeDtypeStruct((rows, width), F32),
             jax.ShapeDtypeStruct((rows, width), BF16),
             jax.ShapeDtypeStruct((1, width), F32),
+            jax.ShapeDtypeStruct((grad.shape[1] // width, units, width), BF16),
         ],
         scratch_shapes=[
+            pltpu.VMEM(hidden.shape, BF16), pltpu.VMEM(grad.shape, BF16),
             pltpu.VMEM(gate.shape, BF16), pltpu.VMEM(up.shape, BF16),
-            pltpu.VMEM(weight.shape, BF16), pltpu.VMEM((2, tokens, hidden), BF16),
+            pltpu.VMEM(weight.shape, BF16), pltpu.VMEM((2, tokens, units), BF16),
             pltpu.VMEM((4, 8, rows), F32),
-            sems(8), sems(PlaneScatter.SEMS + 3), sems(PlaneScatter.SEMS + 3),
+            sems(10), sems(PlaneScatter.SEMS + 3), sems(PlaneScatter.SEMS + 3),
             *scatter_scratch(rows, width),
+        ],
+        compiler_params=pltpu.CompilerParams(
+            collective_id=collective_id, has_side_effects=True, vmem_limit_bytes=63 << 20
+        ),
+        cost_estimate=taking(50),
+        name="back_second",
+    )(gate, up, weight, hidden, grad, values, stats, gain.reshape(1, width), base)
+
+
+def back_first_kernel(
+    grad_ref, weight_ref, values_ref, stats_ref, gain_ref, base_ref, part_ref, ffn_ref, heads_ref,
+    out_ref, dgain_ref, query_ref, key_ref, value_ref, gate_ref, up_grad_ref, out_grad_ref,
+    sums_ref, up_ref, down_line_ref, heads_up_ref, heads_down_ref, swap_ref, swapped_ref, turn_ref,
+    send_sem, recv_sem, *scratch,
+):
+    line_sems, scratch = scratch[:12], scratch[12:]
+    rows, width = out_ref.shape
+    x, _, _, row, col = places()
+    devices = around()
+    size = PAIR * LINES
+    meet((*devices, ((row + PAIR) % size, col), ((row + size - PAIR) % size, col)))
+    copies = Copies(send_sem, recv_sem, devices[2])
+    depth, columns = up_ref.shape[2:]
+
+    def line_of(k):
+        at = pl.ds(k * columns, columns)
+        return LineScatter(
+            *line_sems[4 * k : 4 * k + 4],
+            lambda b: part_ref.at[pl.ds(pl.multiple_of(b * depth, 128), depth), at],
+            up_ref.at[k], down_line_ref.at[k],
+        )
+
+    out_depth = out_grad_ref.shape[0]
+    heads = LineScatter(
+        *line_sems[8:],
+        lambda b: heads_ref.at[pl.ds(pl.multiple_of(b * out_depth, 128), out_depth), :],
+        heads_up_ref, heads_down_ref,
+    )
+    lines = [line_of(k) for k in range(2)] + [heads]
+    for line in lines:
+        line.clear()
+        line.start()
+
+    def product(at, c):
+        weight = weight_ref[pl.ds(pl.multiple_of(c * width, 128), width), :]
+        return dot(grad_ref[at, :], weight, (1,), (1,))
+
+    scatter = PlaneScatter(copies, 0, filling(rows, product), *scratch)
+    norm = NormBack(
+        copies, PlaneScatter.SEMS, values_ref, stats_ref, gain_ref, base_ref, out_ref, None,
+        dgain_ref, sums_ref,
+    )
+    half = depth // PAIR
+    theirs = pl.multiple_of((1 - x) * half, 128)
+    ours = pl.multiple_of(x * half, 128)
+    swap = PlaneScatter.SEMS + 3
+    units = ffn_ref.shape[2]
+    scatter.first()
+    for line in lines:
+        line.hop(0)
+    scatter.settle()
+    scatter.second()
+    here = pl.ds(pl.multiple_of(x * units, 16), units)
+    there = pl.ds(pl.multiple_of((1 - x) * units, 16), units)
+    for w in range(2):
+        copies.send(
+            swap + 2 + w, ffn_ref.at[0, w, :, pl.ds(theirs, half)], turn_ref.at[w, here, :], devices[0]
+        )
+        turn_ref[w, here, :] = ffn_ref[0, w, :, pl.ds(ours, half)]
+    for line in lines:
+        line.hop(1)
+    scatter.third()
+    norm.start(scatter.result, devices[1:4])
+    part = width // PAIR
+    outs = (query_ref, key_ref, value_ref)
+
+    def pieces(k):
+        for w in range(3):
+            start, end = max(k * columns, w * part), min((k + 1) * columns, (w + 1) * part)
+            if start < end:
+                yield outs[w], start - w * part, start, end - start
+
+    def close(k):
+        lines[k].receive()
+        at = pl.ds(k * columns, columns)
+        swap_ref[:, at] = lines[k].total(pl.ds(theirs, half)).astype(BF16)
+        copies.send(swap + k, swap_ref.at[:, at], swapped_ref.at[:, at], devices[0])
+        total = lines[k].total(pl.ds(ours, half))
+        for ref, place, start, size in pieces(k):
+            columns_at = pl.ds(pl.multiple_of(x * part + place, 128), size)
+            ref[:, columns_at] = total[:, start - k * columns : start - k * columns + size]
+
+    close(0)
+    norm.finish()
+    close(1)
+    for w, ref in enumerate((gate_ref, up_grad_ref)):
+        copies.wait(swap + 2 + w, turn_ref.at[w, there, :])
+        for j in range(PAIR * units // 128):
+            at = slice(j * 128, (j + 1) * 128)
+            ref[:, at] = turn_ref[w, at, :].T.astype(F32)
+    heads.receive()
+    out_grad_ref[...] = heads.total(pl.ds(0, out_depth))
+    heads.finish()
+    for k in range(2):
+        at = pl.ds(k * columns, columns)
+        copies.wait(swap + k, swapped_ref.at[:, at])
+        for ref, place, start, size in pieces(k):
+            columns_at = pl.ds(pl.multiple_of((1 - x) * part + place, 128), size)
+            ref[:, columns_at] = swapped_ref[:, start : start + size].astype(F32)
+        lines[k].finish()
+    copies.finish()
+
+
+def back_first(
+    grad, weight, values, stats, gain, base, part, ffn, heads, collective_id
+):
+    rows, width = values.shape
+    depth, columns = part.shape[0] // LINES, part.shape[1]
+    vmem = pl.BlockSpec(memory_space=pltpu.VMEM)
+    sems = lambda n: pltpu.SemaphoreType.DMA((n,))
+    count = PlaneScatter.SEMS + 7
+    units = ffn.shape[2]
+    return pl.pallas_call(
+        back_first_kernel,
+        in_specs=[vmem] * 9,
+        out_specs=[vmem] * 8,
+        out_shape=[
+            jax.ShapeDtypeStruct((rows, width), F32),
+            jax.ShapeDtypeStruct((1, width), F32),
+        ]
+        + [jax.ShapeDtypeStruct((depth // PAIR, width), F32)] * 3
+        + [jax.ShapeDtypeStruct((depth // PAIR, PAIR * units), F32)] * 2
+        + [jax.ShapeDtypeStruct((heads.shape[0] // LINES, width), F32)],
+        scratch_shapes=[
+            pltpu.VMEM((4, 8, rows), F32),
+            pltpu.VMEM((2, LINES - 1, depth, columns // 2), BF16),
+            pltpu.VMEM((2, LINES - 1, depth, columns // 2), BF16),
+            *[pltpu.VMEM((LINES - 1, heads.shape[0] // LINES, width), BF16)] * 2,
+            pltpu.VMEM((depth // PAIR, columns), BF16), pltpu.VMEM((depth // PAIR, columns), BF16),
+            pltpu.VMEM((2, PAIR * units, depth // PAIR), BF16),
+            sems(count), sems(count), *[sems(LINES - 1)] * 12,
+            *scatter_scratch(rows, width),
+        ],
+        compiler_params=pltpu.CompilerParams(
+            collective_id=collective_id, has_side_effects=True, vmem_limit_bytes=63 << 20
+        ),
+        cost_estimate=taking(60),
+        name="back_first",
+    )(grad, weight, values, stats, gain.reshape(1, width), base, part, ffn, heads)
+
+
+def back_heads_kernel(
+    low_ref, weight_ref, attn_hbm, hidden_hbm, down_hbm, blocks_ref,
+    out_ref, part_ref, mix_ref, all_ref,
+    stage_ref, attn_ref, hidden_ref, down_ref, left_ref, sent_ref, own_ref, core_ref, y_ref, give_ref, come_ref,
+    load_sem, out_sem, send_sem, recv_sem,
+):
+    rows, width = low_ref.shape
+    half = width // PAIR
+    count = rows // CHUNKS
+    x, y, core, row, col = places()
+    over_x, over_y, over_core = peers(row, col)
+    over_far = (row, 3 - col)
+    loads = [
+        pltpu.make_async_copy(source, place, load_sem.at[i])
+        for i, (source, place) in enumerate(
+            ((attn_hbm, attn_ref), (hidden_hbm, hidden_ref), (down_hbm, down_ref))
+        )
+    ]
+    for load in loads:
+        load.start()
+    stage = pltpu.make_async_copy(blocks_ref.at[col], stage_ref, load_sem.at[3])
+    stage.start()
+    meet((over_x, over_y, over_core, over_far))
+    copies = Copies(send_sem, recv_sem, over_core)
+    sides = (1 - y, y)
+
+    def at_chunk(s):
+        return pl.ds(s * count, count)
+
+    def product(s, c):
+        weight = weight_ref[pl.ds(pl.multiple_of(c * width, 128), width), :]
+        return dot(low_ref[at_chunk(s), :], weight, (1,), (1,))
+
+    def give(i, s):
+        at = at_chunk(s)
+        sent_ref[i, at, :] = product(s, 2 * sides[i] + 1 - core).astype(BF16)
+        copies.send(i * CHUNKS + s, sent_ref.at[i, at, :], core_ref.at[i, at, :], over_core)
+
+    def keep(i, s):
+        at = at_chunk(s)
+        part = product(s, 2 * sides[i] + core)
+        copies.wait(i * CHUNKS + s, core_ref.at[i, at, :])
+        own_ref[i, at, :] = (part + core_ref[i, at, :].astype(F32)).astype(BF16)
+        if i == 0:
+            copies.send(2 * CHUNKS + s, own_ref.at[0, at, :], y_ref.at[at, :], over_y)
+
+    depth = give_ref.shape[1]
+
+    def out_grad(z, x):
+        at = pl.ds(pl.multiple_of((PAIR * z + x) * depth, 128), depth)
+        return dot(attn_ref[:, at], low_ref[...], (0,), (0,))
+
+    others = (((col + 2) % 4, over_y), (3 - col, over_far), (col + 1 - 2 * core, over_core))
+    for s in range(CHUNKS):
+        give(0, s)
+    loads[0].wait()
+    for z in range(LINES):
+        give_ref[z] = out_grad(z, 1 - x).astype(BF16)
+    copies.send(4 * CHUNKS, give_ref, come_ref, over_x)
+    for s in range(CHUNKS):
+        keep(0, s)
+    for i, (other, device) in enumerate(others):
+        copies.send(4 * CHUNKS + 1 + i, blocks_ref.at[other], all_ref.at[col], device)
+    for s in range(CHUNKS):
+        give(1, s)
+    for s in range(CHUNKS):
+        keep(1, s)
+    for z in range(LINES):
+        part_ref[z * depth : (z + 1) * depth, :] = out_grad(z, x).astype(BF16)
+    stage.wait()
+    stage = pltpu.make_async_copy(stage_ref, all_ref.at[col], load_sem.at[3])
+    stage.start()
+    for load in loads[1:]:
+        load.wait()
+    for a in range(PAIR):
+        turn_rows(left_ref, hidden_ref, a, rows)
+    kept = []
+    for s in range(CHUNKS):
+
+        @pl.loop(0, PAIR * rows // TILE)
+        def _(i):
+            a, start = i // (rows // TILE), pl.multiple_of(i % (rows // TILE) * TILE, TILE)
+            left = left_ref[pl.ds(pl.multiple_of(i * TILE, TILE), TILE), :]
+            mix_ref[a * CHUNKS + s, pl.ds(start, TILE), :] = dot(left, down_ref[s]).astype(BF16)
+
+        at = at_chunk(s)
+        copies.wait(2 * CHUNKS + s, y_ref.at[at, :])
+        own_ref[1, at, :] = (
+            own_ref[1, at, :].astype(F32) + y_ref[at, :].astype(F32)
+        ).astype(BF16)
+        place = out_ref.at[pl.ds(pl.multiple_of(x * rows + s * count, 128), count), :]
+        theirs = own_ref.at[1, at, pl.ds(pl.multiple_of((1 - x) * half, 128), half)]
+        ours = own_ref.at[1, at, pl.ds(pl.multiple_of(x * half, 128), half)]
+        copies.send(3 * CHUNKS + s, theirs, place, over_x)
+        task = pltpu.make_async_copy(ours, place, out_sem.at[s])
+        task.start()
+        kept.append(task)
+    copies.wait(4 * CHUNKS, come_ref)
+    for z in range(LINES):
+        at = pl.ds(z * depth, depth)
+        add_rows(part_ref.at[at, :], part_ref.at[at, :], come_ref.at[z], depth)
+    for s in range(CHUNKS):
+        copies.wait(
+            3 * CHUNKS + s,
+            out_ref.at[pl.ds(pl.multiple_of((1 - x) * rows + s * count, 128), count), :],
+        )
+    for i, (other, _) in enumerate(others):
+        copies.wait(4 * CHUNKS + 1 + i, all_ref.at[other])
+    copies.finish()
+    stage.wait()
+    for task in kept:
+        task.wait()
+
+
+def back_heads(low, weight, attn, hidden, down, blocks, collective_id):
+    rows, width = low.shape
+    depth = weight.shape[0] // (PAIR * LINES)
+    vmem, anywhere = pl.BlockSpec(memory_space=pltpu.VMEM), pl.BlockSpec(memory_space=pl.ANY)
+    sems = lambda n: pltpu.SemaphoreType.DMA((n,))
+    wide = pltpu.VMEM((2, rows, width), BF16)
+    swapped = pltpu.VMEM((LINES, depth, width), BF16)
+    return pl.pallas_call(
+        back_heads_kernel,
+        in_specs=[vmem] * 2 + [anywhere] * 4,
+        out_specs=[anywhere, vmem, vmem, anywhere],
+        out_shape=[
+            jax.ShapeDtypeStruct((PAIR * rows, width // PAIR), BF16),
+            jax.ShapeDtypeStruct((LINES * depth, width), BF16),
+            jax.ShapeDtypeStruct((PAIR * CHUNKS, rows, width), BF16),
+            jax.ShapeDtypeStruct(blocks.shape, BF16),
+        ],
+        scratch_shapes=[
+            pltpu.VMEM(blocks.shape[1:], BF16),
+            pltpu.VMEM(attn.shape, BF16), pltpu.VMEM(hidden.shape, BF16),
+            pltpu.VMEM(down.shape, BF16), pltpu.VMEM(hidden.shape[::-1], BF16),
+            wide, wide, wide, pltpu.VMEM((rows, width), BF16),
+            swapped, swapped,
+            sems(4), sems(CHUNKS), sems(4 * CHUNKS + 4), sems(4 * CHUNKS + 4),
         ],
         compiler_params=pltpu.CompilerParams(
             collective_id=collective_id, has_side_effects=True, vmem_limit_bytes=60 << 20
         ),
-        cost_estimate=taking(50),
-        name="back_second",
-    )(gate, up, weight, values, stats, gain.reshape(1, width), base)
-
-
-def back_first_kernel(
-    grad_ref, weight_ref, hidden_ref, down_ref, values_ref, stats_ref, gain_ref, base_ref, resid_ref,
-    out_ref, dgain_ref, mixed_ref,
-    left_ref, sums_ref, send_sem, recv_sem, *scratch,
-):
-    rows, width = out_ref.shape
-    x, _, _, _, _ = places()
-    devices = around()
-    meet(devices)
-    copies = Copies(send_sem, recv_sem, devices[2])
-
-    def product(at, c):
-        weight = weight_ref[pl.ds(pl.multiple_of(c * width, 128), width), :]
-        return dot(grad_ref[at, :], weight, (1,), (1,))
-
-    def mix(at, c):
-        return dot(left_ref[at, :], down_ref[c])
-
-    scatter = PlaneScatter(copies, 0, filling(rows, product), *scratch[:6])
-    mixing = PlaneScatter(copies, PlaneScatter.SEMS + 3, filling(rows, mix), *scratch[6:])
-    norm = NormBack(
-        copies, PlaneScatter.SEMS, values_ref, stats_ref, gain_ref, base_ref, out_ref, None,
-        dgain_ref, sums_ref,
-    )
-    scatter.first()
-    for a in range(PAIR):
-        turn_rows(left_ref, hidden_ref, a, rows)
-    mixing.first()
-    scatter.second()
-    scatter.third()
-    norm.start(scatter.result, devices[1:])
-    mixing.second()
-    norm.finish()
-    mixing.third()
-    for start in range(0, rows, STEP):
-        at = pl.ds(start, STEP)
-        mixed_ref[at, :] = (resid_ref[at, :] + mixing.result(start, STEP)).astype(BF16)
-    copies.finish()
-
-
-def back_first(grad, weight, hidden, down, values, stats, gain, base, resid, collective_id):
-    rows, width = values.shape
-    vmem = pl.BlockSpec(memory_space=pltpu.VMEM)
-    sems = lambda n: pltpu.SemaphoreType.DMA((n,))
-    return pl.pallas_call(
-        back_first_kernel,
-        in_specs=[vmem] * 9,
-        out_specs=[vmem] * 3,
-        out_shape=[
-            jax.ShapeDtypeStruct((rows, width), F32),
-            jax.ShapeDtypeStruct((1, width), F32),
-            jax.ShapeDtypeStruct((rows, width), BF16),
-        ],
-        scratch_shapes=[
-            pltpu.VMEM(hidden.shape[::-1], BF16), pltpu.VMEM((4, 8, rows), F32),
-            sems(2 * PlaneScatter.SEMS + 3), sems(2 * PlaneScatter.SEMS + 3),
-            *scatter_scratch(rows, width), *scatter_scratch(rows, width),
-        ],
-        compiler_params=pltpu.CompilerParams(
-            collective_id=collective_id, has_side_effects=True, vmem_limit_bytes=62 << 20
-        ),
-        cost_estimate=taking(80),
-        name="back_first",
-    )(grad, weight, hidden, down, values, stats, gain.reshape(1, width), base, resid)
+        cost_estimate=taking(60),
+        name="back_heads",
+    )(low, weight, attn, hidden, down, blocks)
 
 
 def per_device(
@@ -1662,11 +1956,14 @@
     normed_second, hidden_low, grad_gate, grad_up, stats_second = feed_forward(
         resid_all, gains[1], ffn_weight, grad_all, down_all
     )
-    grad_ffn = weight_grads((grad_gate, grad_up), normed_second, width, "ffn_grads")
+    if fast:
+        grad_ffn = weight_grads((grad_gate, grad_up), normed_second, width, "ffn_grads")
+    else:
+        grad_ffn = weight_grads((grad_gate, grad_up), normed_second, width, "ffn_grads")
     own_stats = pick(stats_second, x, 0)
     if fast:
-        grad_resid, grad_resid_low, mlp_gain_part = back_second(
-            after(grad_gate, grad_ffn), grad_up, ffn_weight,
+        grad_resid, grad_resid_low, mlp_gain_part, down_blocks = back_second(
+            after(grad_gate, grad_ffn), grad_up, ffn_weight, hidden_low, grad_all,
             resid, own_stats, mlp_gain, out_grad, 4,
         )
         mlp_gain_part = mlp_gain_part[0]
@@ -1682,37 +1979,49 @@
         grad_resid_low = grad_resid.astype(BF16)
     grad_ffn = scatter_line(grad_ffn)
 
-    grad_out_weight = dot(attn_all, grad_resid_low, (0,), (0,)).astype(BF16)
-    grad_out_weight = grad_out_weight.reshape(lines, PAIR, depth, width)
-    grad_out_other = swap_rows(pick(grad_out_weight, 1 - x, 1))
-    grad_attn = scatter_heads(dot(grad_resid_low, out_all, (1,), (1,)).astype(BF16), x, 5)
-    grad_out_weight = pick(grad_out_weight, x, 1) + grad_out_other
-    grad_attn = after(grad_attn, grad_out_weight)
-    grad_down = weight_grads((after(hidden_low, grad_attn),), grad_all, width, "down_grads")
-    grad_down = grad_down.reshape(cols, hidden, width)
-    backward = (queries, keys, values, grad_attn, lse, cosine, sine, plane_segments)
     if fast:
-        grad_qkv, bias_sums, grad_down = attention_backward(*backward, grad_down, 9)
+        grad_attn, grad_out_weight, mixed, grad_down = back_heads(
+            grad_resid_low, out_all, attn_all, hidden_low, down_all, down_blocks, 5
+        )
+        grad_qkv, bias_sums, mixed = attention_backward(
+            queries, keys, values, grad_attn, lse, cosine, sine, plane_segments, mixed, resid, 9
+        )
     else:
-        grad_qkv, bias_sums = attention_backward(*backward)
-        grad_down = lax.all_to_all(grad_down, "col", split_axis=0, concat_axis=0, tiled=True)
+        grad_out_weight = dot(attn_all, grad_resid_low, (0,), (0,)).astype(BF16)
+        grad_out_weight = grad_out_weight.reshape(lines, PAIR, depth, width)
+        grad_out_weight = pick(grad_out_weight, x, 1) + swap_rows(pick(grad_out_weight, 1 - x, 1))
+        grad_out_weight = scatter_line(grad_out_weight.reshape(lines * depth, width)).astype(F32)
+        grad_attn = scatter_heads(dot(grad_resid_low, out_all, (1,), (1,)).astype(BF16), x)
+        grad_qkv, bias_sums = attention_backward(
+            queries, keys, values, grad_attn, lse, cosine, sine, plane_segments
+        )
+        grad_down = weight_grads((hidden_low,), grad_all, width, "down_grads")
+        grad_down = lax.all_to_all(
+            grad_down.reshape(cols, hidden, width), "col", split_axis=0, concat_axis=0, tiled=True
+        )
     grad_qkv_weight = dot(normed_first, grad_qkv, (0,), (0,)).astype(BF16)
-    grad_out_weight = scatter_line(
-        after(grad_out_weight, grad_ffn).reshape(lines * depth, width)
-    )
-    grad_down = scatter_line(
-        after(grad_down, grad_out_weight).reshape(lines * hidden, width)
-    )
+    grad_down = scatter_line(after(grad_down, grad_ffn).reshape(lines * hidden, width))
     grad_qkv_later = after(grad_qkv, grad_qkv_weight)
-    grad_qkv_weight = scatter_line(grad_qkv_weight)
     own_stats = pick(stats_first, x, 0)
     if fast:
-        tokens_grad, attn_gain_part, mixed = back_first(
-            grad_qkv_later, qkv_weight, hidden_low, down_all,
-            tokens, own_stats, attn_gain, grad_resid, resid, 6,
+        (
+            tokens_grad, attn_gain_part, query_grad, key_grad, value_grad, gate_grad, up_grad,
+            grad_out_weight,
+        ) = back_first(
+            after(grad_qkv_later, grad_down), qkv_weight,
+            tokens, own_stats, attn_gain, grad_resid, grad_qkv_weight, grad_ffn, grad_out_weight, 6,
         )
         attn_gain_part = attn_gain_part[0]
     else:
+        kept, other = pick(grad_ffn[0], x, 2), swap_rows(pick(grad_ffn[0], 1 - x, 2))
+        gate_grad, up_grad = (
+            in_order(x, kept[i], other[i], 0).T.astype(F32) for i in range(2)
+        )
+        kept, other = own_rows(scatter_line(grad_qkv_weight), x)
+        query_grad, key_grad, value_grad = (
+            in_order(x, kept[:, at : at + half], other[:, at : at + half], 1).astype(F32)
+            for at in (0, half, 2 * half)
+        )
         grad_first = scatter_plane(
             dot(grad_qkv_later, qkv_weight, (1,), (1,)).astype(BF16), "scatter_first", 6
         )
@@ -1725,10 +2034,6 @@
             back_project((hidden_low,), down_all[:, None], "mix"), "scatter_mixed", 10
         )
         mixed = mixed.astype(BF16)
-    kept, other = pick(grad_ffn[0], x, 2), swap_rows(pick(grad_ffn[0], 1 - x, 2))
-    gate_grad, up_grad = (
-        in_order(x, kept[i], other[i], 0).T.astype(F32) for i in range(2)
-    )
 
     bias_part = jnp.sum(bias_sums, axis=(0, 1)).reshape(3, half)
     bias_part = jnp.where(
@@ -1738,25 +2043,19 @@
         jnp.concatenate(
             [bias_part, attn_gain_part[None], mlp_gain_part[None], jnp.zeros((3, width), F32)]
         ),
-        7,
+        11,
     )
-    grad_qkv_weight = own_rows(grad_qkv_weight, x)
-    wide = lambda w: jnp.where(
-        x == 0,
-        jnp.concatenate([grad_qkv_weight[0][:, w], grad_qkv_weight[1][:, w]], axis=1),
-        jnp.concatenate([grad_qkv_weight[1][:, w], grad_qkv_weight[0][:, w]], axis=1),
-    ).astype(F32)
     return (
         mixed,
         tokens_grad,
         vectors[3],
-        wide(slice(0, half)),
+        query_grad,
         vectors[0],
-        wide(slice(half, 2 * half)),
+        key_grad,
         vectors[1],
-        wide(slice(2 * half, 3 * half)),
+        value_grad,
         vectors[2],
-        grad_out_weight.astype(F32),
+        grad_out_weight,
         vectors[4],
         gate_grad,
         up_grad,

time: 631 us -> 614 us (0.973)
  Pallas kernels: 530 us -> 549 us
  waiting for transfers between devices: 15.9 us -> 0.8 us
  matrix products: 25.6 us -> 18.5 us
    pallas_call x2, Pallas kernels: 87.9 us -> 121 us  [the longest x1 65.8 us: back_heads(): pl.pallas_call(back_heads_kernel, in_specs=[vmem] * 2 + [anywhere] * 4, o...]
    ppermute x3 -> x0, waiting for transfers between devices: 15.1 us -> none  [swap_rows(): return lax.ppermute(values, 'row', row_pairs())]
    pallas_call x1, Pallas kernels: 89.6 us -> 77.8 us  [back_first(): pl.pallas_call(back_first_kernel, in_specs=[vmem] * 9, out_specs=[vmem] *...]
    pallas_call x2 -> x1, Pallas kernels: 27.4 us -> 17.1 us  [weight_grads(): pl.pallas_call(weight_grads_kernel, grid=(blocks,), in_specs=[whole((hidd...]
    pallas_call x1, Pallas kernels: 37 us -> 45.4 us  [attention_backward(): pl.pallas_call(kernel, grid=(seqs,), in_specs=in_specs, out_specs=out_spe...]
    dot_general x4 -> x2, matrix products: 25.6 us -> 18.5 us  [dot(): lax.dot_general(left, right, ((left_dims, right_dims), ((), ())), preferr...]
  transfers between devices with their start and end apart: 9 -> 4, of which waited for: 2 -> 0; matrix products, arithmetic and copies ran while one was open for 8% -> 5% of each run, Pallas kernels for 78% -> 68%
where the time goes in v3:
time: 614 us; the launch traced here: 610 us
  Pallas kernels  549 us (89%)
  local copies, waits for them, and re-layouts  20.2 us (3%)
  matrix products  18.5 us (3%)
  between operations  14.4 us (2%)
  other arithmetic  6.64 us (1%)
    pallas_call x1, Pallas kernels, gather_first(): pl.pallas_call(gather_first_kernel, in_specs=[pl.BlockSpec(memory_space=p...  139 us
    pallas_call x1, Pallas kernels, back_first(): pl.pallas_call(back_first_kernel, in_specs=[vmem] * 9, out_specs=[vmem] *...  77.8 us
    pallas_call x1, Pallas kernels, back_heads(): pl.pallas_call(back_heads_kernel, in_specs=[vmem] * 2 + [anywhere] * 4, o...  65.8 us
    pallas_call x1, Pallas kernels, back_second(): pl.pallas_call(back_second_kernel, in_specs=[anywhere] * 5 + [vmem] * 4,...  55.4 us
    pallas_call x1, Pallas kernels, attention_backward(): pl.pallas_call(kernel, grid=(seqs,), in_specs=in_specs, out_specs=out_spe...  45.4 us
    pallas_call x1, Pallas kernels, gather_plane(): pl.pallas_call(gather_plane_kernel, in_specs=[pl.BlockSpec(memory_space=p...  40.7 us
    pallas_call x1, Pallas kernels, gather_heads(): pl.pallas_call(gather_heads_kernel, in_specs=[pl.BlockSpec(memory_space=p...  29.5 us
    pallas_call x1, Pallas kernels, feed_forward(): pl.pallas_call(feed_forward_kernel, grid=(rows // TILE,), in_specs=[tiled...  28.1 us
  transfers between devices with their start and end apart: 4, of which 0 were waited for; matrix products, arithmetic and copies ran while one was open for 5% of the time, Pallas kernels for 68%

profile of v3, /device:TPU:0, one launch (start us, length us, event | category | flops | bytes accessed | tf_op | source)
XLA Modules:
  0.0 610.3 jit_solution(9669450898137382518)
XLA Ops:
  8.7 1.3 select_maximum_fusion.gains_ref
  10.6 139.0 %gather_first.1 = (bf16[2048,2048]{1,0:T(8,128)(2,1)}, bf16[2048,2048]{1,0:T(8,128)(2,1)}, bf16[2048,768]{1,0:T(8,128)(2,1)}, bf16[2048,512]{1,0:T(8,128)(2,1)},...) custom-call(bf16[1024,512]{1,0:T(8,128)(2,1)} %values_ref.1, bf16[1024,512]{1,0:T(8,128)(2,1)} %base_ref.1, ...), custom_call_target="tpu_custom_call" | custom-call | flops 109999996928 | bytes 110000000 | tf_op jit(solution)/shard_map/gather_first/pallas_call | solution.py:659
  150.1 1.5 fusion.2
  152.5 1.4 copy.39.refs_3_.refs_7_
  154.0 1.3 copy.38.refs_5_.refs_6_
  155.3 1.5 fusion.1
  157.2 19.2 %project_heads.1 = (bf16[2048,2048]{1,0:T(8,128)(2,1)}, bf16[2048,256]{1,0:T(8,128)(2,1)S(1)}, bf16[2048,256]{1,0:T(8,128)(2,1)S(1)}, bf16[2048,256]{1,0:T(8,128...) custom-call(bf16[2048,2048]{1,0:T(8,128)(2,1)} %get-tuple-element.60.refs_0_, ...), custom_call_target="tpu_custom_call" | custom-call | flops 16000000000 | bytes 16000000 | tf_op jit(solution)/shard_map/project_heads/pallas_call | solution.py:1093
  179.4 21.1 %attention_forward.1 = (bf16[2048,256]{1,0:T(8,128)(2,1)}, f32[2,8,1024]{2,1,0:T(8,128)}, bf16[4,704,512]{2,1,0:T(8,128)(2,1)}) custom-call(bf16[2048,256]{1,0:T(8,128)(2,1)} %copy-done.1, bf16[2048,256]{1,0:T(8,128)(2,1)} %copy-done.2, bf16[2048,256]{1,0:T(8,128)(2,1)} %copy-done.3, ...), custom_call_target="tpu_custom_call", output_to_operand_aliasing={{2}: (6, {})} | custom-call | flops 20999999488 | bytes 21000000 | tf_op jit(solution)/shard_map/attention_forward/pallas_call | solution.py:107
  200.5 29.5 %gather_heads.1.attn_hbm = bf16[1024,2048]{1,0:T(8,128)(2,1)} custom-call(bf16[2048,256]{1,0:T(8,128)(2,1)} %get-tuple-element.69.src_ref), custom_call_target="tpu_custom_call" | custom-call | flops 28000000000 | bytes 28000000 | tf_op jit(solution)/shard_map/gather_heads/pallas_call | solution.py:884
  230.1 6.9 %fusion.4 = (bf16[1024,512]{1,0:T(8,128)(2,1)}, f32[1024,512]{1,0:T(8,128)}) fusion(bf16[1024,2048]{1,0:T(8,128)(2,1)} %gather_heads.1.attn_hbm, bf16[2048,512]{1,0:T(8,128)(2,1)} %get-tuple-element.70.weight_ref, bf16[1024,512]{1,0:T(8,128)(2,1)S(1)} %copy-done.20), kind=kOutput, calls=%fused_computation.23 | convolution fusion | flops 2149056512 | bytes 10485760 | tf_op jit(solution)/shard_map/dot_general | solution.py:24
  237.0 40.7 %gather_residual.1.resid_ref = bf16[2048,2048]{1,0:T(8,128)(2,1)} custom-call(bf16[1024,512]{1,0:T(8,128)(2,1)} %get-tuple-element.119.src_ref), custom_call_target="tpu_custom_call" | custom-call | flops 40000000000 | bytes 40000000 | tf_op jit(solution)/shard_map/gather_residual/pallas_call | solution.py:689
  277.7 28.1 %feed_forward.1 = (bf16[2048,2048]{1,0:T(8,128)(2,1)}, bf16[704,2048]{1,0:T(8,128)(2,1)}, bf16[704,2048]{1,0:T(8,128)(2,1)}, bf16[704,2048]{1,0:T(8,128)(2,1)}, f32[2048,8]{1,0:T(8,128)}) custom-call(bf16[2048,2048]{1,0:T(8,128)(2,1)} %gather_residual.1.resid_ref, f32[1,2048]{1,0:T(1,128)} %get-tuple-element.106.gain_ref, ...), custom_call_target="tpu_custom_call" | custom-call | flops 28000000000 | bytes 28000000 | tf_op jit(solution)/shard_map/feed_forward/pallas_call | solution.py:1133
  305.8 17.1 %ffn_grads.1 = bf16[4,2,704,512]{3,2,1,0:T(8,128)(2,1)} custom-call(bf16[704,2048]{1,0:T(8,128)(2,1)} %get-tuple-element.78.refs_0_.gate_ref, bf16[704,2048]{1,0:T(8,128)(2,1)} %get-tuple-element.76.refs_1_.up_ref, bf16[2048,2048]{1,0:T(8,128)(2,1)} %get-tuple-element.77.refs_2_), custom_call_target="tpu_custom_call" | custom-call | flops 17999998976 | bytes 18000000 | tf_op jit(solution)/shard_map/ffn_grads/pallas_call | solution.py:1158
  325.8 55.4 %back_second.1 = (f32[1024,512]{1,0:T(8,128)}, bf16[1024,512]{1,0:T(8,128)(2,1)}, f32[1,512]{1,0:T(1,128)}, bf16[4,704,512]{2,1,0:T(8,128)(2,1)}) custom-call(bf16[704,2048]{1,0:T(8,128)(2,1)} %get-tuple-element.78.refs_0_.gate_ref, bf16[704,2048]{1,0:T(8,128)(2,1)} %get-tuple-element.76.refs_1_.up_ref, ...), custom_call_target="tpu_custom_call" | custom-call | flops 49999998976 | bytes 50000000 | tf_op jit(solution)/shard_map/back_second/pallas_call | solution.py:1576
  381.1 65.8 %back_heads.1 = (bf16[2048,256]{1,0:T(8,128)(2,1)}, bf16[1024,512]{1,0:T(8,128)(2,1)}, bf16[8,1024,512]{2,1,0:T(8,128)(2,1)}, bf16[4,704,512]{2,1,0:T(8,128)(2,1)}) custom-call(bf16[1024,512]{1,0:T(8,128)(2,1)} %get-tuple-element.81.low_ref, bf16[2048,512]{1,0:T(8,128)(2,1)} %get-tuple-element.70.weight_ref, bf16[1024,2048]{1,0:T(8,128)(2,1)} %gather_heads.1.attn_hbm, ...), custom_call_target="tpu_custom_call" | custom-call | flops 60000002048 | bytes 60000000 | tf_op jit(solution)/shard_map/back_heads/pallas_call | solution.py:1865
  447.0 45.4 %attention_backward.1 = (bf16[2048,768]{1,0:T(8,128)(2,1)}, f32[2,1,768]{2,1,0:T(1,128)}, bf16[1024,512]{1,0:T(8,128)(2,1)}) custom-call(bf16[2048,256]{1,0:T(8,128)(2,1)} %copy-done.1, bf16[2048,256]{1,0:T(8,128)(2,1)} %copy-done.2, bf16[2048,256]{1,0:T(8,128)(2,1)} %copy-done.3, bf16[2048,256]{1,0:T(8,128)(2,1)} %get-tuple-element.83.refs_3_, ...), custom_call_target="tpu_custom_call" | custom-call | flops 41999998976 | bytes 42000000 | tf_op jit(solution)/shard_map/attention_backward/pallas_call | solution.py:245
  492.4 11.6 %convolution_convert_fusion.part_ref = bf16[2048,768]{1,0:T(8,128)(2,1)} fusion(bf16[2048,2048]{1,0:T(8,128)(2,1)} %get-tuple-element.88, bf16[2048,768]{1,0:T(8,128)(2,1)} %get-tuple-element.92.grad_ref), kind=kOutput, calls=%fused_computation | convolution fusion | flops 6444023808 | bytes 14680064 | tf_op jit(solution)/shard_map/dot_general | solution.py:24
  504.1 77.8 %back_first.1 = (f32[1024,512]{1,0:T(8,128)}, f32[1,512]{1,0:T(1,128)}, f32[256,512]{1,0:T(8,128)}, f32[256,512]{1,0:T(8,128)}, f32[256,512]{1,0:T(8,128)}, /*in...) custom-call(bf16[2048,768]{1,0:T(8,128)(2,1)} %get-tuple-element.92.grad_ref, ...), custom_call_target="tpu_custom_call" | custom-call | flops 60000002048 | bytes 60000000 | tf_op jit(solution)/shard_map/back_first/pallas_call | solution.py:1715
  581.9 1.3 pad_maximum_fusion.part_ref
  583.2 9.8 %sum_rows.1 = f32[8,512]{1,0:T(8,128)} custom-call(f32[8,512]{1,0:T(8,128)} %pad_maximum_fusion.part_ref), custom_call_target="tpu_custom_call" | custom-call | flops 8000000000 | bytes 8000000 | tf_op jit(solution)/shard_map/sum_rows/pallas_call | solution.py:934
  593.0 1.5 fusion.3
  594.5 1.3 convert_element_type.29
  596.8 1.3 copy.54
  601.3 1.1 copy.59
  (88 shorter events, 15.0 us)
Async XLA Ops:
  7.2 149.7 %all-gather.3.cloned.1.call-start = ((), (), s32[]{:S(2)}) async-start(), calls=%async_computation.2 | async-start | bytes 3604480 | tf_op jit(solution)/shard_map/all_gather | solution.py:280
  7.9 269.8 %all-gather.5.cloned.1.call-start = ((), (), s32[]{:S(2)}) async-start(), calls=%async_computation.3 | async-start | bytes 7208960 | tf_op jit(solution)/shard_map/all_gather | solution.py:280
  10.6 139.2 %copy-start.17 = (f32[512]{0:T(512)S(1)}, f32[512]{0:T(512)}, u32[]{:S(2)}) copy-start(f32[512]{0:T(512)} %param.21) | copy-start | bytes 6148
  10.6 139.3 %copy-start.18 = (f32[512]{0:T(512)S(1)}, f32[512]{0:T(512)}, u32[]{:S(2)}) copy-start(f32[512]{0:T(512)} %param.23) | copy-start | bytes 6148
  10.6 139.4 %copy-start.19 = (f32[512]{0:T(512)S(1)}, f32[512]{0:T(512)}, u32[]{:S(2)}) copy-start(f32[512]{0:T(512)} %param.25) | copy-start | bytes 6148
  152.5 4.7 copy-start
  156.9 290.1 %reduce-scatter.3.cloned.1.call-start = ((), (), s32[]{:S(2)}) async-start(), calls=%async_computation.4 | async-start | bytes 7208960 | tf_op jit(solution)/shard_map/reduce_scatter | solution.py:284
  176.5 1.0 copy-start.1
  177.4 1.0 copy-start.2
  200.5 29.5 %copy-start.20 = (bf16[1024,512]{1,0:T(8,128)(2,1)S(1)}, bf16[1024,512]{1,0:T(8,128)(2,1)}, u32[]{:S(2)}) copy-start(bf16[1024,512]{1,0:T(8,128)(2,1)} %values_ref.1) | copy-start | bytes 3145732
  322.9 2.1 copy-start.13
  322.9 181.2 %reduce-scatter.5.cloned.1.call-start = ((), (), s32[]{:S(2)}) async-start(), calls=%async_computation.5 | async-start | bytes 3604480 | tf_op jit(solution)/shard_map/reduce_scatter | solution.py:284
  492.4 11.6 %copy-start.14 = (f32[2,1,768]{2,1,0:T(1,128)S(1)}, f32[2,1,768]{2,1,0:T(1,128)}, u32[]{:S(2)}) copy-start(f32[2,1,768]{2,1,0:T(1,128)} %get-tuple-element.97) | copy-start | bytes 18436
  492.4 11.7 %copy-start.16 = (pred[512]{0:T(512)(128)(4,1)S(1)}, pred[512]{0:T(512)(128)(4,1)}, u32[]{:S(2)}) copy-start(pred[512]{0:T(512)(128)(4,1)} %broadcast_in_dim.37) | copy-start | bytes 1540
  504.1 77.8 %copy-start.15 = (f32[1,512]{1,0:T(1,128)S(1)}, f32[1,512]{1,0:T(1,128)}, u32[]{:S(2)}) copy-start(f32[1,512]{1,0:T(1,128)} %get-tuple-element.99) | copy-start | bytes 6148
  583.2 11.3 %copy-start.8 = (bf16[704,512]{1,0:T(8,128)(2,1)S(1)}, bf16[704,512]{1,0:T(8,128)(2,1)}, u32[]{:S(2)}) copy-start(bf16[704,512]{1,0:T(8,128)(2,1)} %reduce-scatter.5.cloned.1.call-done) | copy-start | bytes 2162692
  583.2 12.6 %copy-start.7 = (bf16[1024,512]{1,0:T(8,128)(2,1)S(1)}, bf16[1024,512]{1,0:T(8,128)(2,1)}, u32[]{:S(2)}) copy-start(bf16[1024,512]{1,0:T(8,128)(2,1)} %get-tuple-element.137) | copy-start | bytes 3145732
  593.0 3.8 copy-start.4
  595.8 2.3 copy-start.12
  596.8 2.1 copy-start.11
  596.8 2.9 copy-start.10
  596.8 3.7 copy-start.9
  598.1 3.2 copy-start.6
  598.9 3.5 copy-start.5
  (1 other events, 1.0 us)
Sparse Core Ops, SparseCore 0:
  9.6 80.2 all-gather.2
  157.0 104.2 all-gather.4
  323.0 100.4 reduce-scatter.2
  447.1 53.6 reduce-scatter.4

commit v4 on v3

--- a/solution.py
+++ b/solution.py
@@ -399,12 +399,31 @@
         for s in self.second + self.first:
             self.send(1, s, self.own(s), self.piece(self.x, self.col, s), self.over_y)
 
-    def start_core(self):
+    def start_chunk(self, s):
+        self.send(0, s, self.own(s), self.piece(self.x, self.col, s), self.over_x)
+        self.send(1, s, self.own(s), self.piece(self.x, self.col, s), self.over_y)
+        self.send(4, s, self.own(s), self.piece(self.x, self.col, s), self.over_core)
+
+    def near_in_order(self, s):
+        x, col, col_y = self.x, self.col, self.col_y
+        self.wait(0, 1 - x, col, s)
+        if s in self.first:
+            self.pass_on(2, 1 - x, col, s, self.over_y)
+        self.pass_on(5, 1 - x, col, s, self.over_core)
+        self.wait(1, x, col_y, s)
+        if s in self.second:
+            self.pass_on(2, x, col_y, s, self.over_x)
+        self.pass_on(6, x, col_y, s, self.over_core)
+
+    def keep_own(self):
         self.local = pltpu.make_async_copy(
             self.src, block_at(self.out, self.x, self.col, self.rows, self.width, 0, self.rows),
             self.local_sem,
         )
         self.local.start()
+
+    def start_core(self):
+        self.keep_own()
         for s in range(CHUNKS):
             self.send(4, s, self.own(s), self.piece(self.x, self.col, s), self.over_core)
 
@@ -812,139 +831,134 @@
     )(values)
 
 
-def gather_heads_kernel(src_ref, out_ref, local_sem, send_sem, recv_sem):
-    rows, width = out_ref.shape[0], src_ref.shape[1]
+def gather_heads(values, x):
+    here = in_order(x, pick(values, x, 0), swap_rows(pick(values, 1 - x, 0)), 1)
+    return lax.all_gather(here, "col", axis=1, tiled=True)
+
+
+def scatter_heads(values, x):
+    mine = lax.psum_scatter(values, "col", scatter_dimension=1, tiled=True)
+    return in_order(x, pick(mine, x, 1), swap_rows(pick(mine, 1 - x, 1)), 0)
+
+
+def project_out_kernel(
+    heads_ref, weight_ref, tokens_ref, all_ref, resid_ref, resid_all_ref,
+    joined_ref, low_ref, local_sem, send_sem, recv_sem,
+):
+    rows, width = resid_ref.shape
+    part = heads_ref.shape[1]
     x, y, core, row, col = places()
     over_x, over_y, over_core = peers(row, col)
+    count = rows // CHUNKS
+    col_y, col_core = (col + 2) % 4, col + 1 - 2 * core
+    corner = (col_core + 2) % 4
     meet((over_x, over_y, over_core))
-    count = rows // 2
-    col_y = (col + 2) % 4
-    col_core = col + 1 - 2 * core
+    copies = Copies(send_sem, recv_sem, over_core)
+    base = 8 * CHUNKS
 
     def piece(c, a, s):
-        at = pl.multiple_of((PAIR * c + a) * width, 128)
-        return out_ref.at[pl.ds(s * count, count), pl.ds(at, width)]
+        at = pl.multiple_of((PAIR * c + a) * part, 128)
+        return joined_ref.at[pl.ds(s * count, count), pl.ds(at, part)]
 
     def mine(a, s):
-        return src_ref.at[pl.ds(pl.multiple_of(a * rows + s * count, 128), count), :]
-
-    def copy(index, source, place, device):
-        return pltpu.make_async_remote_copy(
-            source, place, send_sem.at[index], recv_sem.at[index],
-            device_id=device, device_id_type=MESH,
-        )
-
-    sent = []
-
-    def send(index, source, place, device):
-        task = copy(index, source, place, device)
-        task.start()
-        sent.append(task)
-
-    def wait(index, place):
-        copy(index, place, place, over_core).wait_recv()
+        return heads_ref.at[pl.ds(pl.multiple_of(a * rows + s * count, 128), count), :]
+
+    def send(group, s, source, place, device):
+        copies.send(base + group * CHUNKS + s, source, place, device)
+
+    def pass_on(group, s, place, device):
+        send(group, s, place, place, device)
+
+    def wait(group, s, place):
+        copies.wait(base + group * CHUNKS + s, place)
 
     local = []
-    for s in range(2):
-        send(s, mine(1 - x, s), piece(col, x, s), over_x)
-        send(2 + s, mine(x, s), piece(col, x, s), over_y)
+    for s in range(CHUNKS):
+        send(0, s, mine(1 - x, s), piece(col, x, s), over_x)
+        send(1, s, mine(x, s), piece(col, x, s), over_y)
+        send(2, s, mine(x, s), piece(col, x, s), over_core)
         task = pltpu.make_async_copy(mine(x, s), piece(col, x, s), local_sem.at[s])
         task.start()
         local.append(task)
-    for s in range(2):
-        send(4 + s, mine(x, s), piece(col, x, s), over_core)
-    for s in range(2):
-        wait(s, piece(col, 1 - x, s))
-        send(6 + s, piece(col, 1 - x, s), piece(col, 1 - x, s), over_y)
-        send(8 + s, piece(col, 1 - x, s), piece(col, 1 - x, s), over_core)
-    for s in range(2):
-        wait(2 + s, piece(col_y, x, s))
-        send(10 + s, piece(col_y, x, s), piece(col_y, x, s), over_core)
-    for s in range(2):
-        wait(6 + s, piece(col_y, 1 - x, s))
-        send(12 + s, piece(col_y, 1 - x, s), piece(col_y, 1 - x, s), over_core)
-    far = (col_core + 2) % 4
-    for s in range(2):
-        wait(4 + s, piece(col_core, x, s))
-        wait(8 + s, piece(col_core, 1 - x, s))
-        wait(10 + s, piece(far, x, s))
-        wait(12 + s, piece(far, 1 - x, s))
-    for task in sent:
-        task.wait_send()
-    for task in local:
-        task.wait()
-
-
-def gather_heads(values, x, collective_id):
-    cols = lax.axis_size("col")
-    if cols != 4:
-        here = in_order(x, pick(values, x, 0), swap_rows(pick(values, 1 - x, 0)), 1)
-        return lax.all_gather(here, "col", axis=1, tiled=True)
-    rows, width = values.shape[0] // PAIR, values.shape[1]
+    gather = PlaneGather(copies, 0, low_ref, resid_all_ref, local_sem.at[CHUNKS])
+
+    def relay(s):
+        wait(0, s, piece(col, 1 - x, s))
+        pass_on(3, s, piece(col, 1 - x, s), over_y)
+        pass_on(4, s, piece(col, 1 - x, s), over_core)
+
+    relay(0)
+    for s in range(CHUNKS):
+        if s + 1 < CHUNKS:
+            relay(s + 1)
+        wait(1, s, piece(col_y, x, s))
+        pass_on(5, s, piece(col_y, x, s), over_core)
+        wait(3, s, piece(col_y, 1 - x, s))
+        pass_on(6, s, piece(col_y, 1 - x, s), over_core)
+        wait(2, s, piece(col_core, x, s))
+        wait(4, s, piece(col_core, 1 - x, s))
+        wait(5, s, piece(corner, x, s))
+        wait(6, s, piece(corner, 1 - x, s))
+        local[s].wait()
+        at = pl.ds(s * count, count)
+        result = tokens_ref[at, :].astype(F32) + dot(joined_ref[at, :], weight_ref[...])
+        resid_ref[at, :] = result
+        low_ref[at, :] = result.astype(BF16)
+        gather.start_chunk(s)
+    store = pltpu.make_async_copy(joined_ref, all_ref, local_sem.at[CHUNKS + 1])
+    store.start()
+    gather.keep_own()
+    for s in range(CHUNKS):
+        gather.near_in_order(s)
+    gather.far()
+    gather.finish()
+    copies.finish()
+    store.wait()
+
+
+def project_out(heads, weight, tokens, collective_id):
+    rows, width = tokens.shape
+    vmem, anywhere = pl.BlockSpec(memory_space=pltpu.VMEM), pl.BlockSpec(memory_space=pl.ANY)
+    sems = lambda n: pltpu.SemaphoreType.DMA((n,))
     return pl.pallas_call(
-        gather_heads_kernel,
-        in_specs=[pl.BlockSpec(memory_space=pltpu.VMEM)],
-        out_specs=pl.BlockSpec(memory_space=pl.ANY),
-        out_shape=jax.ShapeDtypeStruct((rows, PAIR * cols * width), values.dtype),
+        project_out_kernel,
+        in_specs=[vmem] * 3,
+        out_specs=[anywhere, vmem, anywhere],
+        out_shape=[
+            jax.ShapeDtypeStruct((rows, 4 * width), BF16),
+            jax.ShapeDtypeStruct((rows, width), F32),
+            jax.ShapeDtypeStruct((PAIR * rows, 4 * width), BF16),
+        ],
         scratch_shapes=[
-            pltpu.SemaphoreType.DMA((2,)),
-            pltpu.SemaphoreType.DMA((14,)),
-            pltpu.SemaphoreType.DMA((14,)),
+            pltpu.VMEM((rows, 4 * width), BF16), pltpu.VMEM((rows, width), BF16),
+            sems(CHUNKS + 2), sems(15 * CHUNKS), sems(15 * CHUNKS),
         ],
-        cost_estimate=taking(28),
-        compiler_params=pltpu.CompilerParams(collective_id=collective_id, has_side_effects=True),
-        name="gather_heads",
-    )(values)
-
-
-def scatter_heads(values, x):
-    mine = lax.psum_scatter(values, "col", scatter_dimension=1, tiled=True)
-    return in_order(x, pick(mine, x, 1), swap_rows(pick(mine, 1 - x, 1)), 0)
-
-
-def sum_rows_kernel(part_ref, out_ref, slots_ref, send_sem, recv_sem):
-    size = slots_ref.shape[0]
-    row, col = lax.axis_index("row"), lax.axis_index("col")
-    others = [(lax.rem(row + step, size), col) for step in range(1, size)]
-    meet(others)
-    slots_ref[0] = part_ref[...]
-    copies = [
-        pltpu.make_async_remote_copy(
-            slots_ref.at[0], slots_ref.at[step], send_sem.at[step], recv_sem.at[step],
-            device_id=others[step - 1], device_id_type=MESH,
-        )
-        for step in range(1, size)
-    ]
-    for copy in copies:
-        copy.start()
-    for copy in copies:
-        copy.wait_recv()
-    total = jnp.zeros(part_ref.shape, F32)
-    for r in range(size):
-        total += slots_ref[lax.rem(row + size - r, size)]
-    out_ref[...] = total
-    for copy in copies:
-        copy.wait_send()
-
-
-def sum_rows(part, collective_id):
-    size = lax.axis_size("row")
-    if size != 8:
-        return lax.psum(part, "row")
-    return pl.pallas_call(
-        sum_rows_kernel,
-        in_specs=[pl.BlockSpec(memory_space=pltpu.VMEM)],
-        out_specs=pl.BlockSpec(memory_space=pltpu.VMEM),
-        out_shape=jax.ShapeDtypeStruct(part.shape, F32),
-        scratch_shapes=[
-            pltpu.VMEM((size,) + part.shape, F32),
-            pltpu.SemaphoreType.DMA((size,)),
-            pltpu.SemaphoreType.DMA((size,)),
-        ],
-        cost_estimate=taking(8),
-        compiler_params=pltpu.CompilerParams(collective_id=collective_id, has_side_effects=True),
-        name="sum_rows",
-    )(part)
+        compiler_params=pltpu.CompilerParams(
+            collective_id=collective_id, has_side_effects=True, vmem_limit_bytes=60 << 20
+        ),
+        cost_estimate=taking(66),
+        name="project_out",
+    )(heads, weight, tokens)
+
+
+class RowSum:
+    def __init__(self, copies, base, slots_ref):
+        self.copies, self.base, self.slots = copies, base, slots_ref
+        self.row, self.col = lax.axis_index("row"), lax.axis_index("col")
+        self.size = slots_ref.shape[0]
+        self.others = [((self.row + step) % self.size, self.col) for step in range(1, self.size)]
+
+    def start(self):
+        for step, device in enumerate(self.others, 1):
+            self.copies.send(self.base + step - 1, self.slots.at[0], self.slots.at[step], device)
+
+    def finish(self):
+        for step in range(1, self.size):
+            self.copies.wait(self.base + step - 1, self.slots.at[step])
+        total = jnp.zeros(self.slots.shape[1:], F32)
+        for r in range(self.size):
+            total += self.slots[(self.row + self.size - r) % self.size]
+        return total
 
 
 def row_stats(values):
@@ -1097,7 +1111,7 @@
         out_specs=out_specs,
         out_shape=out_shape,
         scratch_shapes=scratch,
-        compiler_params=pltpu.CompilerParams(vmem_limit_bytes=48 << 20, **params),
+        compiler_params=pltpu.CompilerParams(vmem_limit_bytes=60 << 20, **params),
         cost_estimate=taking(16),
         name="project_heads",
     )(*operands)
@@ -1238,16 +1252,20 @@
         if h == 1 and i in (0, 2):
             self.send(10 + i // 2, self.own.at[i, at, :], self.y_ref.at[i // 2], self.over_y)
 
-    def first(self):
+    def begin(self):
         self.give(0, 0)
         self.give(0, 1)
         self.keep(0, 0)
         self.keep(0, 1)
+
+    def proceed(self):
         for h in range(2):
             self.give(1, h)
             self.give(2, h)
         self.keep(1, 0)
         self.keep(2, 1)
+
+    def complete(self):
         self.keep(2, 0)
         self.keep(1, 1)
         for h in range(2):
@@ -1601,17 +1619,18 @@
 
 def back_first_kernel(
     grad_ref, weight_ref, values_ref, stats_ref, gain_ref, base_ref, part_ref, ffn_ref, heads_ref,
-    out_ref, dgain_ref, query_ref, key_ref, value_ref, gate_ref, up_grad_ref, out_grad_ref,
-    sums_ref, up_ref, down_line_ref, heads_up_ref, heads_down_ref, swap_ref, swapped_ref, turn_ref,
+    vectors_ref,
+    out_ref, vector_sums_ref, query_ref, key_ref, value_ref, gate_ref, up_grad_ref, out_grad_ref,
+    dgain_ref, slots_ref, sums_ref, up_ref, down_line_ref, heads_up_ref, heads_down_ref, swap_ref, swapped_ref, turn_ref,
     send_sem, recv_sem, *scratch,
 ):
     line_sems, scratch = scratch[:12], scratch[12:]
     rows, width = out_ref.shape
     x, _, _, row, col = places()
     devices = around()
-    size = PAIR * LINES
-    meet((*devices, ((row + PAIR) % size, col), ((row + size - PAIR) % size, col)))
     copies = Copies(send_sem, recv_sem, devices[2])
+    vectors = RowSum(copies, PlaneScatter.SEMS + 7, slots_ref)
+    meet((*devices[1:], *vectors.others))
     depth, columns = up_ref.shape[2:]
 
     def line_of(k):
@@ -1631,7 +1650,7 @@
     lines = [line_of(k) for k in range(2)] + [heads]
     for line in lines:
         line.clear()
-        line.start()
+    lines[0].start()
 
     def product(at, c):
         weight = weight_ref[pl.ds(pl.multiple_of(c * width, 128), width), :]
@@ -1647,11 +1666,17 @@
     ours = pl.multiple_of(x * half, 128)
     swap = PlaneScatter.SEMS + 3
     units = ffn_ref.shape[2]
-    scatter.first()
-    for line in lines:
-        line.hop(0)
+    scatter.begin()
+    lines[1].start()
+    scatter.proceed()
+    lines[0].hop(0)
+    heads.start()
+    scatter.complete()
+    lines[1].hop(0)
     scatter.settle()
+    heads.hop(0)
     scatter.second()
+    lines[0].hop(1)
     here = pl.ds(pl.multiple_of(x * units, 16), units)
     there = pl.ds(pl.multiple_of((1 - x) * units, 16), units)
     for w in range(2):
@@ -1659,10 +1684,13 @@
             swap + 2 + w, ffn_ref.at[0, w, :, pl.ds(theirs, half)], turn_ref.at[w, here, :], devices[0]
         )
         turn_ref[w, here, :] = ffn_ref[0, w, :, pl.ds(ours, half)]
-    for line in lines:
-        line.hop(1)
+    lines[1].hop(1)
     scatter.third()
+    heads.hop(1)
     norm.start(scatter.result, devices[1:4])
+    slots_ref[0] = vectors_ref[...]
+    slots_ref[0, 3:4, :] = dgain_ref[...]
+    vectors.start()
     part = width // PAIR
     outs = (query_ref, key_ref, value_ref)
 
@@ -1693,6 +1721,7 @@
     heads.receive()
     out_grad_ref[...] = heads.total(pl.ds(0, out_depth))
     heads.finish()
+    vector_sums_ref[...] = vectors.finish()
     for k in range(2):
         at = pl.ds(k * columns, columns)
         copies.wait(swap + k, swapped_ref.at[:, at])
@@ -1704,26 +1733,27 @@
 
 
 def back_first(
-    grad, weight, values, stats, gain, base, part, ffn, heads, collective_id
+    grad, weight, values, stats, gain, base, part, ffn, heads, vectors, collective_id
 ):
     rows, width = values.shape
     depth, columns = part.shape[0] // LINES, part.shape[1]
     vmem = pl.BlockSpec(memory_space=pltpu.VMEM)
     sems = lambda n: pltpu.SemaphoreType.DMA((n,))
-    count = PlaneScatter.SEMS + 7
+    count = PlaneScatter.SEMS + 7 + PAIR * LINES - 1
     units = ffn.shape[2]
     return pl.pallas_call(
         back_first_kernel,
-        in_specs=[vmem] * 9,
+        in_specs=[vmem] * 10,
         out_specs=[vmem] * 8,
         out_shape=[
             jax.ShapeDtypeStruct((rows, width), F32),
-            jax.ShapeDtypeStruct((1, width), F32),
+            jax.ShapeDtypeStruct(vectors.shape, F32),
         ]
         + [jax.ShapeDtypeStruct((depth // PAIR, width), F32)] * 3
         + [jax.ShapeDtypeStruct((depth // PAIR, PAIR * units), F32)] * 2
         + [jax.ShapeDtypeStruct((heads.shape[0] // LINES, width), F32)],
         scratch_shapes=[
+            pltpu.VMEM((1, width), F32), pltpu.VMEM((PAIR * LINES,) + vectors.shape, F32),
             pltpu.VMEM((4, 8, rows), F32),
             pltpu.VMEM((2, LINES - 1, depth, columns // 2), BF16),
             pltpu.VMEM((2, LINES - 1, depth, columns // 2), BF16),
@@ -1736,9 +1766,9 @@
         compiler_params=pltpu.CompilerParams(
             collective_id=collective_id, has_side_effects=True, vmem_limit_bytes=63 << 20
         ),
-        cost_estimate=taking(60),
+        cost_estimate=taking(10),
         name="back_first",
-    )(grad, weight, values, stats, gain.reshape(1, width), base, part, ffn, heads)
+    )(grad, weight, values, stats, gain.reshape(1, width), base, part, ffn, heads, vectors)
 
 
 def back_heads_kernel(
@@ -1948,11 +1978,13 @@
         normed_first, queries, keys, values, stats_first = project_heads(*projections)
         attended, lse = attention_forward(queries, keys, values, plane_segments)
         down_all = lax.all_to_all(down_blocks, "col", split_axis=0, concat_axis=0, tiled=True)
-    attn_all = gather_heads(attended, x, 2)
-    inputs = tokens.astype(F32)
-    resid = inputs + dot(attn_all, out_all)
-
-    resid_all = gather_plane(resid.astype(BF16), "gather_residual", 3)
+    if fast:
+        attn_all, resid, resid_all = project_out(attended, out_all, tokens, 2)
+    else:
+        attn_all = gather_heads(attended, x)
+        resid = tokens.astype(F32) + dot(attn_all, out_all)
+        resid_all = gather_plane(resid.astype(BF16), "gather_residual", 3)
+
     normed_second, hidden_low, grad_gate, grad_up, stats_second = feed_forward(
         resid_all, gains[1], ffn_weight, grad_all, down_all
     )
@@ -2003,15 +2035,22 @@
     grad_down = scatter_line(after(grad_down, grad_ffn).reshape(lines * hidden, width))
     grad_qkv_later = after(grad_qkv, grad_qkv_weight)
     own_stats = pick(stats_first, x, 0)
+    bias_part = jnp.sum(bias_sums, axis=(0, 1)).reshape(3, half)
+    bias_part = jnp.where(
+        (jnp.arange(PAIR) == x)[None, :, None], bias_part[:, None, :], 0.0
+    ).reshape(3, width)
     if fast:
         (
-            tokens_grad, attn_gain_part, query_grad, key_grad, value_grad, gate_grad, up_grad,
+            tokens_grad, vectors, query_grad, key_grad, value_grad, gate_grad, up_grad,
             grad_out_weight,
         ) = back_first(
-            after(grad_qkv_later, grad_down), qkv_weight,
-            tokens, own_stats, attn_gain, grad_resid, grad_qkv_weight, grad_ffn, grad_out_weight, 6,
-        )
-        attn_gain_part = attn_gain_part[0]
+            grad_qkv_later, qkv_weight,
+            tokens, own_stats, attn_gain, grad_resid, grad_qkv_weight, grad_ffn, grad_out_weight,
+            jnp.concatenate(
+                [bias_part, jnp.zeros((1, width), F32), mlp_gain_part[None], jnp.zeros((3, width), F32)]
+            ),
+            6,
+        )
     else:
         kept, other = pick(grad_ffn[0], x, 2), swap_rows(pick(grad_ffn[0], 1 - x, 2))
         gate_grad, up_grad = (
@@ -2027,24 +2066,17 @@
         )
         mean_here, inv_here = own_stats[:, 0:1], own_stats[:, 1:2]
         grad_input, attn_gain_part = norm_backward(
-            grad_first, (inputs - mean_here) * inv_here, inv_here, attn_gain
+            grad_first, (tokens.astype(F32) - mean_here) * inv_here, inv_here, attn_gain
         )
         tokens_grad = grad_input + grad_resid
+        vectors = lax.psum(
+            jnp.concatenate([bias_part, attn_gain_part[None], mlp_gain_part[None]]), "row"
+        )
         mixed = resid + scatter_plane(
             back_project((hidden_low,), down_all[:, None], "mix"), "scatter_mixed", 10
         )
         mixed = mixed.astype(BF16)
 
-    bias_part = jnp.sum(bias_sums, axis=(0, 1)).reshape(3, half)
-    bias_part = jnp.where(
-        (jnp.arange(PAIR) == x)[None, :, None], bias_part[:, None, :], 0.0
-    ).reshape(3, width)
-    vectors = sum_rows(
-        jnp.concatenate(
-            [bias_part, attn_gain_part[None], mlp_gain_part[None], jnp.zeros((3, width), F32)]
-        ),
-        11,
-    )
     return (
         mixed,
         tokens_grad,

time: 614 us -> 602 us (0.980)
  Pallas kernels: 549 us -> 542 us
  matrix products: 18.5 us -> 11.7 us
    dot_general x2 -> x1, matrix products: 18.5 us -> 11.7 us  [dot(): lax.dot_general(left, right, ((left_dims, right_dims), ((), ())), preferr...]
    pallas_call x4 -> x2, Pallas kernels: 158 us -> 151 us  [the longest x1 83.4 us: back_first(): pl.pallas_call(back_first_kernel, in_specs=[vmem] * 10, out_specs=[vmem]...]
  transfers between devices with their start and end apart: 4 -> 4, of which waited for: 0 -> 0; matrix products, arithmetic and copies ran while one was open for 5% -> 5% of each run, Pallas kernels for 68% -> 83%
where the time goes in v4:
time: 602 us; the launch traced here: 598 us
  Pallas kernels  542 us (90%)
  local copies, waits for them, and re-layouts  20.8 us (3%)
  between operations  14.3 us (2%)
  matrix products  11.7 us (2%)
  other arithmetic  7.14 us (1%)
    pallas_call x1, Pallas kernels, gather_first(): pl.pallas_call(gather_first_kernel, in_specs=[pl.BlockSpec(memory_space=p...  139 us
    pallas_call x1, Pallas kernels, back_first(): pl.pallas_call(back_first_kernel, in_specs=[vmem] * 10, out_specs=[vmem]...  83.4 us
    pallas_call x1, Pallas kernels, project_out(): pl.pallas_call(project_out_kernel, in_specs=[vmem] * 3, out_specs=[anywhe...  68.1 us
    pallas_call x1, Pallas kernels, back_heads(): pl.pallas_call(back_heads_kernel, in_specs=[vmem] * 2 + [anywhere] * 4, o...  65.2 us
    pallas_call x1, Pallas kernels, back_second(): pl.pallas_call(back_second_kernel, in_specs=[anywhere] * 5 + [vmem] * 4,...  55.6 us
    pallas_call x1, Pallas kernels, attention_backward(): pl.pallas_call(kernel, grid=(seqs,), in_specs=in_specs, out_specs=out_spe...  45.3 us
    pallas_call x1, Pallas kernels, feed_forward(): pl.pallas_call(feed_forward_kernel, grid=(rows // TILE,), in_specs=[tiled...  28.1 us
    pallas_call x1, Pallas kernels, attention_forward(): pl.pallas_call(kernel, grid=(seqs,), in_specs=in_specs, out_specs=out_spe...  21.2 us
  transfers between devices with their start and end apart: 4, of which 0 were waited for; matrix products, arithmetic and copies ran while one was open for 5% of the time, Pallas kernels for 83%

profile of v4, /device:TPU:0, one launch (start us, length us, event | category | flops | bytes accessed | tf_op | source)
XLA Modules:
  0.0 598.1 jit_solution(6535047929178556466)
XLA Ops:
  8.7 1.3 select_maximum_fusion.gains_ref
  10.6 139.0 %gather_first.1 = (bf16[2048,2048]{1,0:T(8,128)(2,1)}, bf16[2048,2048]{1,0:T(8,128)(2,1)}, bf16[2048,768]{1,0:T(8,128)(2,1)}, bf16[2048,512]{1,0:T(8,128)(2,1)},...) custom-call(bf16[1024,512]{1,0:T(8,128)(2,1)} %values_ref.1, bf16[1024,512]{1,0:T(8,128)(2,1)} %base_ref.1, ...), custom_call_target="tpu_custom_call" | custom-call | flops 109999996928 | bytes 110000000 | tf_op jit(solution)/shard_map/gather_first/pallas_call | solution.py:678
  150.7 1.5 fusion.2
  152.8 1.3 copy.37.refs_4_.refs_5_
  154.1 1.3 copy.39.refs_3_.refs_7_
  155.5 1.3 copy.38.refs_5_.refs_6_
  156.8 1.5 fusion.1
  158.7 19.5 %project_heads.1 = (bf16[2048,2048]{1,0:T(8,128)(2,1)}, bf16[2048,256]{1,0:T(8,128)(2,1)}, bf16[2048,256]{1,0:T(8,128)(2,1)}, bf16[2048,256]{1,0:T(8,128)(2,1)},...) custom-call(bf16[2048,2048]{1,0:T(8,128)(2,1)} %get-tuple-element.62.refs_0_, f32[1,2048]{1,0:T(1,128)} %get-tuple-element.111.refs_1_, ...), custom_call_target="tpu_custom_call" | custom-call | flops 16000000000 | bytes 16000000 | tf_op jit(solution)/shard_map/project_heads/pallas_call | solution.py:1107
  178.2 21.2 %attention_forward.1 = (bf16[2048,256]{1,0:T(8,128)(2,1)}, f32[2,8,1024]{2,1,0:T(8,128)}, bf16[4,704,512]{2,1,0:T(8,128)(2,1)}) custom-call(bf16[2048,256]{1,0:T(8,128)(2,1)} %get-tuple-element.67.refs_0_, bf16[2048,256]{1,0:T(8,128)(2,1)} %get-tuple-element.68.refs_1_, ...), custom_call_target="tpu_custom_call", output_to_operand_aliasing={{2}: (6, {})} | custom-call | flops 20999999488 | bytes 21000000 | tf_op jit(solution)/shard_map/attention_forward/pallas_call | solution.py:107
  199.4 68.1 %project_out.1 = (bf16[1024,2048]{1,0:T(8,128)(2,1)}, f32[1024,512]{1,0:T(8,128)}, bf16[2048,2048]{1,0:T(8,128)(2,1)}) custom-call(bf16[2048,256]{1,0:T(8,128)(2,1)} %get-tuple-element.71.heads_ref, bf16[2048,512]{1,0:T(8,128)(2,1)} %get-tuple-element.72.weight_ref, bf16[1024,512]{1,0:T(8,128)(2,1)} %values_ref.1), custom_call_target="tpu_custom_call" | custom-call | flops 65999998976 | bytes 66000000 | tf_op jit(solution)/shard_map/project_out/pallas_call | solution.py:923
  267.5 28.1 %feed_forward.1 = (bf16[2048,2048]{1,0:T(8,128)(2,1)}, bf16[704,2048]{1,0:T(8,128)(2,1)}, bf16[704,2048]{1,0:T(8,128)(2,1)}, bf16[704,2048]{1,0:T(8,128)(2,1)}, f32[2048,8]{1,0:T(8,128)}) custom-call(bf16[2048,2048]{1,0:T(8,128)(2,1)} %get-tuple-element.73.resid_ref, f32[1,2048]{1,0:T(1,128)} %get-tuple-element.110.gain_ref, ...), custom_call_target="tpu_custom_call" | custom-call | flops 28000000000 | bytes 28000000 | tf_op jit(solution)/shard_map/feed_forward/pallas_call | solution.py:1147
  295.6 17.1 %ffn_grads.1 = bf16[4,2,704,512]{3,2,1,0:T(8,128)(2,1)} custom-call(bf16[704,2048]{1,0:T(8,128)(2,1)} %get-tuple-element.81.refs_0_.gate_ref, bf16[704,2048]{1,0:T(8,128)(2,1)} %get-tuple-element.79.refs_1_.up_ref, bf16[2048,2048]{1,0:T(8,128)(2,1)} %get-tuple-element.80.refs_2_), custom_call_target="tpu_custom_call" | custom-call | flops 17999998976 | bytes 18000000 | tf_op jit(solution)/shard_map/ffn_grads/pallas_call | solution.py:1172
  314.6 0.8 constant_dynamic-slice_fusion.stats_ref
  316.2 55.6 %back_second.1 = (f32[1024,512]{1,0:T(8,128)}, bf16[1024,512]{1,0:T(8,128)(2,1)}, f32[1,512]{1,0:T(1,128)}, bf16[4,704,512]{2,1,0:T(8,128)(2,1)}) custom-call(bf16[704,2048]{1,0:T(8,128)(2,1)} %get-tuple-element.81.refs_0_.gate_ref, bf16[704,2048]{1,0:T(8,128)(2,1)} %get-tuple-element.79.refs_1_.up_ref, ...), custom_call_target="tpu_custom_call" | custom-call | flops 49999998976 | bytes 50000000 | tf_op jit(solution)/shard_map/back_second/pallas_call | solution.py:1594
  371.8 65.2 %back_heads.1 = (bf16[2048,256]{1,0:T(8,128)(2,1)}, bf16[1024,512]{1,0:T(8,128)(2,1)}, bf16[8,1024,512]{2,1,0:T(8,128)(2,1)}, bf16[4,704,512]{2,1,0:T(8,128)(2,1)}) custom-call(bf16[1024,512]{1,0:T(8,128)(2,1)} %get-tuple-element.85.low_ref, bf16[2048,512]{1,0:T(8,128)(2,1)} %get-tuple-element.72.weight_ref, bf16[1024,2048]{1,0:T(8,128)(2,1)} %get-tuple-element.86.attn_hbm, ...), custom_call_target="tpu_custom_call" | custom-call | flops 60000002048 | bytes 60000000 | tf_op jit(solution)/shard_map/back_heads/pallas_call | solution.py:1895
  437.1 45.3 %attention_backward.1 = (bf16[2048,768]{1,0:T(8,128)(2,1)}, f32[2,1,768]{2,1,0:T(1,128)}, bf16[1024,512]{1,0:T(8,128)(2,1)}) custom-call(bf16[2048,256]{1,0:T(8,128)(2,1)} %get-tuple-element.67.refs_0_, bf16[2048,256]{1,0:T(8,128)(2,1)} %get-tuple-element.68.refs_1_, bf16[2048,256]{1,0:T(8,128)(2,1)} %get-tuple-element.69.refs_2_, ...), custom_call_target="tpu_custom_call" | custom-call | flops 41999998976 | bytes 42000000 | tf_op jit(solution)/shard_map/attention_backward/pallas_call | solution.py:245
  482.4 11.7 %convolution_convert_fusion.part_ref = bf16[2048,768]{1,0:T(8,128)(2,1)} fusion(bf16[2048,2048]{1,0:T(8,128)(2,1)} %get-tuple-element.93, bf16[2048,768]{1,0:T(8,128)(2,1)} %get-tuple-element.94.grad_ref), kind=kOutput, calls=%fused_computation | convolution fusion | flops 6444023808 | bytes 14680064 | tf_op jit(solution)/shard_map/dot_general | solution.py:24
  494.9 83.4 %back_first.1 = (f32[1024,512]{1,0:T(8,128)}, f32[8,512]{1,0:T(8,128)}, f32[256,512]{1,0:T(8,128)}, f32[256,512]{1,0:T(8,128)}, f32[256,512]{1,0:T(8,128)}, /*in...) custom-call(bf16[2048,768]{1,0:T(8,128)(2,1)} %get-tuple-element.94.grad_ref, ...), custom_call_target="tpu_custom_call" | custom-call | flops 10000000000 | bytes 10000000 | tf_op jit(solution)/shard_map/back_first/pallas_call | solution.py:1744
  578.3 1.5 fusion.3
  579.8 2.4 convert_element_type.21
  582.2 2.3 copy.53
  584.6 1.3 copy.54
  589.1 1.1 copy.59
  590.2 1.1 copy.60
  (76 shorter events, 10.8 us)
Async XLA Ops:
  7.2 151.2 %all-gather.3.cloned.1.call-start = ((), (), s32[]{:S(2)}) async-start(), calls=%async_computation.2 | async-start | bytes 3604480 | tf_op jit(solution)/shard_map/all_gather | solution.py:280
  7.9 259.6 %all-gather.5.cloned.1.call-start = ((), (), s32[]{:S(2)}) async-start(), calls=%async_computation.3 | async-start | bytes 7208960 | tf_op jit(solution)/shard_map/all_gather | solution.py:280
  10.6 139.2 %copy-start.13 = (f32[512]{0:T(512)S(1)}, f32[512]{0:T(512)}, u32[]{:S(2)}) copy-start(f32[512]{0:T(512)} %param.21) | copy-start | bytes 6148
  10.6 139.3 %copy-start.14 = (f32[512]{0:T(512)S(1)}, f32[512]{0:T(512)}, u32[]{:S(2)}) copy-start(f32[512]{0:T(512)} %param.23) | copy-start | bytes 6148
  10.6 139.4 %copy-start.15 = (f32[512]{0:T(512)S(1)}, f32[512]{0:T(512)}, u32[]{:S(2)}) copy-start(f32[512]{0:T(512)} %param.25) | copy-start | bytes 6148
  158.4 278.6 %reduce-scatter.3.cloned.1.call-start = ((), (), s32[]{:S(2)}) async-start(), calls=%async_computation.4 | async-start | bytes 7208960 | tf_op jit(solution)/shard_map/reduce_scatter | solution.py:284
  312.7 1.9 copy-start.7
  312.7 2.7 copy-start.8
  312.7 267.1 %reduce-scatter.5.cloned.1.call-start = ((), (), s32[]{:S(2)}) async-start(), calls=%async_computation.5 | async-start | bytes 3604480 | tf_op jit(solution)/shard_map/reduce_scatter | solution.py:284
  482.4 11.7 %copy-start.9 = (f32[2,1,768]{2,1,0:T(1,128)S(1)}, f32[2,1,768]{2,1,0:T(1,128)}, u32[]{:S(2)}) copy-start(f32[2,1,768]{2,1,0:T(1,128)} %get-tuple-element.98) | copy-start | bytes 18436
  482.4 11.8 %copy-start.12 = (pred[512]{0:T(512)(128)(4,1)S(1)}, pred[512]{0:T(512)(128)(4,1)}, u32[]{:S(2)}) copy-start(pred[512]{0:T(512)(128)(4,1)} %broadcast_in_dim.40) | copy-start | bytes 1540
  482.4 11.8 %copy-start.10 = (f32[1,512]{1,0:T(1,128)S(1)}, f32[1,512]{1,0:T(1,128)}, u32[]{:S(2)}) copy-start(f32[1,512]{1,0:T(1,128)} %get-tuple-element.99) | copy-start | bytes 6148
  482.4 11.8 %copy-start.11 = (f32[8]{0:T(128)S(1)}, f32[8]{0:T(128)}, u32[]{:S(2)}) copy-start(f32[8]{0:T(128)} %pad.11.clone) | copy-start | bytes 100
  578.3 6.3 %copy-start = (f32[1024,512]{1,0:T(8,128)S(1)}, f32[1024,512]{1,0:T(8,128)}, u32[]{:S(2)}) copy-start(f32[1024,512]{1,0:T(8,128)} %get-tuple-element.140) | copy-start | bytes 6291460
  582.2 3.7 copy-start.6
  582.2 4.5 copy-start.5
  584.6 2.9 copy-start.4
  584.6 3.7 copy-start.3
  584.6 4.5 copy-start.2
  586.7 3.5 copy-start.1
Sparse Core Ops, SparseCore 0:
  9.6 80.2 all-gather.2
  158.5 104.2 all-gather.4
  312.8 100.5 reduce-scatter.2
  437.2 54.2 reduce-scatter.4

commit v5 on v4

--- a/solution.py
+++ b/solution.py
@@ -996,12 +996,13 @@
 TILE = 256
 
 
-def norm_tile(values_ref, gain_ref, stats_ref):
+def norm_tile(values_ref, gain_ref, row, stats_ref):
     values = values_ref[...].astype(F32)
     mean, inv_std = row_stats(values)
+    gain = gain_ref[row : row + 1, :]
     lane = lax.broadcasted_iota(jnp.int32, stats_ref.shape, 1)
     stats_ref[...] = jnp.where(lane == 0, mean, inv_std)
-    return ((values - mean) * inv_std * gain_ref[...]).astype(BF16)
+    return ((values - mean) * inv_std * gain).astype(BF16)
 
 
 def project_heads_kernel(
@@ -1009,7 +1010,7 @@
     normed_ref, q_ref, k_ref, v_ref, stats_ref,
 ):
     width = q_ref.shape[1]
-    normed = norm_tile(tokens_ref, gain_ref, stats_ref)
+    normed = norm_tile(tokens_ref, gain_ref, 0, stats_ref)
     normed_ref[...] = normed
     in_head = lax.broadcasted_iota(jnp.int32, (1, width), 1) % HEAD_DIM
     cosine = jnp.tile(cos_ref[...], (1, width // cos_ref.shape[1]))
@@ -1080,11 +1081,11 @@
     )
 
 
-def project_heads(tokens, gain, weight, bias, cosine, sine, blocks=None, collective_id=None):
+def project_heads(tokens, gains, weight, bias, cosine, sine, blocks=None, collective_id=None):
     rows, depth = tokens.shape
     width = weight.shape[1] // 3
     in_specs = [
-        tiled(depth), whole((1, depth)), whole(weight.shape), whole((1, 3 * width)),
+        tiled(depth), whole(gains.shape), whole(weight.shape), whole((1, 3 * width)),
         tiled(cosine.shape[1]), tiled(cosine.shape[1]),
     ]
     out_specs = [tiled(depth)] + [tiled(width)] * 3 + [tiled(8)]
@@ -1093,7 +1094,7 @@
         *[jax.ShapeDtypeStruct((rows, width), BF16)] * 3,
         jax.ShapeDtypeStruct((rows, 8), F32),
     ]
-    operands = [tokens, gain.reshape(1, depth), weight, bias.reshape(1, 3 * width), cosine, sine]
+    operands = [tokens, gains, weight, bias.reshape(1, 3 * width), cosine, sine]
     params, scratch, kernel = {}, [], project_heads_kernel
     if blocks is not None:
         anywhere = pl.BlockSpec(memory_space=pl.ANY)
@@ -1122,7 +1123,7 @@
     normed_ref, hidden_ref, dgate_ref, dup_ref, stats_ref,
 ):
     lines, _, hidden, width = weight_ref.shape
-    normed_ref[...] = norm_tile(resid_ref, gain_ref, stats_ref)
+    normed_ref[...] = norm_tile(resid_ref, gain_ref, 1, stats_ref)
     gate = jnp.zeros((hidden, TILE), F32)
     up = jnp.zeros((hidden, TILE), F32)
     dhidden = jnp.zeros((hidden, TILE), F32)
@@ -1140,7 +1141,7 @@
     dup_ref[...] = (dhidden * silu).astype(BF16)
 
 
-def feed_forward(resid, gain, weight, grad, down):
+def feed_forward(resid, gains, weight, grad, down):
     rows, depth = resid.shape
     hidden = down.shape[1]
     across = pl.BlockSpec((hidden, TILE), lambda i: (0, i))
@@ -1148,7 +1149,7 @@
         feed_forward_kernel,
         grid=(rows // TILE,),
         in_specs=[
-            tiled(depth), whole((1, depth)), whole(weight.shape), tiled(depth), whole(down.shape)
+            tiled(depth), whole(gains.shape), whole(weight.shape), tiled(depth), whole(down.shape)
         ],
         out_specs=[tiled(depth)] + [across] * 3 + [tiled(8)],
         out_shape=[jax.ShapeDtypeStruct((rows, depth), BF16)]
@@ -1157,7 +1158,7 @@
         compiler_params=pltpu.CompilerParams(vmem_limit_bytes=56 << 20),
         cost_estimate=taking(28),
         name="feed_forward",
-    )(resid, gain.reshape(1, depth), weight, grad, down)
+    )(resid, gains, weight, grad, down)
 
 
 def weight_grads_kernel(*refs):
@@ -1426,9 +1427,14 @@
         self.values, self.stats, self.gain, self.more = values_ref, stats_ref, gain_ref, base_ref
         self.out, self.low, self.dgain, self.sums = out_ref, low_ref, dgain_ref, sums_ref
 
-    def unit_of(self, at):
-        stats = self.stats[at, :]
-        return (self.values[at, :].astype(F32) - stats[:, 0:1]) * stats[:, 1:2]
+    def stats_of(self, start):
+        at = places()[0] * self.out.shape[0] + start
+        return self.stats[pl.ds(pl.multiple_of(at, STEP), STEP), :]
+
+    def unit_of(self, start):
+        stats = self.stats_of(start)
+        values = self.values[pl.ds(start, STEP), :].astype(F32)
+        return (values - stats[:, 0:1]) * stats[:, 1:2]
 
     def start(self, result, devices):
         lane = lax.broadcasted_iota(jnp.int32, (1, 128), 1)
@@ -1437,7 +1443,7 @@
             at = pl.ds(start, STEP)
             grad = result(start, STEP)
             self.out[at, :] = grad
-            unit = self.unit_of(at)
+            unit = self.unit_of(start)
             self.dgain[...] += jnp.sum(grad * unit, axis=0, keepdims=True)
             grad = grad * self.gain[...]
             first = jnp.sum(grad, axis=1, keepdims=True)
@@ -1459,9 +1465,9 @@
             )
             total = jnp.concatenate([total, jnp.zeros((STEP - 8, STEP), F32)], axis=0).T
             total = total * (1.0 / (4 * width))
-            unit = self.unit_of(at)
+            unit = self.unit_of(start)
             grad = self.out[at, :] * self.gain[...]
-            grad = self.stats[at, 1:2] * (grad - total[:, 0:1] - unit * total[:, 1:2])
+            grad = self.stats_of(start)[:, 1:2] * (grad - total[:, 0:1] - unit * total[:, 1:2])
             grad = grad + self.more[at, :].astype(F32)
             self.out[at, :] = grad
             if self.low is not None:
@@ -1618,16 +1624,18 @@
 
 
 def back_first_kernel(
-    grad_ref, weight_ref, values_ref, stats_ref, gain_ref, base_ref, part_ref, ffn_ref, heads_ref,
+    grad_ref, weight_ref, values_ref, stats_ref, gain_ref, base_ref, normed_hbm, ffn_ref, heads_ref,
     vectors_ref,
     out_ref, vector_sums_ref, query_ref, key_ref, value_ref, gate_ref, up_grad_ref, out_grad_ref,
-    dgain_ref, slots_ref, sums_ref, up_ref, down_line_ref, heads_up_ref, heads_down_ref, swap_ref, swapped_ref, turn_ref,
+    normed_ref, part_ref, load_sem, dgain_ref, slots_ref, sums_ref, up_ref, down_line_ref, heads_up_ref, heads_down_ref, swap_ref, swapped_ref, turn_ref,
     send_sem, recv_sem, *scratch,
 ):
     line_sems, scratch = scratch[:12], scratch[12:]
     rows, width = out_ref.shape
     x, _, _, row, col = places()
     devices = around()
+    load = pltpu.make_async_copy(normed_hbm, normed_ref, load_sem)
+    load.start()
     copies = Copies(send_sem, recv_sem, devices[2])
     vectors = RowSum(copies, PlaneScatter.SEMS + 7, slots_ref)
     meet((*devices[1:], *vectors.others))
@@ -1650,7 +1658,7 @@
     lines = [line_of(k) for k in range(2)] + [heads]
     for line in lines:
         line.clear()
-    lines[0].start()
+    heads.start()
 
     def product(at, c):
         weight = weight_ref[pl.ds(pl.multiple_of(c * width, 128), width), :]
@@ -1667,14 +1675,20 @@
     swap = PlaneScatter.SEMS + 3
     units = ffn_ref.shape[2]
     scatter.begin()
+    load.wait()
+    for b in range(LINES):
+        at = slice(b * depth, (b + 1) * depth)
+        part_ref[at, :] = dot(normed_ref[:, at], grad_ref[...], (0,), (0,)).astype(BF16)
+        if b == 1:
+            heads.hop(0)
+    lines[0].start()
     lines[1].start()
     scatter.proceed()
+    heads.hop(1)
+    scatter.complete()
     lines[0].hop(0)
-    heads.start()
-    scatter.complete()
     lines[1].hop(0)
     scatter.settle()
-    heads.hop(0)
     scatter.second()
     lines[0].hop(1)
     here = pl.ds(pl.multiple_of(x * units, 16), units)
@@ -1686,7 +1700,6 @@
         turn_ref[w, here, :] = ffn_ref[0, w, :, pl.ds(ours, half)]
     lines[1].hop(1)
     scatter.third()
-    heads.hop(1)
     norm.start(scatter.result, devices[1:4])
     slots_ref[0] = vectors_ref[...]
     slots_ref[0, 3:4, :] = dgain_ref[...]
@@ -1733,17 +1746,17 @@
 
 
 def back_first(
-    grad, weight, values, stats, gain, base, part, ffn, heads, vectors, collective_id
+    grad, weight, values, stats, gain, base, normed, ffn, heads, vectors, collective_id
 ):
     rows, width = values.shape
-    depth, columns = part.shape[0] // LINES, part.shape[1]
+    depth, columns = normed.shape[1] // LINES, grad.shape[1]
     vmem = pl.BlockSpec(memory_space=pltpu.VMEM)
     sems = lambda n: pltpu.SemaphoreType.DMA((n,))
     count = PlaneScatter.SEMS + 7 + PAIR * LINES - 1
     units = ffn.shape[2]
     return pl.pallas_call(
         back_first_kernel,
-        in_specs=[vmem] * 10,
+        in_specs=[vmem] * 6 + [pl.BlockSpec(memory_space=pl.ANY)] + [vmem] * 3,
         out_specs=[vmem] * 8,
         out_shape=[
             jax.ShapeDtypeStruct((rows, width), F32),
@@ -1753,6 +1766,8 @@
         + [jax.ShapeDtypeStruct((depth // PAIR, PAIR * units), F32)] * 2
         + [jax.ShapeDtypeStruct((heads.shape[0] // LINES, width), F32)],
         scratch_shapes=[
+            pltpu.VMEM(normed.shape, BF16), pltpu.VMEM((normed.shape[1], columns), BF16),
+            pltpu.SemaphoreType.DMA,
             pltpu.VMEM((1, width), F32), pltpu.VMEM((PAIR * LINES,) + vectors.shape, F32),
             pltpu.VMEM((4, 8, rows), F32),
             pltpu.VMEM((2, LINES - 1, depth, columns // 2), BF16),
@@ -1768,7 +1783,7 @@
         ),
         cost_estimate=taking(10),
         name="back_first",
-    )(grad, weight, values, stats, gain.reshape(1, width), base, part, ffn, heads, vectors)
+    )(grad, weight, values, stats, gain.reshape(1, width), base, normed, ffn, heads, vectors)
 
 
 def back_heads_kernel(
@@ -1966,7 +1981,7 @@
     down_blocks = after(down_line, tokens_all).reshape(lines, hidden, width)
     ffn_weight = gather_line(after(ffn_part, down_blocks))
 
-    projections = (tokens_all, gains[0], qkv_weight, bias, cosine, sine)
+    projections = (tokens_all, gains, qkv_weight, bias, cosine, sine)
     if fast:
         normed_first, queries, keys, values, stats_first, down_partly = project_heads(
             *projections, down_blocks, 1
@@ -1986,23 +2001,23 @@
         resid_all = gather_plane(resid.astype(BF16), "gather_residual", 3)
 
     normed_second, hidden_low, grad_gate, grad_up, stats_second = feed_forward(
-        resid_all, gains[1], ffn_weight, grad_all, down_all
+        resid_all, gains, ffn_weight, grad_all, down_all
     )
     if fast:
         grad_ffn = weight_grads((grad_gate, grad_up), normed_second, width, "ffn_grads")
     else:
         grad_ffn = weight_grads((grad_gate, grad_up), normed_second, width, "ffn_grads")
-    own_stats = pick(stats_second, x, 0)
     if fast:
         grad_resid, grad_resid_low, mlp_gain_part, down_blocks = back_second(
             after(grad_gate, grad_ffn), grad_up, ffn_weight, hidden_low, grad_all,
-            resid, own_stats, mlp_gain, out_grad, 4,
+            resid, stats_second, mlp_gain, out_grad, 4,
         )
         mlp_gain_part = mlp_gain_part[0]
     else:
         grad_second = scatter_plane(
             back_project((grad_gate, grad_up), ffn_weight, "back_ffn"), "scatter_second", 4
         )
+        own_stats = pick(stats_second, x, 0)
         mean_here, inv_here = own_stats[:, 0:1], own_stats[:, 1:2]
         grad_resid, mlp_gain_part = norm_backward(
             grad_second, (resid - mean_here) * inv_here, inv_here, mlp_gain
@@ -2031,10 +2046,7 @@
         grad_down = lax.all_to_all(
             grad_down.reshape(cols, hidden, width), "col", split_axis=0, concat_axis=0, tiled=True
         )
-    grad_qkv_weight = dot(normed_first, grad_qkv, (0,), (0,)).astype(BF16)
     grad_down = scatter_line(after(grad_down, grad_ffn).reshape(lines * hidden, width))
-    grad_qkv_later = after(grad_qkv, grad_qkv_weight)
-    own_stats = pick(stats_first, x, 0)
     bias_part = jnp.sum(bias_sums, axis=(0, 1)).reshape(3, half)
     bias_part = jnp.where(
         (jnp.arange(PAIR) == x)[None, :, None], bias_part[:, None, :], 0.0
@@ -2044,8 +2056,8 @@
             tokens_grad, vectors, query_grad, key_grad, value_grad, gate_grad, up_grad,
             grad_out_weight,
         ) = back_first(
-            grad_qkv_later, qkv_weight,
-            tokens, own_stats, attn_gain, grad_resid, grad_qkv_weight, grad_ffn, grad_out_weight,
+            grad_qkv, qkv_weight,
+            tokens, stats_first, attn_gain, grad_resid, normed_first, grad_ffn, grad_out_weight,
             jnp.concatenate(
                 [bias_part, jnp.zeros((1, width), F32), mlp_gain_part[None], jnp.zeros((3, width), F32)]
             ),
@@ -2056,14 +2068,16 @@
         gate_grad, up_grad = (
             in_order(x, kept[i], other[i], 0).T.astype(F32) for i in range(2)
         )
+        grad_qkv_weight = dot(normed_first, grad_qkv, (0,), (0,)).astype(BF16)
         kept, other = own_rows(scatter_line(grad_qkv_weight), x)
         query_grad, key_grad, value_grad = (
             in_order(x, kept[:, at : at + half], other[:, at : at + half], 1).astype(F32)
             for at in (0, half, 2 * half)
         )
         grad_first = scatter_plane(
-            dot(grad_qkv_later, qkv_weight, (1,), (1,)).astype(BF16), "scatter_first", 6
-        )
+            dot(grad_qkv, qkv_weight, (1,), (1,)).astype(BF16), "scatter_first", 6
+        )
+        own_stats = pick(stats_first, x, 0)
         mean_here, inv_here = own_stats[:, 0:1], own_stats[:, 1:2]
         grad_input, attn_gain_part = norm_backward(
             grad_first, (tokens.astype(F32) - mean_here) * inv_here, inv_here, attn_gain

time: 602 us -> 591 us (0.982)
  matrix products: 11.7 us -> 0 us
    dot_general x1 -> x0, matrix products: 11.7 us -> none  [dot(): lax.dot_general(left, right, ((left_dims, right_dims), ((), ())), preferr...]
  transfers between devices with their start and end apart: 4 -> 4, of which waited for: 0 -> 0; matrix products, arithmetic and copies ran while one was open for 5% -> 2% of each run, Pallas kernels for 83% -> 85%
where the time goes in v5:
time: 591 us; the launch traced here: 585 us
  Pallas kernels  544 us (92%)
  local copies, waits for them, and re-layouts  17.5 us (3%)
  between operations  14.3 us (2%)
  other arithmetic  7.83 us (1%)
    pallas_call x1, Pallas kernels, gather_first(): pl.pallas_call(gather_first_kernel, in_specs=[pl.BlockSpec(memory_space=p...  139 us
    pallas_call x1, Pallas kernels, back_first(): pl.pallas_call(back_first_kernel, in_specs=[vmem] * 6 + [pl.BlockSpec(mem...  84.8 us
    pallas_call x1, Pallas kernels, project_out(): pl.pallas_call(project_out_kernel, in_specs=[vmem] * 3, out_specs=[anywhe...  68.1 us
    pallas_call x1, Pallas kernels, back_heads(): pl.pallas_call(back_heads_kernel, in_specs=[vmem] * 2 + [anywhere] * 4, o...  65.4 us
    pallas_call x1, Pallas kernels, back_second(): pl.pallas_call(back_second_kernel, in_specs=[anywhere] * 5 + [vmem] * 4,...  55.4 us
    pallas_call x1, Pallas kernels, attention_backward(): pl.pallas_call(kernel, grid=(seqs,), in_specs=in_specs, out_specs=out_spe...  45.4 us
    pallas_call x1, Pallas kernels, feed_forward(): pl.pallas_call(feed_forward_kernel, grid=(rows // TILE,), in_specs=[tiled...  28.2 us
    pallas_call x1, Pallas kernels, attention_forward(): pl.pallas_call(kernel, grid=(seqs,), in_specs=in_specs, out_specs=out_spe...  21.2 us
  transfers between devices with their start and end apart: 4, of which 0 were waited for; matrix products, arithmetic and copies ran while one was open for 2% of the time, Pallas kernels for 85%

profile of v5, /device:TPU:0, one launch (start us, length us, event | category | flops | bytes accessed | tf_op | source)
XLA Modules:
  0.0 585.2 jit_solution(3213749839395788359)
XLA Ops:
  8.0 1.3 select_maximum_fusion.gains_ref
  10.6 139.0 %gather_first.1 = (bf16[2048,2048]{1,0:T(8,128)(2,1)}, bf16[2048,2048]{1,0:T(8,128)(2,1)}, bf16[2048,768]{1,0:T(8,128)(2,1)}, bf16[2048,512]{1,0:T(8,128)(2,1)},...) custom-call(bf16[1024,512]{1,0:T(8,128)(2,1)} %values_ref.1, bf16[1024,512]{1,0:T(8,128)(2,1)} %base_ref.1, ...), custom_call_target="tpu_custom_call" | custom-call | flops 109999996928 | bytes 110000000 | tf_op jit(solution)/shard_map/gather_first/pallas_call | solution.py:678
  150.7 1.5 fusion.1
  152.8 1.3 copy.37.refs_4_.refs_5_
  154.2 1.3 copy.38.refs_5_.refs_6_
  155.5 1.3 copy.39.refs_3_.refs_7_
  157.1 19.5 %project_heads.1 = (bf16[2048,2048]{1,0:T(8,128)(2,1)}, bf16[2048,256]{1,0:T(8,128)(2,1)}, bf16[2048,256]{1,0:T(8,128)(2,1)}, bf16[2048,256]{1,0:T(8,128)(2,1)},...) custom-call(bf16[2048,2048]{1,0:T(8,128)(2,1)} %get-tuple-element.61.refs_0_, ...), custom_call_target="tpu_custom_call" | custom-call | flops 16000000000 | bytes 16000000 | tf_op jit(solution)/shard_map/project_heads/pallas_call | solution.py:1108
  176.6 21.2 %attention_forward.1 = (bf16[2048,256]{1,0:T(8,128)(2,1)}, f32[2,8,1024]{2,1,0:T(8,128)}, bf16[4,704,512]{2,1,0:T(8,128)(2,1)}) custom-call(bf16[2048,256]{1,0:T(8,128)(2,1)} %get-tuple-element.66.refs_0_, bf16[2048,256]{1,0:T(8,128)(2,1)} %get-tuple-element.67.refs_1_, ...), custom_call_target="tpu_custom_call", output_to_operand_aliasing={{2}: (6, {})} | custom-call | flops 20999999488 | bytes 21000000 | tf_op jit(solution)/shard_map/attention_forward/pallas_call | solution.py:107
  197.7 68.1 %project_out.1 = (bf16[1024,2048]{1,0:T(8,128)(2,1)}, f32[1024,512]{1,0:T(8,128)}, bf16[2048,2048]{1,0:T(8,128)(2,1)}) custom-call(bf16[2048,256]{1,0:T(8,128)(2,1)} %get-tuple-element.70.heads_ref, bf16[2048,512]{1,0:T(8,128)(2,1)} %get-tuple-element.71.weight_ref, bf16[1024,512]{1,0:T(8,128)(2,1)} %values_ref.1), custom_call_target="tpu_custom_call" | custom-call | flops 65999998976 | bytes 66000000 | tf_op jit(solution)/shard_map/project_out/pallas_call | solution.py:923
  265.9 28.2 %feed_forward.1 = (bf16[2048,2048]{1,0:T(8,128)(2,1)}, bf16[704,2048]{1,0:T(8,128)(2,1)}, bf16[704,2048]{1,0:T(8,128)(2,1)}, bf16[704,2048]{1,0:T(8,128)(2,1)}, f32[2048,8]{1,0:T(8,128)}) custom-call(bf16[2048,2048]{1,0:T(8,128)(2,1)} %get-tuple-element.72.resid_ref, f32[8,2048]{1,0:T(8,128)} %get-tuple-element.62.refs_1_.gain_ref, ...), custom_call_target="tpu_custom_call" | custom-call | flops 28000000000 | bytes 28000000 | tf_op jit(solution)/shard_map/feed_forward/pallas_call | solution.py:1148
  294.0 17.1 %ffn_grads.1 = bf16[4,2,704,512]{3,2,1,0:T(8,128)(2,1)} custom-call(bf16[704,2048]{1,0:T(8,128)(2,1)} %get-tuple-element.80.refs_0_.gate_ref, bf16[704,2048]{1,0:T(8,128)(2,1)} %get-tuple-element.78.refs_1_.up_ref, bf16[2048,2048]{1,0:T(8,128)(2,1)} %get-tuple-element.79.refs_2_), custom_call_target="tpu_custom_call" | custom-call | flops 17999998976 | bytes 18000000 | tf_op jit(solution)/shard_map/ffn_grads/pallas_call | solution.py:1173
  312.8 55.4 %back_second.1 = (f32[1024,512]{1,0:T(8,128)}, bf16[1024,512]{1,0:T(8,128)(2,1)}, f32[1,512]{1,0:T(1,128)}, bf16[4,704,512]{2,1,0:T(8,128)(2,1)}) custom-call(bf16[704,2048]{1,0:T(8,128)(2,1)} %get-tuple-element.80.refs_0_.gate_ref, bf16[704,2048]{1,0:T(8,128)(2,1)} %get-tuple-element.78.refs_1_.up_ref, ...), custom_call_target="tpu_custom_call" | custom-call | flops 49999998976 | bytes 50000000 | tf_op jit(solution)/shard_map/back_second/pallas_call | solution.py:1600
  368.2 65.4 %back_heads.1 = (bf16[2048,256]{1,0:T(8,128)(2,1)}, bf16[1024,512]{1,0:T(8,128)(2,1)}, bf16[8,1024,512]{2,1,0:T(8,128)(2,1)}, bf16[4,704,512]{2,1,0:T(8,128)(2,1)}) custom-call(bf16[1024,512]{1,0:T(8,128)(2,1)} %get-tuple-element.84.low_ref, bf16[2048,512]{1,0:T(8,128)(2,1)} %get-tuple-element.71.weight_ref, bf16[1024,2048]{1,0:T(8,128)(2,1)} %get-tuple-element.85.attn_hbm, ...), custom_call_target="tpu_custom_call" | custom-call | flops 60000002048 | bytes 60000000 | tf_op jit(solution)/shard_map/back_heads/pallas_call | solution.py:1910
  433.7 45.4 %attention_backward.1 = (bf16[2048,768]{1,0:T(8,128)(2,1)}, f32[2,1,768]{2,1,0:T(1,128)}, bf16[1024,512]{1,0:T(8,128)(2,1)}) custom-call(bf16[2048,256]{1,0:T(8,128)(2,1)} %get-tuple-element.66.refs_0_, bf16[2048,256]{1,0:T(8,128)(2,1)} %get-tuple-element.67.refs_1_, bf16[2048,256]{1,0:T(8,128)(2,1)} %get-tuple-element.68.refs_2_, ...), custom_call_target="tpu_custom_call" | custom-call | flops 41999998976 | bytes 42000000 | tf_op jit(solution)/shard_map/attention_backward/pallas_call | solution.py:245
  480.5 84.8 %back_first.1 = (f32[1024,512]{1,0:T(8,128)}, f32[8,512]{1,0:T(8,128)}, f32[256,512]{1,0:T(8,128)}, f32[256,512]{1,0:T(8,128)}, f32[256,512]{1,0:T(8,128)}, /*in...) custom-call(bf16[2048,768]{1,0:T(8,128)(2,1)} %get-tuple-element.91.grad_ref, ...), custom_call_target="tpu_custom_call" | custom-call | flops 10000000000 | bytes 10000000 | tf_op jit(solution)/shard_map/back_first/pallas_call | solution.py:1757
  565.4 1.5 fusion.2
  566.9 2.4 convert_element_type.17
  569.3 2.3 copy.53
  571.7 1.3 copy.54
  573.0 0.8 copy.55
  573.8 0.8 copy.56
  574.6 0.8 copy.57
  576.2 1.1 copy.59
  577.3 1.1 copy.60
  (66 shorter events, 7.9 us)
Async XLA Ops:
  7.2 149.7 %all-gather.3.cloned.1.call-start = ((), (), s32[]{:S(2)}) async-start(), calls=%async_computation.2 | async-start | bytes 3604480 | tf_op jit(solution)/shard_map/all_gather | solution.py:280
  7.9 257.9 %all-gather.5.cloned.1.call-start = ((), (), s32[]{:S(2)}) async-start(), calls=%async_computation.3 | async-start | bytes 7208960 | tf_op jit(solution)/shard_map/all_gather | solution.py:280
  10.6 139.1 %copy-start.10 = (f32[512]{0:T(512)S(1)}, f32[512]{0:T(512)}, u32[]{:S(2)}) copy-start(f32[512]{0:T(512)} %param.23) | copy-start | bytes 6148
  10.6 139.1 %copy-start.11 = (f32[512]{0:T(512)S(1)}, f32[512]{0:T(512)}, u32[]{:S(2)}) copy-start(f32[512]{0:T(512)} %param.25) | copy-start | bytes 6148
  10.6 139.2 %copy-start.12 = (f32[512]{0:T(512)S(1)}, f32[512]{0:T(512)}, u32[]{:S(2)}) copy-start(f32[512]{0:T(512)} %param.21) | copy-start | bytes 6148
  156.9 276.7 %reduce-scatter.3.cloned.1.call-start = ((), (), s32[]{:S(2)}) async-start(), calls=%async_computation.4 | async-start | bytes 7208960 | tf_op jit(solution)/shard_map/reduce_scatter | solution.py:284
  311.2 255.8 %reduce-scatter.5.cloned.1.call-start = ((), (), s32[]{:S(2)}) async-start(), calls=%async_computation.5 | async-start | bytes 3604480 | tf_op jit(solution)/shard_map/reduce_scatter | solution.py:284
  433.6 46.2 %copy-start.9 = (pred[512]{0:T(512)(128)(4,1)S(1)}, pred[512]{0:T(512)(128)(4,1)}, u32[]{:S(2)}) copy-start(pred[512]{0:T(512)(128)(4,1)} %broadcast_in_dim.40) | copy-start | bytes 1540
  433.7 46.2 %copy-start.7 = (f32[1,512]{1,0:T(1,128)S(1)}, f32[1,512]{1,0:T(1,128)}, u32[]{:S(2)}) copy-start(f32[1,512]{1,0:T(1,128)} %get-tuple-element.97) | copy-start | bytes 6148
  433.7 46.2 %copy-start.8 = (f32[8]{0:T(128)S(1)}, f32[8]{0:T(128)}, u32[]{:S(2)}) copy-start(f32[8]{0:T(128)} %pad.11.clone) | copy-start | bytes 100
  565.4 6.3 %copy-start = (f32[1024,512]{1,0:T(8,128)S(1)}, f32[1024,512]{1,0:T(8,128)}, u32[]{:S(2)}) copy-start(f32[1024,512]{1,0:T(8,128)} %get-tuple-element.136) | copy-start | bytes 6291460
  569.3 3.7 copy-start.6
  571.7 2.1 copy-start.5
  571.7 2.9 copy-start.4
  571.7 3.7 copy-start.3
  573.0 3.2 copy-start.2
  573.8 3.5 copy-start.1
Sparse Core Ops, SparseCore 0:
  9.6 80.2 all-gather.2
  157.0 104.2 all-gather.4
  311.3 100.5 reduce-scatter.2
  433.8 53.6 reduce-scatter.4

commit v6 on v5

--- a/solution.py
+++ b/solution.py
@@ -1847,8 +1847,6 @@
     copies.send(4 * CHUNKS, give_ref, come_ref, over_x)
     for s in range(CHUNKS):
         keep(0, s)
-    for i, (other, device) in enumerate(others):
-        copies.send(4 * CHUNKS + 1 + i, blocks_ref.at[other], all_ref.at[col], device)
     for s in range(CHUNKS):
         give(1, s)
     for s in range(CHUNKS):
@@ -1862,6 +1860,8 @@
         load.wait()
     for a in range(PAIR):
         turn_rows(left_ref, hidden_ref, a, rows)
+    for i, (other, device) in enumerate(others):
+        copies.send(4 * CHUNKS + 1 + i, blocks_ref.at[other], all_ref.at[col], device)
     kept = []
     for s in range(CHUNKS):
 

time: 591 us -> 591 us (level)
  no operation moved by 1% of the time
where the time goes in v6:
time: 591 us; the launch traced here: 585 us
  Pallas kernels  544 us (92%)
  local copies, waits for them, and re-layouts  17.5 us (3%)
  between operations  14.3 us (2%)
  other arithmetic  7.83 us (1%)
    pallas_call x1, Pallas kernels, gather_first(): pl.pallas_call(gather_first_kernel, in_specs=[pl.BlockSpec(memory_space=p...  139 us
    pallas_call x1, Pallas kernels, back_first(): pl.pallas_call(back_first_kernel, in_specs=[vmem] * 6 + [pl.BlockSpec(mem...  84.8 us
    pallas_call x1, Pallas kernels, project_out(): pl.pallas_call(project_out_kernel, in_specs=[vmem] * 3, out_specs=[anywhe...  68.1 us
    pallas_call x1, Pallas kernels, back_heads(): pl.pallas_call(back_heads_kernel, in_specs=[vmem] * 2 + [anywhere] * 4, o...  65.4 us
    pallas_call x1, Pallas kernels, back_second(): pl.pallas_call(back_second_kernel, in_specs=[anywhere] * 5 + [vmem] * 4,...  55.4 us
    pallas_call x1, Pallas kernels, attention_backward(): pl.pallas_call(kernel, grid=(seqs,), in_specs=in_specs, out_specs=out_spe...  45.4 us
    pallas_call x1, Pallas kernels, feed_forward(): pl.pallas_call(feed_forward_kernel, grid=(rows // TILE,), in_specs=[tiled...  28.2 us
    pallas_call x1, Pallas kernels, attention_forward(): pl.pallas_call(kernel, grid=(seqs,), in_specs=in_specs, out_specs=out_spe...  21.2 us
  transfers between devices with their start and end apart: 4, of which 0 were waited for; matrix products, arithmetic and copies ran while one was open for 2% of the time, Pallas kernels for 85%

profile of v6, /device:TPU:0, one launch (start us, length us, event | category | flops | bytes accessed | tf_op | source)
XLA Modules:
  0.0 585.2 jit_solution(18397861532356265468)
XLA Ops:
  8.0 1.3 select_maximum_fusion.gains_ref
  10.6 139.0 %gather_first.1 = (bf16[2048,2048]{1,0:T(8,128)(2,1)}, bf16[2048,2048]{1,0:T(8,128)(2,1)}, bf16[2048,768]{1,0:T(8,128)(2,1)}, bf16[2048,512]{1,0:T(8,128)(2,1)},...) custom-call(bf16[1024,512]{1,0:T(8,128)(2,1)} %values_ref.1, bf16[1024,512]{1,0:T(8,128)(2,1)} %base_ref.1, ...), custom_call_target="tpu_custom_call" | custom-call | flops 109999996928 | bytes 110000000 | tf_op jit(solution)/shard_map/gather_first/pallas_call | solution.py:678
  150.7 1.5 fusion.1
  152.8 1.3 copy.37.refs_4_.refs_5_
  154.2 1.3 copy.38.refs_5_.refs_6_
  155.5 1.3 copy.39.refs_3_.refs_7_
  157.1 19.5 %project_heads.1 = (bf16[2048,2048]{1,0:T(8,128)(2,1)}, bf16[2048,256]{1,0:T(8,128)(2,1)}, bf16[2048,256]{1,0:T(8,128)(2,1)}, bf16[2048,256]{1,0:T(8,128)(2,1)},...) custom-call(bf16[2048,2048]{1,0:T(8,128)(2,1)} %get-tuple-element.61.refs_0_, ...), custom_call_target="tpu_custom_call" | custom-call | flops 16000000000 | bytes 16000000 | tf_op jit(solution)/shard_map/project_heads/pallas_call | solution.py:1108
  176.6 21.2 %attention_forward.1 = (bf16[2048,256]{1,0:T(8,128)(2,1)}, f32[2,8,1024]{2,1,0:T(8,128)}, bf16[4,704,512]{2,1,0:T(8,128)(2,1)}) custom-call(bf16[2048,256]{1,0:T(8,128)(2,1)} %get-tuple-element.66.refs_0_, bf16[2048,256]{1,0:T(8,128)(2,1)} %get-tuple-element.67.refs_1_, ...), custom_call_target="tpu_custom_call", output_to_operand_aliasing={{2}: (6, {})} | custom-call | flops 20999999488 | bytes 21000000 | tf_op jit(solution)/shard_map/attention_forward/pallas_call | solution.py:107
  197.7 68.1 %project_out.1 = (bf16[1024,2048]{1,0:T(8,128)(2,1)}, f32[1024,512]{1,0:T(8,128)}, bf16[2048,2048]{1,0:T(8,128)(2,1)}) custom-call(bf16[2048,256]{1,0:T(8,128)(2,1)} %get-tuple-element.70.heads_ref, bf16[2048,512]{1,0:T(8,128)(2,1)} %get-tuple-element.71.weight_ref, bf16[1024,512]{1,0:T(8,128)(2,1)} %values_ref.1), custom_call_target="tpu_custom_call" | custom-call | flops 65999998976 | bytes 66000000 | tf_op jit(solution)/shard_map/project_out/pallas_call | solution.py:923
  265.9 28.2 %feed_forward.1 = (bf16[2048,2048]{1,0:T(8,128)(2,1)}, bf16[704,2048]{1,0:T(8,128)(2,1)}, bf16[704,2048]{1,0:T(8,128)(2,1)}, bf16[704,2048]{1,0:T(8,128)(2,1)}, f32[2048,8]{1,0:T(8,128)}) custom-call(bf16[2048,2048]{1,0:T(8,128)(2,1)} %get-tuple-element.72.resid_ref, f32[8,2048]{1,0:T(8,128)} %get-tuple-element.62.refs_1_.gain_ref, ...), custom_call_target="tpu_custom_call" | custom-call | flops 28000000000 | bytes 28000000 | tf_op jit(solution)/shard_map/feed_forward/pallas_call | solution.py:1148
  294.0 17.1 %ffn_grads.1 = bf16[4,2,704,512]{3,2,1,0:T(8,128)(2,1)} custom-call(bf16[704,2048]{1,0:T(8,128)(2,1)} %get-tuple-element.80.refs_0_.gate_ref, bf16[704,2048]{1,0:T(8,128)(2,1)} %get-tuple-element.78.refs_1_.up_ref, bf16[2048,2048]{1,0:T(8,128)(2,1)} %get-tuple-element.79.refs_2_), custom_call_target="tpu_custom_call" | custom-call | flops 17999998976 | bytes 18000000 | tf_op jit(solution)/shard_map/ffn_grads/pallas_call | solution.py:1173
  312.8 55.4 %back_second.1 = (f32[1024,512]{1,0:T(8,128)}, bf16[1024,512]{1,0:T(8,128)(2,1)}, f32[1,512]{1,0:T(1,128)}, bf16[4,704,512]{2,1,0:T(8,128)(2,1)}) custom-call(bf16[704,2048]{1,0:T(8,128)(2,1)} %get-tuple-element.80.refs_0_.gate_ref, bf16[704,2048]{1,0:T(8,128)(2,1)} %get-tuple-element.78.refs_1_.up_ref, ...), custom_call_target="tpu_custom_call" | custom-call | flops 49999998976 | bytes 50000000 | tf_op jit(solution)/shard_map/back_second/pallas_call | solution.py:1600
  368.2 65.4 %back_heads.1 = (bf16[2048,256]{1,0:T(8,128)(2,1)}, bf16[1024,512]{1,0:T(8,128)(2,1)}, bf16[8,1024,512]{2,1,0:T(8,128)(2,1)}, bf16[4,704,512]{2,1,0:T(8,128)(2,1)}) custom-call(bf16[1024,512]{1,0:T(8,128)(2,1)} %get-tuple-element.84.low_ref, bf16[2048,512]{1,0:T(8,128)(2,1)} %get-tuple-element.71.weight_ref, bf16[1024,2048]{1,0:T(8,128)(2,1)} %get-tuple-element.85.attn_hbm, ...), custom_call_target="tpu_custom_call" | custom-call | flops 60000002048 | bytes 60000000 | tf_op jit(solution)/shard_map/back_heads/pallas_call | solution.py:1910
  433.7 45.4 %attention_backward.1 = (bf16[2048,768]{1,0:T(8,128)(2,1)}, f32[2,1,768]{2,1,0:T(1,128)}, bf16[1024,512]{1,0:T(8,128)(2,1)}) custom-call(bf16[2048,256]{1,0:T(8,128)(2,1)} %get-tuple-element.66.refs_0_, bf16[2048,256]{1,0:T(8,128)(2,1)} %get-tuple-element.67.refs_1_, bf16[2048,256]{1,0:T(8,128)(2,1)} %get-tuple-element.68.refs_2_, ...), custom_call_target="tpu_custom_call" | custom-call | flops 41999998976 | bytes 42000000 | tf_op jit(solution)/shard_map/attention_backward/pallas_call | solution.py:245
  480.5 84.8 %back_first.1 = (f32[1024,512]{1,0:T(8,128)}, f32[8,512]{1,0:T(8,128)}, f32[256,512]{1,0:T(8,128)}, f32[256,512]{1,0:T(8,128)}, f32[256,512]{1,0:T(8,128)}, /*in...) custom-call(bf16[2048,768]{1,0:T(8,128)(2,1)} %get-tuple-element.91.grad_ref, ...), custom_call_target="tpu_custom_call" | custom-call | flops 10000000000 | bytes 10000000 | tf_op jit(solution)/shard_map/back_first/pallas_call | solution.py:1757
  565.4 1.5 fusion.2
  566.9 2.4 convert_element_type.17
  569.3 2.3 copy.53
  571.7 1.3 copy.54
  573.0 0.8 copy.55
  573.8 0.8 copy.56
  574.6 0.8 copy.57
  576.2 1.1 copy.59
  577.3 1.1 copy.60
  (66 shorter events, 7.9 us)
Async XLA Ops:
  7.2 149.7 %all-gather.3.cloned.1.call-start = ((), (), s32[]{:S(2)}) async-start(), calls=%async_computation.2 | async-start | bytes 3604480 | tf_op jit(solution)/shard_map/all_gather | solution.py:280
  7.9 257.9 %all-gather.5.cloned.1.call-start = ((), (), s32[]{:S(2)}) async-start(), calls=%async_computation.3 | async-start | bytes 7208960 | tf_op jit(solution)/shard_map/all_gather | solution.py:280
  10.6 139.1 %copy-start.10 = (f32[512]{0:T(512)S(1)}, f32[512]{0:T(512)}, u32[]{:S(2)}) copy-start(f32[512]{0:T(512)} %param.23) | copy-start | bytes 6148
  10.6 139.1 %copy-start.11 = (f32[512]{0:T(512)S(1)}, f32[512]{0:T(512)}, u32[]{:S(2)}) copy-start(f32[512]{0:T(512)} %param.25) | copy-start | bytes 6148
  10.6 139.2 %copy-start.12 = (f32[512]{0:T(512)S(1)}, f32[512]{0:T(512)}, u32[]{:S(2)}) copy-start(f32[512]{0:T(512)} %param.21) | copy-start | bytes 6148
  156.9 276.7 %reduce-scatter.3.cloned.1.call-start = ((), (), s32[]{:S(2)}) async-start(), calls=%async_computation.4 | async-start | bytes 7208960 | tf_op jit(solution)/shard_map/reduce_scatter | solution.py:284
  311.2 255.8 %reduce-scatter.5.cloned.1.call-start = ((), (), s32[]{:S(2)}) async-start(), calls=%async_computation.5 | async-start | bytes 3604480 | tf_op jit(solution)/shard_map/reduce_scatter | solution.py:284
  433.6 46.2 %copy-start.9 = (pred[512]{0:T(512)(128)(4,1)S(1)}, pred[512]{0:T(512)(128)(4,1)}, u32[]{:S(2)}) copy-start(pred[512]{0:T(512)(128)(4,1)} %broadcast_in_dim.40) | copy-start | bytes 1540
  433.7 46.2 %copy-start.7 = (f32[1,512]{1,0:T(1,128)S(1)}, f32[1,512]{1,0:T(1,128)}, u32[]{:S(2)}) copy-start(f32[1,512]{1,0:T(1,128)} %get-tuple-element.97) | copy-start | bytes 6148
  433.7 46.2 %copy-start.8 = (f32[8]{0:T(128)S(1)}, f32[8]{0:T(128)}, u32[]{:S(2)}) copy-start(f32[8]{0:T(128)} %pad.11.clone) | copy-start | bytes 100
  565.4 6.3 %copy-start = (f32[1024,512]{1,0:T(8,128)S(1)}, f32[1024,512]{1,0:T(8,128)}, u32[]{:S(2)}) copy-start(f32[1024,512]{1,0:T(8,128)} %get-tuple-element.136) | copy-start | bytes 6291460
  569.3 3.7 copy-start.6
  571.7 2.1 copy-start.5
  571.7 2.9 copy-start.4
  571.7 3.7 copy-start.3
  573.0 3.2 copy-start.2
  573.8 3.5 copy-start.1
Sparse Core Ops, SparseCore 0:
  9.6 80.2 all-gather.2
  157.0 104.2 all-gather.4
  311.3 100.5 reduce-scatter.2
  433.8 53.6 reduce-scatter.4
